TPU v7x, 32 devices: a whole 2x2x4 slice. The times are simulated.
32 devices in a mesh: batch: 4 (over y, core), seq: 8 (over z, x).
Axes of the slice: x: 2, y: 2, z: 4, core: 2. Of those that a mesh axis runs over, the one named last changes fastest.
Arguments:
- inputs: bfloat16 [4, 1024, 2048], P('batch', 'seq'), may hold values from -6 to 6
- positions: int32 [4, 1024], P('batch', 'seq'), may hold values from 0 to 3069, as said below
- attn_gain: bfloat16 [2048], P(('batch', 'seq')), may hold values from 0.5 to 1.5
- q_weight: bfloat16 [2048, 2048], P(('batch', 'seq')), may hold values from -0.125 to 0.125
- k_weight: bfloat16 [2048, 512], P(('batch', 'seq')), may hold values from -0.125 to 0.125
- v_weight: bfloat16 [2048, 512], P(('batch', 'seq')), may hold values from -0.125 to 0.125
- o_weight: bfloat16 [2048, 2048], P(('batch', 'seq')), may hold values from -0.5 to 0.5
- ffn_gain: bfloat16 [2048], P(('batch', 'seq')), may hold values from 0.5 to 1.5
- gate_weight: bfloat16 [2048, 8192], P(('batch', 'seq')), may hold values from -0.125 to 0.125
- up_weight: bfloat16 [2048, 8192], P(('batch', 'seq')), may hold values from -0.125 to 0.125
- down_weight: bfloat16 [2048, 8192], P(('batch', 'seq')), may hold values from -0.0625 to 0.0625
- cotangent: bfloat16 [4, 1024, 2048], P('batch', 'seq'), may hold values from -6 to 6
Outputs:
- output: bfloat16 [4, 1024, 2048], P('batch', 'seq')
- input_grad: float32 [4, 1024, 2048], P('batch', 'seq')
- attn_gain_grad: float32 [2048], P(('batch', 'seq'))
- q_grad: float32 [2048, 2048], P(('batch', 'seq'))
- k_grad: float32 [2048, 512], P(('batch', 'seq'))
- v_grad: float32 [2048, 512], P(('batch', 'seq'))
- o_grad: float32 [2048, 2048], P(('batch', 'seq'))
- ffn_gain_grad: float32 [2048], P(('batch', 'seq'))
- gate_grad: float32 [2048, 8192], P(('batch', 'seq'))
- up_grad: float32 [2048, 8192], P(('batch', 'seq'))
- down_grad: float32 [2048, 8192], P(('batch', 'seq'))
Inputs may be any that keep to these rules, and one draw needn't show every extreme that they name: Within a sequence the positions rise by one or two from token to token, from a start between 0 and 1023.
All inputs are finite; a program needn't handle non-finite values.
Results may differ from a plain program's by a relative error of at most 0.015.
Values may be sent and summed in bfloat16 or wider, within the bound.
No kernel may reach another device: no remote copies, remote signals or barrier semaphores. Data moves between devices by JAX's collectives and lax.ppermute only.
A program may use at most 768 MiB of HBM per device.

v0:
```python
import math

import jax
import jax.numpy as jnp
from jax import lax
from jax.sharding import PartitionSpec as P

HEADS = 32
KV_HEADS = 8
HEAD_DIM = 64
FF = 8192


epsilon = 1e-05
rope_base = 500000.0
rope_scale = 32.0
low_freq = 1.0
high_freq = 4.0
initial_context = 8192.0


def matmul_rows(left, right):
    return jnp.einsum("rc,dc->rd", left, right, preferred_element_type=jnp.float32)


def contract_rows(left, right):
    return jnp.einsum("ra,rb->ab", left, right, preferred_element_type=jnp.float32)


def product(left, right):
    return jnp.dot(left, right, preferred_element_type=jnp.float32)


def root_mean_square_norm(values):
    factor = lax.rsqrt(jnp.mean(values * values, axis=-1, keepdims=True) + epsilon)
    return (values * factor, factor)


def norm_backward(grad_hat, normed, factor):
    return factor * (grad_hat - normed * jnp.mean(grad_hat * normed, axis=-1, keepdims=True))


def frequencies():
    half = HEAD_DIM // 2
    base_freqs = rope_base ** (-(jnp.arange(half, dtype=jnp.float32) * 2.0 / HEAD_DIM))
    wavelen = 2.0 * math.pi / base_freqs
    smooth = (initial_context / wavelen - low_freq) / (high_freq - low_freq)
    middle = (1.0 - smooth) * base_freqs / rope_scale + smooth * base_freqs
    return jnp.where(
        wavelen < initial_context / high_freq,
        base_freqs,
        jnp.where(wavelen > initial_context / low_freq, base_freqs / rope_scale, middle),
    )


def angles_of(positions):
    freqs = frequencies()
    turned = positions.astype(jnp.float32)[:, None] * freqs[None, :]
    return (jnp.cos(turned)[:, None, :], jnp.sin(turned)[:, None, :])


def rotate(values, cosine, sine):
    half = values.shape[-1] // 2
    first_half = values[..., :half]
    second_half = values[..., half:]
    return jnp.concatenate(
        [first_half * cosine - second_half * sine, second_half * cosine + first_half * sine],
        axis=-1,
    )


def unrotate(values, cosine, sine):
    half = values.shape[-1] // 2
    first_half = values[..., :half]
    second_half = values[..., half:]
    return jnp.concatenate(
        [first_half * cosine + second_half * sine, second_half * cosine - first_half * sine],
        axis=-1,
    )


def causal_scores(query_block, keys_heads, offset, length):
    scores = jnp.einsum(
        "gqehd,gked->gehqk", query_block, keys_heads, preferred_element_type=jnp.float32
    ) * HEAD_DIM ** (-0.5)
    row_ids = offset + jnp.arange(query_block.shape[1], dtype=jnp.int32)
    col_ids = jnp.arange(length, dtype=jnp.int32)
    return jnp.where(col_ids[None, :] <= row_ids[:, None], scores, -1e30)


def body(
    inputs,
    positions,
    attn_gain,
    q_weight,
    k_weight,
    v_weight,
    o_weight,
    ffn_gain,
    gate_weight,
    up_weight,
    down_weight,
    cotangent,
):
    seq_devices = lax.axis_size("seq")
    groups, span_len, model_width = inputs.shape
    token_rows = groups * span_len
    length = span_len * seq_devices
    heads_local = HEADS // seq_devices
    expanded = max(KV_HEADS, seq_devices)
    kv_local = expanded // seq_devices
    copies = expanded // KV_HEADS
    per_group = heads_local // kv_local
    query_cols = heads_local * HEAD_DIM
    kv_cols = kv_local * HEAD_DIM
    block_rows = min(512, length)
    blocks = length // block_rows
    score_scale = HEAD_DIM ** (-0.5)
    attn_cols = HEADS * HEAD_DIM
    key_cols = KV_HEADS * HEAD_DIM
    attn_full = (
        lax.all_gather(attn_gain, ("batch", "seq"), axis=0, tiled=True),
        lax.all_gather(q_weight, ("batch", "seq"), axis=0, tiled=True),
        lax.all_gather(k_weight, ("batch", "seq"), axis=0, tiled=True),
        lax.all_gather(v_weight, ("batch", "seq"), axis=0, tiled=True),
        lax.all_gather(o_weight, ("batch", "seq"), axis=0, tiled=True),
    )
    attention_norm_weight, query_full, key_full, value_full, output_full = attn_full
    token_states = inputs.reshape(token_rows, model_width).astype(jnp.float32)
    first_unit_rows, first_inverse_norm = root_mean_square_norm(token_states)
    first_normalized_input = (first_unit_rows * attention_norm_weight.astype(jnp.float32)).astype(
        jnp.bfloat16
    )
    cosine, sine = angles_of(positions.reshape(token_rows))
    queries = product(first_normalized_input, query_full).reshape(token_rows, HEADS, HEAD_DIM)
    keys_tok = product(first_normalized_input, key_full).reshape(token_rows, KV_HEADS, HEAD_DIM)
    values_tok = (
        product(first_normalized_input, value_full)
        .astype(jnp.bfloat16)
        .reshape(token_rows, KV_HEADS, HEAD_DIM)
    )
    queries_rot = rotate(queries, cosine, sine).astype(jnp.bfloat16)
    keys_rot = rotate(keys_tok, cosine, sine).astype(jnp.bfloat16)
    keys_exp = jnp.repeat(keys_rot, copies, axis=1)
    values_exp = jnp.repeat(values_tok, copies, axis=1)
    packed = jnp.concatenate(
        [
            queries_rot.reshape(groups, span_len, seq_devices, query_cols),
            keys_exp.reshape(groups, span_len, seq_devices, kv_cols),
            values_exp.reshape(groups, span_len, seq_devices, kv_cols),
        ],
        axis=3,
    )
    heads_in = lax.all_to_all(packed, "seq", split_axis=2, concat_axis=1, tiled=True)
    queries_h = heads_in[:, :, 0, :query_cols].reshape(
        groups, length, kv_local, per_group, HEAD_DIM
    )
    keys_h = heads_in[:, :, 0, query_cols : query_cols + kv_cols].reshape(
        groups, length, kv_local, HEAD_DIM
    )
    values_h = heads_in[:, :, 0, query_cols + kv_cols :].reshape(groups, length, kv_local, HEAD_DIM)

    def forward_block(block_index):
        offset = block_index * block_rows
        query_block = lax.dynamic_slice_in_dim(queries_h, offset, block_rows, 1)
        scores = causal_scores(query_block, keys_h, offset, length)
        peak = jnp.max(scores, axis=-1, keepdims=True)
        expd = jnp.exp(scores - peak)
        totals = jnp.sum(expd, axis=-1, keepdims=True)
        probs_low = (expd / totals).astype(jnp.bfloat16)
        attended = jnp.einsum(
            "gehqk,gked->gqehd", probs_low, values_h, preferred_element_type=jnp.float32
        ).astype(jnp.bfloat16)
        return (attended, (peak + jnp.log(totals))[..., 0])

    attended, logsums = lax.map(forward_block, jnp.arange(blocks, dtype=jnp.int32))
    attn_heads = jnp.moveaxis(attended, 0, 1).reshape(groups, length, 1, query_cols)
    attn_back = lax.all_to_all(attn_heads, "seq", split_axis=1, concat_axis=2, tiled=True)
    attn_tokens = attn_back.reshape(token_rows, attn_cols)
    residual_after_attention = token_states + matmul_rows(attn_tokens, output_full)
    ffn_full = (
        lax.all_gather(ffn_gain, ("batch", "seq"), axis=0, tiled=True),
        lax.all_gather(gate_weight, ("batch", "seq"), axis=0, tiled=True),
        lax.all_gather(up_weight, ("batch", "seq"), axis=0, tiled=True),
        lax.all_gather(down_weight, ("batch", "seq"), axis=0, tiled=True),
    )
    feedforward_norm_weight, gate_full, up_full, down_full = ffn_full
    second_unit_rows, second_inverse_norm = root_mean_square_norm(residual_after_attention)
    second_normalized_input = (
        second_unit_rows * feedforward_norm_weight.astype(jnp.float32)
    ).astype(jnp.bfloat16)
    gate_act = product(second_normalized_input, gate_full)
    up_act = product(second_normalized_input, up_full)
    sigmoid_gate = jax.nn.sigmoid(gate_act)
    silu_gate = gate_act * sigmoid_gate
    hidden_low = (silu_gate * up_act).astype(jnp.bfloat16)
    result = residual_after_attention + matmul_rows(hidden_low, down_full)
    output = result.astype(jnp.bfloat16).reshape(groups, span_len, model_width)
    grad_out = cotangent.reshape(token_rows, model_width).astype(jnp.float32)
    grad_out_low = grad_out.astype(jnp.bfloat16)
    ffn_again = (
        lax.all_gather(ffn_gain, ("batch", "seq"), axis=0, tiled=True),
        lax.all_gather(gate_weight, ("batch", "seq"), axis=0, tiled=True),
        lax.all_gather(up_weight, ("batch", "seq"), axis=0, tiled=True),
        lax.all_gather(down_weight, ("batch", "seq"), axis=0, tiled=True),
    )
    feedforward_norm_weight_broadcast, gate_back, up_back, down_back = ffn_again
    grad_hidden = product(grad_out_low, down_back)
    grad_gate = (
        grad_hidden * up_act * sigmoid_gate * (1.0 + gate_act * (1.0 - sigmoid_gate))
    ).astype(jnp.bfloat16)
    grad_up = (grad_hidden * silu_gate).astype(jnp.bfloat16)
    second_normalized_gradient = matmul_rows(grad_gate, gate_back) + matmul_rows(grad_up, up_back)
    feedforward_norm_weight_gradient = jnp.sum(
        second_normalized_gradient * second_unit_rows, axis=0
    )
    grad_hidden_one = grad_out + norm_backward(
        second_normalized_gradient * feedforward_norm_weight_broadcast.astype(jnp.float32),
        second_unit_rows,
        second_inverse_norm,
    )
    ffn_grads = lax.psum_scatter(
        jnp.concatenate(
            [
                contract_rows(second_normalized_input, grad_gate),
                contract_rows(second_normalized_input, grad_up),
                contract_rows(grad_out_low, hidden_low),
            ],
            axis=1,
        ),
        ("batch", "seq"),
        scatter_dimension=0,
        tiled=True,
    )
    attn_again = (
        lax.all_gather(attn_gain, ("batch", "seq"), axis=0, tiled=True),
        lax.all_gather(q_weight, ("batch", "seq"), axis=0, tiled=True),
        lax.all_gather(k_weight, ("batch", "seq"), axis=0, tiled=True),
        lax.all_gather(v_weight, ("batch", "seq"), axis=0, tiled=True),
        lax.all_gather(o_weight, ("batch", "seq"), axis=0, tiled=True),
    )
    attention_norm_weight_broadcast, query_back, key_back, value_back, output_back = attn_again
    grad_branch = grad_hidden_one.astype(jnp.bfloat16)
    grad_attn = product(grad_branch, output_back).astype(jnp.bfloat16)
    grad_heads = lax.all_to_all(
        grad_attn.reshape(groups, span_len, seq_devices, query_cols),
        "seq",
        split_axis=2,
        concat_axis=1,
        tiled=True,
    )
    grad_heads = grad_heads.reshape(groups, length, kv_local, per_group, HEAD_DIM)

    def backward_block(carry, block_index):
        key_sum, value_sum = carry
        offset = block_index * block_rows
        query_block = lax.dynamic_slice_in_dim(queries_h, offset, block_rows, 1)
        grad_block = lax.dynamic_slice_in_dim(grad_heads, offset, block_rows, 1)
        scores = causal_scores(query_block, keys_h, offset, length)
        probs = jnp.exp(scores - logsums[block_index][..., None])
        probs_low = probs.astype(jnp.bfloat16)
        grad_probs = jnp.einsum(
            "gqehd,gked->gehqk", grad_block, values_h, preferred_element_type=jnp.float32
        )
        centred = jnp.sum(probs * grad_probs, axis=-1, keepdims=True)
        grad_scores = (probs * (grad_probs - centred)).astype(jnp.bfloat16)
        grad_query = (
            jnp.einsum("gehqk,gked->gqehd", grad_scores, keys_h, preferred_element_type=jnp.float32)
            * score_scale
        ).astype(jnp.bfloat16)
        key_sum = (
            key_sum
            + jnp.einsum(
                "gehqk,gqehd->gked", grad_scores, query_block, preferred_element_type=jnp.float32
            )
            * score_scale
        )
        value_sum = value_sum + jnp.einsum(
            "gehqk,gqehd->gked", probs_low, grad_block, preferred_element_type=jnp.float32
        )
        return ((key_sum, value_sum), grad_query)

    zeros_kv = jnp.zeros((groups, length, kv_local, HEAD_DIM), jnp.float32)
    (key_sum, value_sum), grad_queries = lax.scan(
        backward_block, (zeros_kv, zeros_kv), jnp.arange(blocks, dtype=jnp.int32)
    )
    packed_back = jnp.concatenate(
        [
            jnp.moveaxis(grad_queries, 0, 1).reshape(groups, length, 1, query_cols),
            key_sum.astype(jnp.bfloat16),
            value_sum.astype(jnp.bfloat16),
        ],
        axis=3,
    )
    tokens_back = lax.all_to_all(packed_back, "seq", split_axis=1, concat_axis=2, tiled=True)
    grad_qrot = (
        tokens_back[..., :query_cols].reshape(token_rows, HEADS, HEAD_DIM).astype(jnp.float32)
    )
    grad_krot = (
        tokens_back[..., query_cols : query_cols + kv_cols]
        .reshape(token_rows, KV_HEADS, copies, HEAD_DIM)
        .astype(jnp.float32)
        .sum(axis=2)
    )
    grad_vals = (
        tokens_back[..., query_cols + kv_cols :]
        .reshape(token_rows, KV_HEADS, copies, HEAD_DIM)
        .astype(jnp.float32)
        .sum(axis=2)
    )
    grad_query_tok = (
        unrotate(grad_qrot, cosine, sine).astype(jnp.bfloat16).reshape(token_rows, attn_cols)
    )
    grad_key_tok = (
        unrotate(grad_krot, cosine, sine).astype(jnp.bfloat16).reshape(token_rows, key_cols)
    )
    grad_value_tok = grad_vals.astype(jnp.bfloat16).reshape(token_rows, key_cols)
    first_normalized_gradient = (
        matmul_rows(grad_query_tok, query_back)
        + matmul_rows(grad_key_tok, key_back)
        + matmul_rows(grad_value_tok, value_back)
    )
    attention_norm_weight_gradient = jnp.sum(first_normalized_gradient * first_unit_rows, axis=0)
    input_grad = grad_hidden_one + norm_backward(
        first_normalized_gradient * attention_norm_weight_broadcast.astype(jnp.float32),
        first_unit_rows,
        first_inverse_norm,
    )
    attn_term = jnp.concatenate(
        [
            contract_rows(first_normalized_input, grad_query_tok),
            contract_rows(first_normalized_input, grad_key_tok),
            contract_rows(first_normalized_input, grad_value_tok),
            contract_rows(grad_branch, attn_tokens),
        ],
        axis=1,
    )
    attn_sums, gain_one_sum, gain_two_sum = (
        lax.psum_scatter(attn_term, ("batch", "seq"), scatter_dimension=0, tiled=True),
        lax.psum_scatter(
            attention_norm_weight_gradient, ("batch", "seq"), scatter_dimension=0, tiled=True
        ),
        lax.psum_scatter(
            feedforward_norm_weight_gradient, ("batch", "seq"), scatter_dimension=0, tiled=True
        ),
    )
    q_grad = attn_sums[:, :attn_cols]
    k_grad = attn_sums[:, attn_cols : attn_cols + key_cols]
    v_grad = attn_sums[:, attn_cols + key_cols : attn_cols + 2 * key_cols]
    o_grad = attn_sums[:, attn_cols + 2 * key_cols :]
    gate_grad = ffn_grads[:, :FF]
    up_grad = ffn_grads[:, FF : 2 * FF]
    down_grad = ffn_grads[:, 2 * FF :]
    return (
        output,
        input_grad.reshape(groups, span_len, model_width),
        gain_one_sum,
        q_grad,
        k_grad,
        v_grad,
        o_grad,
        gain_two_sum,
        gate_grad,
        up_grad,
        down_grad,
    )


def solution(mesh):
    placed = (
        P("batch", "seq", None),
        P("batch", "seq"),
        P(("batch", "seq")),
        P(("batch", "seq"), None),
        P(("batch", "seq"), None),
        P(("batch", "seq"), None),
        P(("batch", "seq"), None),
        P(("batch", "seq")),
        P(("batch", "seq"), None),
        P(("batch", "seq"), None),
        P(("batch", "seq"), None),
        P("batch", "seq", None),
    )
    return jax.shard_map(
        body,
        mesh=mesh,
        in_specs=placed,
        out_specs=(
            P("batch", "seq", None),
            P("batch", "seq", None),
            P(("batch", "seq")),
            P(("batch", "seq"), None),
            P(("batch", "seq"), None),
            P(("batch", "seq"), None),
            P(("batch", "seq"), None),
            P(("batch", "seq")),
            P(("batch", "seq"), None),
            P(("batch", "seq"), None),
            P(("batch", "seq"), None),
        ),
        check_vma=False,
    )
```

profile of v0, /device:TPU:8, one launch (start us, length us, event | category | flops | bytes accessed | tf_op | source)
XLA Modules:
  0.0 3613.8 jit_solution(9117840776508373672)
XLA Ops:
  13.6 40.7 %all-reduce.5 = (bf16[2048]{0:T(1024)(128)(2,1)S(1)}, bf16[2048]{0:T(1024)(128)(2,1)S(1)}) all-reduce(bf16[2048]{0:T(1024)(128)(2,1)S(1)} %dynamic-update-slice, bf16[2048]{0:T(1024)(128)(2,1)S(1)} %dynamic-update-slice.1), channel_id=1, replica_groups=mesh['batch'=4,'seq'=8] {'batch','seq'}, use_global_device_ids=true, to_apply=%add | all-reduce | flops 4096 | bytes 16384
  70.3 56.1 %all-gather.10.cloned.1.call-done = bf16[2048,512]{1,0:T(8,128)(2,1)} async-done(((bf16[64,512]{1,0:T(8,128)(2,1)}), bf16[2048,512]{1,0:T(8,128)(2,1)}) %all-gather.10.cloned.1.call-update) | async-done | bytes 2097168 | tf_op jit(solution)/shard_map/all_gather | solution.py:124
  130.2 76.4 %all-gather.8.cloned.1.call-done = bf16[2048,2048]{1,0:T(8,128)(2,1)} async-done(((bf16[64,2048]{1,0:T(8,128)(2,1)}), bf16[2048,2048]{1,0:T(8,128)(2,1)}) %all-gather.8.cloned.1.call-update) | async-done | bytes 8388624 | tf_op jit(solution)/shard_map/all_gather | solution.py:123
  230.8 29.8 all-to-all-done
  261.7 17.6 while.27
  313.0 176.3 %all-gather.18.cloned.1.call-done = bf16[2048,8192]{1,0:T(8,128)(2,1)} async-done(((bf16[64,8192]{1,0:T(8,128)(2,1)}), bf16[2048,8192]{1,0:T(8,128)(2,1)}) %all-gather.18.cloned.1.call-update) | async-done | bytes 33554448 | tf_op jit(solution)/shard_map/all_gather | solution.py:184
  489.3 17.0 fusion.115
  506.3 178.8 %all-gather.16.cloned.1.call-done = bf16[2048,8192]{1,0:T(8,128)(2,1)} async-done(((bf16[64,8192]{1,0:T(8,128)(2,1)}), bf16[2048,8192]{1,0:T(8,128)(2,1)}) %all-gather.16.cloned.1.call-update) | async-done | bytes 33554448 | tf_op jit(solution)/shard_map/all_gather | solution.py:183
  685.2 17.1 fusion.114
  702.3 178.9 %all-gather.20.cloned.1.call-done = bf16[2048,8192]{1,0:T(8,128)(2,1)} async-done(((bf16[64,8192]{1,0:T(8,128)(2,1)}), bf16[2048,8192]{1,0:T(8,128)(2,1)}) %all-gather.20.cloned.1.call-update) | async-done | bytes 33554448 | tf_op jit(solution)/shard_map/all_gather | solution.py:185
  881.2 19.6 multiply_convert_fusion
  900.8 16.4 fusion.116
  917.2 17.8 multiply_reduce_fusion
  963.3 29.8 while.28
  1054.9 29.0 pad_maximum_fusion.1
  1083.8 38.9 %copy.126 = f32[2048,5120]{1,0:T(8,128)} copy(f32[2048,5120]{0,1:T(8,128)} %pad_maximum_fusion.1) | data formatting | bytes 83886080
  1123.7 26.1 fusion.119
  1149.8 23.3 fusion.118
  1173.1 23.3 convolution_bitcast_fusion.1
  1196.4 131.0 %pad_maximum_fusion = f32[2048,24576]{1,0:T(8,128)} fusion(f32[2048,8192]{1,0:T(8,128)} %convolution_bitcast_fusion.1, f32[2048,8192]{1,0:T(8,128)} %fusion.119, f32[2048,8192]{1,0:T(8,128)} %fusion.118), kind=kLoop, calls=%fused_computation.66 | loop fusion | flops 100663296 | bytes 402653184 | tf_op jit(solution)/shard_map/concatenate | solution.py:223
  1329.4 17.2 fusion.65
  1355.1 51.3 %all-reduce.4 = (f32[2048]{0:T(1024)S(1)}, f32[2048]{0:T(1024)S(1)}) all-reduce(f32[2048]{0:T(1024)S(1)} %get-tuple-element.242, f32[2048]{0:T(1024)S(1)} %copy-done.34), channel_id=2, replica_groups=mesh['batch'=4,'seq'=8] {'batch','seq'}, use_global_device_ids=true, to_apply=%region_12.13.clone | all-reduce | flops 4096 | bytes 32768
  1408.9 595.9 %reduce-scatter.7.cloned.1.call-done = f32[64,5120]{1,0:T(8,128)} async-done(((f32[2048,5120]{1,0:T(8,128)}), f32[64,5120]{1,0:T(8,128)}) %reduce-scatter.7.cloned.1.call-update) | async-done | bytes 1310736
  2008.7 1592.7 %reduce-scatter.5.cloned.1.call-done = f32[64,24576]{1,0:T(8,128)} async-done(((f32[2048,24576]{1,0:T(8,128)}), f32[64,24576]{1,0:T(8,128)}) %reduce-scatter.5.cloned.1.call-update) | async-done | bytes 6291472 | tf_op jit(solution)/shard_map/reduce_scatter | solution.py:222
  (225 shorter events, 238.7 us)
Async XLA Ops:
  7.2 122.2 %copy-start = (bf16[1,128,2048]{2,1,0:T(8,128)(2,1)S(1)}, bf16[1,128,2048]{2,1,0:T(8,128)(2,1)}, u32[]{:S(2)}) copy-start(bf16[1,128,2048]{2,1,0:T(8,128)(2,1)} %param.16) | copy-start | bytes 1572868
  7.2 60.7 %all-gather.12.cloned.1.call-start = ((), (), s32[]{:S(2)}) async-start(), calls=%async_computation.8 | async-start | bytes 2162688 | tf_op jit(solution)/shard_map/all_gather | solution.py:125
  7.9 118.5 %all-gather.10.cloned.1.call-start = ((), (), s32[]{:S(2)}) async-start(), calls=%async_computation.7 | async-start | bytes 2162688 | tf_op jit(solution)/shard_map/all_gather | solution.py:124
  8.7 198.0 %all-gather.8.cloned.1.call-start = ((), (), s32[]{:S(2)}) async-start(), calls=%async_computation.6 | async-start | bytes 8650752 | tf_op jit(solution)/shard_map/all_gather | solution.py:123
  9.4 296.6 %all-gather.14.cloned.1.call-start = ((), (), s32[]{:S(2)}) async-start(), calls=%async_computation.9 | async-start | bytes 8650752 | tf_op jit(solution)/shard_map/all_gather | solution.py:126
  10.0 479.3 %all-gather.18.cloned.1.call-start = ((), (), s32[]{:S(2)}) async-start(), calls=%async_computation.11 | async-start | bytes 34603008 | tf_op jit(solution)/shard_map/all_gather | solution.py:184
  10.6 674.6 %all-gather.16.cloned.1.call-start = ((), (), s32[]{:S(2)}) async-start(), calls=%async_computation.10 | async-start | bytes 34603008 | tf_op jit(solution)/shard_map/all_gather | solution.py:183
  11.1 870.0 %all-gather.20.cloned.1.call-start = ((), (), s32[]{:S(2)}) async-start(), calls=%async_computation.12 | async-start | bytes 34603008 | tf_op jit(solution)/shard_map/all_gather | solution.py:185
  54.3 164.7 %copy-start.25 = (f32[2048]{0:T(1024)}, f32[2048]{0:T(1024)S(1)}, u32[]{:S(2)}) copy-start(f32[2048]{0:T(1024)S(1)} %convert_element_type.184) | copy-start | bytes 24580
  56.2 162.7 %copy-start.35 = (f32[128]{0:T(128)}, f32[128]{0:T(128)S(1)}, u32[]{:S(2)}) copy-start(f32[128]{0:T(128)S(1)} %add_rsqrt_fusion.1) | copy-start | bytes 1540
  56.4 168.4 %copy-start.28 = (f32[128,32]{0,1:T(8,128)}, f32[128,32]{0,1:T(8,128)S(1)}, u32[]{:S(2)}) copy-start(f32[128,32]{0,1:T(8,128)S(1)} %get-tuple-element.308) | copy-start | bytes 49156
  56.4 168.4 %copy-start.30 = (f32[128,32]{0,1:T(8,128)}, f32[128,32]{0,1:T(8,128)S(1)}, u32[]{:S(2)}) copy-start(f32[128,32]{0,1:T(8,128)S(1)} %get-tuple-element.309) | copy-start | bytes 49156
  226.0 34.6 all-to-all-start
  286.0 19.1 all-to-all-start.1
  306.0 200.3 %copy-start.16 = (bf16[1,128,8,1,256]{1,4,2,3,0:T(8,128)(2,1)}, bf16[1,128,8,1,256]{1,4,2,3,0:T(8,128)(2,1)S(1)}, u32[]{:S(2)}) copy-start(bf16[1,128,8,1,256]{1,4,2,3,0:T(8,128)(2,1)S(1)} %copy.111) | copy-start | bytes 1572868
  312.8 622.2 %copy-start.3 = (f32[128,2048]{1,0:T(8,128)}, f32[128,2048]{1,0:T(8,128)S(1)}, u32[]{:S(2)}) copy-start(f32[128,2048]{1,0:T(8,128)S(1)} %get-tuple-element.311) | copy-start | bytes 3145732
  313.0 372.1 %copy-start.7 = (bf16[128,2048]{1,0:T(8,128)(2,1)}, bf16[128,2048]{1,0:T(8,128)(2,1)S(1)}, u32[]{:S(2)}) copy-start(bf16[128,2048]{1,0:T(8,128)(2,1)S(1)} %multiply_convert_fusion.3) | copy-start | bytes 1572868
  506.3 374.8 %copy-start.18 = (bf16[1,128,2048]{2,1,0:T(8,128)(2,1)S(1)}, bf16[1,128,2048]{2,1,0:T(8,128)(2,1)}, u32[]{:S(2)}) copy-start(bf16[1,128,2048]{2,1,0:T(8,128)(2,1)} %param.27) | copy-start | bytes 1572868
  936.7 80.1 %copy-start.5 = (f32[128,2048]{1,0:T(8,128)}, f32[128,2048]{1,0:T(8,128)S(1)}, u32[]{:S(2)}) copy-start(f32[128,2048]{1,0:T(8,128)S(1)} %multiply_add_fusion) | copy-start | bytes 3145732
  942.8 19.9 all-to-all-start.2
  1011.4 23.7 all-to-all-start.3
  1016.7 988.0 %reduce-scatter.7.cloned.1.call-start = ((), (), s32[]{:S(2)}) async-start(), calls=%async_computation.14 | async-start | bytes 43253760
  1122.7 2478.7 %reduce-scatter.5.cloned.1.call-start = ((), (), s32[]{:S(2)}) async-start(), calls=%async_computation.13 | async-start | bytes 207618048 | tf_op jit(solution)/shard_map/reduce_scatter | solution.py:222
  1346.6 60.9 %copy-start.6 = (f32[128,2048]{1,0:T(8,128)S(1)}, f32[128,2048]{1,0:T(8,128)}, u32[]{:S(2)}) copy-start(f32[128,2048]{1,0:T(8,128)} %copy-done.5) | copy-start | bytes 3145732
  (29 other events, 304.6 us)
Sparse Core Ops, SparseCore 0:
  11.0 56.8 all-gather.11
  70.9 55.4 all-gather.9
  129.4 77.1 all-gather.7
  209.5 85.4 all-gather.13
  297.8 191.5 all-gather.17
  492.2 192.9 all-gather.15
  688.2 192.9 all-gather.19
  1122.8 881.8 reduce-scatter.6
  2011.2 1590.1 reduce-scatter.4
where the time goes:
time: 3620 us; the launch traced here: 3610 us
  waiting for transfers between devices  2940 us (81%)
  matrix products  256 us (7%)
  other arithmetic  190 us (5%)
  local copies, waits for them, and re-layouts  93.8 us (3%)
  blocking collectives  92 us (3%)
    reduce_scatter x1, waiting for transfers between devices, body(): lax.psum_scatter(jnp.concatenate([contract_rows(second_normalized_input,...  1590 us
    unnamed x10, waiting for transfers between devices  600 us
    all_gather x1, waiting for transfers between devices, body(): lax.all_gather(down_weight, ('batch', 'seq'), axis=0, tiled=True)  179 us
    all_gather x1, waiting for transfers between devices, body(): lax.all_gather(gate_weight, ('batch', 'seq'), axis=0, tiled=True)  179 us
    all_gather x1, waiting for transfers between devices, body(): lax.all_gather(up_weight, ('batch', 'seq'), axis=0, tiled=True)  176 us
    concatenate x1, other arithmetic, body(): jnp.concatenate([contract_rows(second_normalized_input, grad_gate), contr...  131 us
    dot_general x7, matrix products, contract_rows(): jnp.einsum('ra,rb->ab', left, right, preferred_element_type=jnp.float32)  94.6 us
    unnamed x2, blocking collectives  92 us
  transfers between devices with their start and end apart: 13, of which 12 were waited for; matrix products, arithmetic and copies ran while one was open for 9% of the time, Pallas kernels for 0%

commit v1 on v0

v1 whole, which is shorter than its diff:
```python
import math

import jax
import jax.numpy as jnp
from jax import lax
from jax.sharding import PartitionSpec as P

HEADS = 32
KV_HEADS = 8
HEAD_DIM = 64

epsilon = 1e-05
rope_base = 500000.0
rope_scale = 32.0
low_freq = 1.0
high_freq = 4.0
initial_context = 8192.0

BF = jnp.bfloat16
F32 = jnp.float32


def frequencies():
    half = HEAD_DIM // 2
    base_freqs = rope_base ** (-(jnp.arange(half, dtype=F32) * 2.0 / HEAD_DIM))
    wavelen = 2.0 * math.pi / base_freqs
    smooth = (initial_context / wavelen - low_freq) / (high_freq - low_freq)
    middle = (1.0 - smooth) * base_freqs / rope_scale + smooth * base_freqs
    return jnp.where(
        wavelen < initial_context / high_freq,
        base_freqs,
        jnp.where(wavelen > initial_context / low_freq, base_freqs / rope_scale, middle),
    )


def angles_of(positions):
    turned = positions.astype(F32)[:, None] * frequencies()[None, :]
    return (jnp.cos(turned)[:, None, :], jnp.sin(turned)[:, None, :])


def rotate(values, cosine, sine):
    half = values.shape[-1] // 2
    first, second = values[..., :half], values[..., half:]
    return jnp.concatenate(
        [first * cosine - second * sine, second * cosine + first * sine], axis=-1
    )


def product(left, right):
    return jnp.dot(left, right, preferred_element_type=F32)


def product_t(left, right):
    return jnp.einsum("rc,dc->rd", left, right, preferred_element_type=F32)


def contract_rows(left, right):
    return jnp.einsum("ra,rb->ab", left, right, preferred_element_type=F32)


def norm_of(values):
    factor = lax.rsqrt(jnp.mean(values * values, axis=-1, keepdims=True) + epsilon)
    return (values * factor, factor)


def norm_backward(grad_hat, normed, factor):
    return factor * (grad_hat - normed * jnp.mean(grad_hat * normed, axis=-1, keepdims=True))


def pick(array, index, axis):
    return lax.dynamic_index_in_dim(array, index, axis, keepdims=False)


def put(buffer, block, *places):
    shape, start = list(buffer.shape), [0] * buffer.ndim
    for axis, index in places:
        shape[axis], start[axis] = 1, index
    return lax.dynamic_update_slice(buffer, block.reshape(shape), start)


def after(value, *others):
    return lax.optimization_barrier((value, *others))[0]


class Grid:
    def __init__(self):
        batch, seq = lax.axis_size("batch"), lax.axis_size("seq")
        self.cn, self.zn = 2, 4
        self.yn, self.xn = batch // self.cn, seq // self.zn
        b, s = lax.axis_index("batch"), lax.axis_index("seq")
        self.y, self.c = b // self.cn, b % self.cn
        self.z, self.x = s // self.xn, s % self.xn
        self.sizes = (self.yn, self.cn, self.zn, self.xn)

    def send(self, value, y=0, c=0, z=0, x=0):
        yn, cn, zn, xn = self.sizes
        pairs = []
        for i in range(yn * cn * zn * xn):
            here = (i // (cn * zn * xn), i // (zn * xn) % cn, i // xn % zn, i % xn)
            there = (here[0] ^ y, here[1] ^ c, here[2] ^ z, here[3] ^ x)
            pairs.append((i, ((there[0] * cn + there[1]) * zn + there[2]) * xn + there[3]))
        return lax.ppermute(value, ("batch", "seq"), pairs)

    def plane(self):
        return [(ky, kx) for ky in range(self.yn) for kx in range(self.xn) if ky or kx]


def attention_weights(grid, packed):
    rows, _, cols = packed.shape
    yn, cn, zn, xn = grid.sizes
    mine = jnp.zeros((yn, xn, rows, cols), BF)
    mine = put(mine, pick(packed, grid.y * xn + grid.x, 1), (0, grid.y), (1, grid.x))
    for ky, kx in grid.plane():
        there = (grid.y ^ ky) * xn + (grid.x ^ kx)
        got = grid.send(pick(packed, there, 1), y=ky, x=kx)
        mine = put(mine, got, (0, grid.y ^ ky), (1, grid.x ^ kx))
    full = jnp.zeros((yn, cn, zn, xn, rows, cols), BF)
    for kz in range(zn):
        block = grid.send(mine, z=kz) if kz else mine
        full = put(full, block, (1, grid.c), (2, grid.z ^ kz))
        full = put(full, grid.send(block, c=1), (1, grid.c ^ 1), (2, grid.z ^ kz))
    return full.reshape(-1, cols)


def attention_grads(grid, partial):
    yn, cn, zn, xn = grid.sizes
    cols = partial.shape[1]
    partial = partial.reshape(yn, cn, zn, xn, -1, cols)
    got = grid.send(pick(partial, grid.c ^ 1, 1).astype(BF), c=1)
    total = pick(partial, grid.c, 1) + got.astype(F32)
    mine = pick(total, grid.z, 1)
    for kz in range(1, zn):
        mine = mine + grid.send(pick(total, grid.z ^ kz, 1).astype(BF), z=kz).astype(F32)
    mine = mine.astype(BF)
    rows = mine.shape[2]
    result = jnp.zeros((rows, yn * xn, cols), BF)
    result = put(result, pick(pick(mine, grid.y, 0), grid.x, 0), (1, grid.y * xn + grid.x))
    for ky, kx in grid.plane():
        got = grid.send(pick(pick(mine, grid.y ^ ky, 0), grid.x ^ kx, 0), y=ky, x=kx)
        result = put(result, got, (1, (grid.y ^ ky) * xn + (grid.x ^ kx)))
    return result.astype(F32)


def ffn_weights_near(grid, weight):
    yn, cn, zn, xn = grid.sizes
    rows = weight.shape[0]
    weight = weight.reshape(rows, zn, cn, -1)
    cols = weight.shape[3]
    both = jnp.zeros((cn, rows, zn, cols), BF)
    both = put(both, pick(weight, grid.c, 2), (0, grid.c))
    both = put(both, grid.send(pick(weight, grid.c ^ 1, 2), c=1), (0, grid.c ^ 1))
    near = jnp.zeros((cn, zn, rows, cols), BF)
    for kz in range(zn):
        block = pick(both, grid.z ^ kz, 2)
        near = put(near, grid.send(block, z=kz) if kz else block, (1, grid.z ^ kz))
    return near


def ffn_weights_far(grid, near):
    yn, cn, zn, xn = grid.sizes
    _, _, rows, cols = near.shape
    half = cols // 2
    full = jnp.zeros((yn, cn, zn, xn, rows, cols), BF)
    full = put(full, near, (0, grid.y), (3, grid.x))
    over_x = {kx: grid.send(near, x=kx) for kx in range(1, xn)}
    over_y = {ky: grid.send(near, y=ky) for ky in range(1, yn)}
    for kx, got in over_x.items():
        full = put(full, got, (0, grid.y), (3, grid.x ^ kx))
    for ky, got in over_y.items():
        full = put(full, got, (0, grid.y ^ ky), (3, grid.x))
    for ky in over_y:
        for kx in over_x:
            low = grid.send(over_x[kx][..., :half], y=ky)
            high = grid.send(over_y[ky][..., half:], x=kx)
            both = jnp.concatenate([low, high], axis=-1)
            full = put(full, both, (0, grid.y ^ ky), (3, grid.x ^ kx))
    return full.reshape(-1, cols)


def ffn_grads(grid, partial):
    yn, cn, zn, xn = grid.sizes
    cols = partial.shape[1]
    half = cols // 2
    partial = partial.reshape(yn, cn, zn, xn, -1, cols)

    def sum_x(part, axis):
        total = pick(part, grid.x, axis).astype(F32)
        for kx in range(1, xn):
            total = total + grid.send(pick(part, grid.x ^ kx, axis), x=kx).astype(F32)
        return total.astype(BF)

    def sum_y(part):
        total = pick(part, grid.y, 0).astype(F32)
        for ky in range(1, yn):
            total = total + grid.send(pick(part, grid.y ^ ky, 0), y=ky).astype(F32)
        return total.astype(BF)

    low = sum_y(sum_x(partial[..., :half], 3))
    high = sum_x(sum_y(partial[..., half:]), 2)
    mine = jnp.concatenate([low, high], axis=-1)
    rows = mine.shape[2]
    wide = jnp.zeros((cn, rows, zn, cols), BF)
    for kz in range(zn):
        block = pick(mine, grid.z ^ kz, 1)
        wide = put(wide, grid.send(block, z=kz) if kz else block, (2, grid.z ^ kz))
    result = jnp.zeros((rows, zn, cn, cols), BF)
    result = put(result, pick(wide, grid.c, 0), (2, grid.c))
    result = put(result, grid.send(pick(wide, grid.c ^ 1, 0), c=1), (2, grid.c ^ 1))
    return result.reshape(rows, zn * cn * cols).astype(F32)


def gather_plane(grid, block):
    full = jnp.zeros((grid.yn, grid.xn) + block.shape, block.dtype)
    full = put(full, block, (0, grid.y), (1, grid.x))
    for ky, kx in grid.plane():
        full = put(full, grid.send(block, y=ky, x=kx), (0, grid.y ^ ky), (1, grid.x ^ kx))
    return full


def scatter_plane(grid, partial):
    total = pick(pick(partial, grid.y, 0), grid.x, 0)
    for ky, kx in grid.plane():
        block = pick(pick(partial, grid.y ^ ky, 0), grid.x ^ kx, 0).astype(BF)
        total = total + grid.send(block, y=ky, x=kx).astype(F32)
    return total


def exchange_z(grid, blocks):
    out = jnp.zeros_like(blocks)
    for kz in range(grid.zn):
        block = pick(blocks, grid.z ^ kz, 0)
        out = put(out, grid.send(block, z=kz) if kz else block, (0, grid.z ^ kz))
    return out


def gather_column(grid, block):
    own = [grid.send(block, z=kz) if kz else block for kz in range(grid.zn)]
    other = [grid.send(part, c=1) for part in own]
    return jnp.concatenate(own + other, axis=0)


def scatter_column(grid, near, far):
    total = near + grid.send(far.astype(BF), c=1).astype(F32)
    result = total[0]
    for kz in range(1, grid.zn):
        result = result + grid.send(total[kz].astype(BF), z=kz).astype(F32)
    return result


def causal_scores(query_block, keys, offset):
    scores = (
        jnp.einsum("qehd,ked->ehqk", query_block, keys, preferred_element_type=F32)
        * HEAD_DIM ** (-0.5)
    )
    row_ids = offset + jnp.arange(query_block.shape[0], dtype=jnp.int32)
    col_ids = jnp.arange(keys.shape[0], dtype=jnp.int32)
    return jnp.where(col_ids[None, :] <= row_ids[:, None], scores, -1e30)


def attention_forward(queries, keys, values):
    length = queries.shape[0]
    block_rows = min(512, length)

    def block(index):
        offset = index * block_rows
        scores = causal_scores(
            lax.dynamic_slice_in_dim(queries, offset, block_rows, 0), keys, offset
        )
        peak = jnp.max(scores, axis=-1, keepdims=True)
        expd = jnp.exp(scores - peak)
        totals = jnp.sum(expd, axis=-1, keepdims=True)
        probs = (expd / totals).astype(BF)
        attended = jnp.einsum("ehqk,ked->qehd", probs, values, preferred_element_type=F32)
        return (attended.astype(BF), (peak + jnp.log(totals))[..., 0])

    attended, logsums = lax.map(block, jnp.arange(length // block_rows, dtype=jnp.int32))
    return (attended.reshape(length, -1), logsums)


def attention_backward(queries, keys, values, grads, logsums):
    length = queries.shape[0]
    block_rows = min(512, length)
    scale = HEAD_DIM ** (-0.5)

    def block(carry, index):
        key_sum, value_sum = carry
        offset = index * block_rows
        query_block = lax.dynamic_slice_in_dim(queries, offset, block_rows, 0)
        grad_block = lax.dynamic_slice_in_dim(grads, offset, block_rows, 0)
        scores = causal_scores(query_block, keys, offset)
        probs = jnp.exp(scores - logsums[index][..., None])
        probs_low = probs.astype(BF)
        grad_probs = jnp.einsum("qehd,ked->ehqk", grad_block, values, preferred_element_type=F32)
        centred = jnp.sum(probs * grad_probs, axis=-1, keepdims=True)
        grad_scores = (probs * (grad_probs - centred)).astype(BF)
        grad_query = (
            jnp.einsum("ehqk,ked->qehd", grad_scores, keys, preferred_element_type=F32) * scale
        ).astype(BF)
        key_sum = key_sum + scale * jnp.einsum(
            "ehqk,qehd->ked", grad_scores, query_block, preferred_element_type=F32
        )
        value_sum = value_sum + jnp.einsum(
            "ehqk,qehd->ked", probs_low, grad_block, preferred_element_type=F32
        )
        return ((key_sum, value_sum), grad_query)

    zeros = jnp.zeros(keys.shape, F32)
    (key_sum, value_sum), grad_queries = lax.scan(
        block, (zeros, zeros), jnp.arange(length // block_rows, dtype=jnp.int32)
    )
    return (grad_queries.reshape(queries.shape), key_sum.astype(BF), value_sum.astype(BF))


def body(
    inputs,
    positions,
    attn_gain,
    q_weight,
    k_weight,
    v_weight,
    o_weight,
    ffn_gain,
    gate_weight,
    up_weight,
    down_weight,
    cotangent,
):
    grid = Grid()
    yn, cn, zn, xn = grid.sizes
    _, span, width = inputs.shape
    slices = yn * xn
    expanded = max(KV_HEADS, 2 * slices)
    copies = expanded // KV_HEADS
    rows = q_weight.shape[0]
    halves = zn // yn
    q_cols = HEADS * HEAD_DIM // (slices * halves)
    kv_cols = expanded * HEAD_DIM // (slices * halves)
    part_cols = q_cols + 2 * kv_cols
    kv_part = kv_cols // HEAD_DIM
    per_kv = q_cols // kv_cols
    length = zn * xn * span

    gain_one = attn_gain.astype(F32)[:, None]
    gain_two = ffn_gain.astype(F32)[:, None]

    def widen(weight):
        return jnp.repeat(weight.reshape(rows, KV_HEADS, HEAD_DIM), copies, axis=1)

    def parts(weight, cols):
        return weight.reshape(rows, slices, halves, cols)

    wide_k, wide_v = widen(k_weight), widen(v_weight)
    qkv_rows = jnp.concatenate(
        [parts(q_weight, q_cols), parts(wide_k, kv_cols), parts(wide_v, kv_cols)], axis=3
    ).reshape(rows, slices, halves * part_cols)
    qkv_scaled = (qkv_rows.astype(F32) * gain_one[:, :, None]).astype(BF)
    gate_scaled = (gate_weight.astype(F32) * gain_two).astype(BF)
    up_scaled = (up_weight.astype(F32) * gain_two).astype(BF)

    states = inputs.reshape(span, width).astype(F32)
    unit_one, factor_one = norm_of(states)
    unit_one_low = unit_one.astype(BF)
    tokens_one = gather_plane(grid, unit_one_low).reshape(-1, width)
    qkv_full = attention_weights(grid, qkv_scaled)
    o_full = attention_weights(
        grid, o_weight.reshape(rows, slices, halves * q_cols)
    )

    spots = jnp.zeros((yn, xn, span), jnp.int32)
    spots = gather_plane(grid, positions.reshape(span))
    spots = exchange_z(grid, jnp.repeat(spots, halves, axis=0).reshape(zn, xn * span))
    cosine, sine = angles_of(spots.reshape(length))

    projected = product(tokens_one, qkv_full).reshape(
        yn, xn * span, halves, part_cols
    )
    heads_cos, heads_sin = None, None
    plane_spots = gather_plane(grid, positions.reshape(span)).reshape(yn * xn * span)
    plane_cos, plane_sin = angles_of(plane_spots)
    turn = (projected[..., : q_cols + kv_cols]).reshape(yn * xn * span, -1, HEAD_DIM)
    turned = rotate(turn, plane_cos, plane_sin).astype(BF)
    turned = turned.reshape(yn, xn * span, halves, q_cols + kv_cols)
    packed = jnp.concatenate([turned, projected[..., q_cols + kv_cols :].astype(BF)], axis=3)
    packed = packed.transpose(0, 2, 1, 3).reshape(zn, xn * span, part_cols)
    heads_in = exchange_z(grid, packed).reshape(length, part_cols)
    queries = heads_in[:, :q_cols].reshape(length, kv_part, per_kv, HEAD_DIM)
    keys = heads_in[:, q_cols : q_cols + kv_cols].reshape(length, kv_part, HEAD_DIM)
    values = heads_in[:, q_cols + kv_cols :].reshape(length, kv_part, HEAD_DIM)

    attended, logsums = attention_forward(queries, keys, values)

    def to_tokens(heads, cols):
        back = exchange_z(grid, heads.reshape(zn, xn * span, cols))
        back = back.reshape(yn, halves, xn * span, cols).transpose(0, 2, 1, 3)
        return back.reshape(yn * xn * span, halves * cols)

    attn_tokens = to_tokens(attended, q_cols)
    hidden_one = states + scatter_plane(
        grid, product_t(attn_tokens, o_full).reshape(yn, xn, span, width)
    )

    near = [ffn_weights_near(grid, w) for w in (gate_scaled, up_scaled, down_weight)]
    gate_full, up_full, down_full = [ffn_weights_far(grid, n) for n in near]
    grad_low = cotangent.reshape(span, width)
    grad_out = grad_low.astype(F32)
    grad_tokens = gather_column(grid, grad_low)
    unit_two, factor_two = norm_of(hidden_one)
    tokens_two = gather_column(grid, unit_two.astype(BF))
    gate_act = product(tokens_two, gate_full)
    up_act = product(tokens_two, up_full)
    sigmoid_gate = jax.nn.sigmoid(gate_act)
    silu_gate = gate_act * sigmoid_gate
    hidden_low = (silu_gate * up_act).astype(BF)
    grad_hidden = product(grad_tokens, down_full)
    grad_gate = (
        grad_hidden * up_act * sigmoid_gate * (1.0 + gate_act * (1.0 - sigmoid_gate))
    ).astype(BF)
    grad_up = (grad_hidden * silu_gate).astype(BF)
    grad_unit = product_t(grad_gate, gate_full) + product_t(grad_up, up_full)
    grad_unit = grad_unit.reshape(cn, zn, span, width)
    grad_hat = scatter_column(grid, grad_unit[0], grad_unit[1])
    grad_one = grad_out + norm_backward(grad_hat, unit_two, factor_two)
    result = product_t(hidden_low, down_full).reshape(cn, zn, span, width)
    output = (hidden_one + scatter_column(grid, result[0], result[1])).astype(BF)

    gate_sum = ffn_grads(grid, contract_rows(tokens_two, grad_gate).astype(BF))
    up_sum = ffn_grads(grid, contract_rows(tokens_two, grad_up).astype(BF))
    down_grad = ffn_grads(grid, contract_rows(grad_tokens, hidden_low).astype(BF))
    gate_grad = gate_sum * gain_two
    up_grad = up_sum * gain_two
    ffn_gain_grad = jnp.sum(
        gate_sum * gate_weight.astype(F32) + up_sum * up_weight.astype(F32), axis=1
    )

    branch_tokens = gather_plane(grid, grad_one.astype(BF)).reshape(-1, width)
    grad_attn = product(branch_tokens, o_full).astype(BF)
    o_sum = attention_grads(grid, contract_rows(branch_tokens, attn_tokens))
    grad_attn = grad_attn.reshape(yn, xn * span, halves, q_cols).transpose(0, 2, 1, 3)
    grad_heads = exchange_z(grid, grad_attn.reshape(zn, xn * span, q_cols))
    grad_queries, grad_keys, grad_values = attention_backward(
        queries, keys, values, grad_heads.reshape(queries.shape), logsums
    )
    heads_out = jnp.concatenate(
        [
            grad_queries.reshape(length, q_cols),
            grad_keys.reshape(length, kv_cols),
            grad_values.reshape(length, kv_cols),
        ],
        axis=1,
    )
    turn = heads_out[:, : q_cols + kv_cols].astype(F32).reshape(length, -1, HEAD_DIM)
    turned = rotate(turn, cosine, -sine).astype(BF).reshape(length, q_cols + kv_cols)
    heads_out = jnp.concatenate([turned, heads_out[:, q_cols + kv_cols :]], axis=1)
    grad_qkv = to_tokens(heads_out, part_cols)
    grad_hat_one = scatter_plane(
        grid, product_t(grad_qkv, qkv_full).reshape(yn, xn, span, width)
    )
    input_grad = grad_one + norm_backward(grad_hat_one, unit_one, factor_one)
    qkv_sum = attention_grads(grid, contract_rows(tokens_one, grad_qkv))
    attn_gain_grad = jnp.sum(qkv_sum * qkv_rows.astype(F32), axis=(1, 2))
    qkv_grad = (qkv_sum * gain_one[:, :, None]).reshape(rows, slices, halves, part_cols)

    def narrow(part):
        part = part.reshape(rows, KV_HEADS, copies, HEAD_DIM).sum(axis=2)
        return part.reshape(rows, KV_HEADS * HEAD_DIM)

    q_grad = qkv_grad[..., :q_cols].reshape(rows, HEADS * HEAD_DIM)
    k_grad = narrow(qkv_grad[..., q_cols : q_cols + kv_cols])
    v_grad = narrow(qkv_grad[..., q_cols + kv_cols :])
    return (
        output.reshape(1, span, width),
        input_grad.reshape(1, span, width),
        attn_gain_grad,
        q_grad,
        k_grad,
        v_grad,
        o_sum.reshape(rows, HEADS * HEAD_DIM),
        ffn_gain_grad,
        gate_grad,
        up_grad,
        down_grad,
    )


def solution(mesh):
    tokens = P("batch", "seq", None)
    rows = P(("batch", "seq"), None)
    gain = P(("batch", "seq"))
    return jax.shard_map(
        body,
        mesh=mesh,
        in_specs=(
            tokens, P("batch", "seq"), gain, rows, rows, rows, rows, gain, rows, rows, rows, tokens
        ),
        out_specs=(tokens, tokens, gain, rows, rows, rows, rows, gain, rows, rows, rows),
        check_vma=False,
    )
```

time: 3620 us -> 1220 us (0.34)
  waiting for transfers between devices: 2940 us -> 530 us
  local copies, waits for them, and re-layouts: 93.8 us -> 342 us
  other arithmetic: 190 us -> 57 us
  matrix products: 256 us -> 136 us
  starting transfers between devices: 22.4 us -> 129 us
  blocking collectives: 92 us -> 0 us
    reduce_scatter x1 -> x0, waiting for transfers between devices: 1590 us -> none  [body(): lax.psum_scatter(jnp.concatenate([contract_rows(second_normalized_input,...]
    all_gather x7 -> x0, waiting for transfers between devices: 678 us -> none  [the longest x1 179 us: body(): lax.all_gather(down_weight, ('batch', 'seq'), axis=0, tiled=True)]
    unnamed x10 -> x0, waiting for transfers between devices: 600 us -> none
    ppermute x0 -> x134, waiting for transfers between devices: none -> 530 us  [send(): return lax.ppermute(value, ('batch', 'seq'), pairs)]
    concatenate x6 -> x3, other arithmetic: 162 us -> 0.14 us  [the longest x2 0.1 us: rotate(): jnp.concatenate([first * cosine - second * sine, second * cosine + first...]
    dynamic_update_slice x0 -> x103, local copies, waits for them, and re-layouts: none -> 143 us  [put(): return lax.dynamic_update_slice(buffer, block.reshape(shape), start)]
    ppermute x0 -> x134, starting transfers between devices: none -> 129 us  [send(): return lax.ppermute(value, ('batch', 'seq'), pairs)]
    dot_general x35 -> x29, matrix products: 256 us -> 136 us  [the longest x5 30.3 us: product_t(): return jnp.einsum('rc,dc->rd', left, right, preferred_element_type=F32)]
  transfers between devices with their start and end apart: 13 -> 134, of which waited for: 12 -> 72; matrix products, arithmetic and copies ran while one was open for 9% -> 39% of each run, Pallas kernels for 0% -> 0%
where the time goes in v1:
time: 1220 us; the launch traced here: 1200 us
  waiting for transfers between devices  530 us (43%)
  local copies, waits for them, and re-layouts  342 us (28%)
  matrix products  136 us (11%)
  starting transfers between devices  129 us (11%)
  other arithmetic  57 us (5%)
    ppermute x134, waiting for transfers between devices, send(): return lax.ppermute(value, ('batch', 'seq'), pairs)  530 us
    dynamic_update_slice x103, local copies, waits for them, and re-layouts, put(): return lax.dynamic_update_slice(buffer, block.reshape(shape), start)  143 us
    ppermute x134, starting transfers between devices, send(): return lax.ppermute(value, ('batch', 'seq'), pairs)  129 us
    dynamic_slice x22, local copies, waits for them, and re-layouts, pick(): return lax.dynamic_index_in_dim(array, index, axis, keepdims=False)  34.6 us
    unnamed x207, local copies, waits for them, and re-layouts  33.3 us
    dot_general x5, matrix products, product_t(): return jnp.einsum('rc,dc->rd', left, right, preferred_element_type=F32)  30.3 us
    dot_general x5, matrix products, product(): return jnp.dot(left, right, preferred_element_type=F32)  28.9 us
    dot_general x5, matrix products, contract_rows(): return jnp.einsum('ra,rb->ab', left, right, preferred_element_type=F32)  27.4 us
  transfers between devices with their start and end apart: 134, of which 72 were waited for; matrix products, arithmetic and copies ran while one was open for 39% of the time, Pallas kernels for 0%

profile of v1, /device:TPU:8, one launch (start us, length us, event | category | flops | bytes accessed | tf_op | source)
XLA Modules:
  0.0 1204.9 jit_solution(17565750689490532801)
XLA Ops:
  99.3 11.4 collective-permute-done.70
  115.7 18.3 %collective-permute-done.71 = bf16[128,2048]{1,0:T(8,128)(2,1)} collective-permute-done((bf16[128,2048]{1,0:T(8,128)(2,1)S(1)}, bf16[128,2048]{1,0:T(8,128)(2,1)}, u32[]{:S(2)}, u32[]{:S(2)}) %collective-permute-start.71) | collective-permute-done | bytes 524320 | tf_op jit(solution)/shard_map/ppermute | solution.py:102
  149.6 27.0 %collective-permute-done.72 = bf16[128,2048]{1,0:T(8,128)(2,1)} collective-permute-done((bf16[128,2048]{1,0:T(8,128)(2,1)S(1)}, bf16[128,2048]{1,0:T(8,128)(2,1)}, u32[]{:S(2)}, u32[]{:S(2)}) %collective-permute-start.72) | collective-permute-done | bytes 524320 | tf_op jit(solution)/shard_map/ppermute | solution.py:102
  185.3 14.4 %copy.428 = bf16[2048,512]{1,0:T(8,128)(2,1)} copy(bf16[2048,512]{0,1:T(8,128)(2,1)} %bitcast.212) | data formatting | bytes 4194304 | tf_op jit(solution)/shard_map/ra,rb->ab/dot_general | solution.py:58
  237.4 14.8 %collective-permute-done.52 = bf16[2,64,1024]{2,1,0:T(8,128)(2,1)S(1)} collective-permute-done((bf16[2,64,1024]{2,1,0:T(8,128)(2,1)S(1)}, bf16[2,64,1024]{2,1,0:T(8,128)(2,1)S(1)}, u32[]{:S(2)}, u32[]{:S(2)}) %collective-permute-start.52) | collective-permute-done | bytes 262176 | tf_op jit(solution)/shard_map/ppermute | solution.py:102
  341.1 18.7 %while.27 = (s32[]{:T(128)}, bf16[2,512,1,4,64]{1,4,3,2,0:T(8,128)(2,1)}, f32[2,1,4,512]{3,2,1,0:T(4,128)S(1)}, s32[2]{0:T(128)S(1)}, bf16[1024,1,4,64]{0,3,2,1:...) while((s32[]{:T(128)}, ...), condition=%wide.region_4.5_spmd, body=%wide.region_1.4_spmd.sunk | while | flops 562690560 | bytes 28119732 | solution.py:276
  414.6 11.3 collective-permute-done.33
  430.0 17.6 %collective-permute-done.46 = bf16[2,4,64,1024]{3,2,1,0:T(8,128)(2,1)} collective-permute-done((bf16[2,4,64,1024]{3,2,1,0:T(8,128)(2,1)}, bf16[2,4,64,1024]{3,2,1,0:T(8,128)(2,1)}, u32[]{:S(2)}, u32[]{:S(2)}) %collective-permute-start.46) | collective-permute-done | bytes 1048608 | tf_op jit(solution)/shard_map/ppermute | solution.py:102
  449.7 20.3 %collective-permute-done.54 = bf16[2,4,64,1024]{3,2,1,0:T(8,128)(2,1)S(1)} collective-permute-done((bf16[2,4,64,1024]{3,2,1,0:T(8,128)(2,1)S(1)}, bf16[2,4,64,1024]{3,2,1,0:T(8,128)(2,1)S(1)}, u32[]{:S(2)}, u32[]{:S(2)}) %collective-permute-start.54) | collective-permute-done | bytes 1048608 | tf_op jit(solution)/shard_map/ppermute | solution.py:102
  471.7 19.7 %collective-permute-done.62 = bf16[2,4,64,1024]{3,2,1,0:T(8,128)(2,1)S(1)} collective-permute-done((bf16[2,4,64,1024]{3,2,1,0:T(8,128)(2,1)}, bf16[2,4,64,1024]{3,2,1,0:T(8,128)(2,1)S(1)}, u32[]{:S(2)}, u32[]{:S(2)}) %collective-permute-start.62) | collective-permute-done | bytes 1048608 | tf_op jit(solution)/shard_map/ppermute | solution.py:102
  627.1 10.9 collective-permute-done.110
  646.0 14.5 %collective-permute-done.118 = bf16[2,2,4,64,512]{4,3,1,2,0:T(8,128)(2,1)S(1)} collective-permute-done((bf16[2,2,4,64,512]{4,3,1,2,0:T(8,128)(2,1)S(1)}, bf16[2,2,4,64,512]{4,3,1,2,0:T(8,128)(2,1)S(1)}, u32[]{:S(2)}, u32[]{:S(2)}) %collective-permute-start.118) | collective-permute-done | bytes 1048608 | tf_op jit(solution)/shard_map/ppermute | solution.py:102
  720.6 11.8 collective-permute-done.123
  743.0 16.2 %collective-permute-done.67 = bf16[128,2048]{1,0:T(8,128)(2,1)S(1)} collective-permute-done((bf16[128,2048]{1,0:T(8,128)(2,1)S(1)}, bf16[128,2048]{1,0:T(8,128)(2,1)S(1)}, u32[]{:S(2)}, u32[]{:S(2)}) %collective-permute-start.67) | collective-permute-done | bytes 524320 | tf_op jit(solution)/shard_map/ppermute | solution.py:102
  775.5 42.1 %collective-permute-done.69 = bf16[128,2048]{1,0:T(8,128)(2,1)S(1)} collective-permute-done((bf16[128,2048]{1,0:T(8,128)(2,1)S(1)}, bf16[128,2048]{1,0:T(8,128)(2,1)S(1)}, u32[]{:S(2)}, u32[]{:S(2)}) %collective-permute-start.69) | collective-permute-done | bytes 524320 | tf_op jit(solution)/shard_map/ppermute | solution.py:102
  828.3 11.8 collective-permute-done.80
  858.8 17.4 %dynamic_update_slice.461 = bf16[64,4,2,1024]{3,2,1,0:T(2,128)(2,1)} dynamic-update-slice(bf16[64,4,2,1024]{3,2,1,0:T(2,128)(2,1)} %broadcast.296.clone.2, bf16[64,4,1,1024]{3,2,1,0:T(2,128)(2,1)S(1)} %copy.453, s32[]{:T(128)} %constant.757.clone.1, s32[]{:T(128)} %constant.757.clone.1, s32[]{:T(128)S(6)} %select_n.426, s32[]{:T(128)} %constant.757.clone.1) | dynamic-update-slice | bytes 1048580 | tf_op jit(solution)/shard_map/dynamic_update_slice | solution.py:78
  878.1 17.7 %dynamic_update_slice.449 = bf16[64,4,2,1024]{3,2,1,0:T(2,128)(2,1)} dynamic-update-slice(bf16[64,4,2,1024]{3,2,1,0:T(2,128)(2,1)} %broadcast.296.clone.1, bf16[64,4,1,1024]{3,2,1,0:T(2,128)(2,1)} %copy.445, s32[]{:T(128)} %constant.757.clone.1, s32[]{:T(128)} %constant.757.clone.1, s32[]{:T(128)S(6)} %select_n.426, s32[]{:T(128)} %constant.757.clone.1) | dynamic-update-slice | bytes 1048580 | tf_op jit(solution)/shard_map/dynamic_update_slice | solution.py:78
  897.8 17.4 %dynamic_update_slice.455 = bf16[64,4,2,1024]{3,2,1,0:T(2,128)(2,1)} dynamic-update-slice(bf16[64,4,2,1024]{3,2,1,0:T(2,128)(2,1)} %broadcast.296.clone, bf16[64,4,1,1024]{3,2,1,0:T(2,128)(2,1)S(1)} %copy-done.27, s32[]{:T(128)} %constant.757.clone.1, s32[]{:T(128)} %constant.757.clone.1, s32[]{:T(128)S(6)} %select_n.426, s32[]{:T(128)} %constant.757.clone.1) | dynamic-update-slice | bytes 1048580 | tf_op jit(solution)/shard_map/dynamic_update_slice | solution.py:78
  917.4 17.4 %dynamic_update_slice.450 = bf16[64,4,2,1024]{3,2,1,0:T(2,128)(2,1)} dynamic-update-slice(bf16[64,4,2,1024]{3,2,1,0:T(2,128)(2,1)} %dynamic_update_slice.449, bf16[64,4,1,1024]{3,2,1,0:T(2,128)(2,1)S(1)} %copy.446, s32[]{:T(128)} %constant.757.clone.1, s32[]{:T(128)} %constant.757.clone.1, s32[]{:T(128)S(6)} %select_n.429, s32[]{:T(128)} %constant.757.clone.1) | dynamic-update-slice | bytes 1048580 | tf_op jit(solution)/shard_map/dynamic_update_slice | solution.py:78
  939.7 17.4 %dynamic_update_slice.456 = bf16[64,4,2,1024]{3,2,1,0:T(2,128)(2,1)} dynamic-update-slice(bf16[64,4,2,1024]{3,2,1,0:T(2,128)(2,1)} %dynamic_update_slice.455, bf16[64,4,1,1024]{3,2,1,0:T(2,128)(2,1)S(1)} %copy.450, s32[]{:T(128)} %constant.757.clone.1, s32[]{:T(128)} %constant.757.clone.1, s32[]{:T(128)S(6)} %select_n.429, s32[]{:T(128)} %constant.757.clone.1) | dynamic-update-slice | bytes 1048580 | tf_op jit(solution)/shard_map/dynamic_update_slice | solution.py:78
  964.3 11.0 collective-permute-done.83
  998.8 56.9 %while.28 = (s32[]{:T(128)}, f32[1024,1,64]{0,2,1:T(8,128)S(1)}, f32[1024,1,64]{0,2,1:T(8,128)}, bf16[2,512,1,4,64]{1,4,3,2,0:T(8,128)(2,1)S(1)}, s32[2]{0:T(128...) while((s32[]{:T(128)}, f32[1024,1,64]{0,2,1:T(8,128)S(1)}, ...), condition=%wide.region_9.10_spmd.clone, body=%wide.region_7.9_spmd.clone.sunk | while | flops 1374747136 | bytes 112390576 | solution.py:308
  1168.2 14.9 %collective-permute-done.98 = bf16[2,2,64,768]{3,2,1,0:T(8,128)(2,1)S(1)} collective-permute-done((bf16[2,2,64,768]{3,2,1,0:T(8,128)(2,1)S(1)}, bf16[2,2,64,768]{3,2,1,0:T(8,128)(2,1)S(1)}, u32[]{:S(2)}, u32[]{:S(2)}) %collective-permute-start.98) | collective-permute-done | bytes 393248 | tf_op jit(solution)/shard_map/ppermute | solution.py:102
  (854 shorter events, 818.8 us)
Async XLA Ops:
  3.9 132.0 %collective-permute-start = (bf16[128,2048]{1,0:T(8,128)(2,1)}, bf16[128,2048]{1,0:T(8,128)(2,1)}, u32[]{:S(2)}, u32[]{:S(2)}) collective-permute-start(bf16[128,2048]{1,0:T(8,128)(2,1)} %fusion.80), channel_id=1, source_target_pairs={{0,1},{1,0},{2,3},{3,2},{4,5},{5,4},{6,7},{7,6},{8,9},{9,8},{10,11... | collective-permute-start | bytes 1572872 | tf_op jit(solution)/shard_map/ppermute | solution.py:102
  5.4 135.9 %collective-permute-start.1 = (bf16[128,2048]{1,0:T(8,128)(2,1)}, bf16[128,2048]{1,0:T(8,128)(2,1)}, u32[]{:S(2)}, u32[]{:S(2)}) collective-permute-start(bf16[128,2048]{1,0:T(8,128)(2,1)} %fusion.80), channel_id=1, source_target_pairs={{0,16},{1,17},{2,18},{3,19},{4,20},{5,21},{6,22},{7,23},{8,24},{9,... | collective-permute-start | bytes 1572872 | tf_op jit(solution)/shard_map/ppermute | solution.py:102
  113.6 62.9 %collective-permute-start.72 = (bf16[128,2048]{1,0:T(8,128)(2,1)S(1)}, bf16[128,2048]{1,0:T(8,128)(2,1)}, u32[]{:S(2)}, u32[]{:S(2)}) collective-permute-start(bf16[128,2048]{1,0:T(8,128)(2,1)S(1)} %bitcast.1003), channel_id=1, source_target_pairs={{0,6},{1,7},{2,4},{3,5},{4,2},{5,3},{6,0},{7,1},{8,14},{9,15},{10,... | collective-permute-start | bytes 1572872 | tf_op jit(solution)/shard_map/ppermute | solution.py:102
  134.0 66.2 %collective-permute-start.73 = (bf16[128,2048]{1,0:T(8,128)(2,1)S(1)}, bf16[128,2048]{1,0:T(8,128)(2,1)}, u32[]{:S(2)}, u32[]{:S(2)}) collective-permute-start(bf16[128,2048]{1,0:T(8,128)(2,1)S(1)} %bitcast.1004), channel_id=1, source_target_pairs={{0,8},{1,9},{2,10},{3,11},{4,12},{5,13},{6,14},{7,15},{8,0},{9,1},... | collective-permute-start | bytes 1572872 | tf_op jit(solution)/shard_map/ppermute | solution.py:102
  141.3 58.5 %collective-permute-start.30 = (bf16[2,2,64,512]{3,2,1,0:T(8,128)(2,1)S(1)}, bf16[2,2,64,512]{3,2,1,0:T(8,128)(2,1)}, u32[]{:S(2)}, u32[]{:S(2)}) collective-permute-start(bf16[2,2,64,512]{3,2,1,0:T(8,128)(2,1)S(1)} %bitcast_dynamic-update-slice_fusion.81), channel_id=1, source_target_pairs={{0,6},{1,7},{2,4},{3,5},{4,2},{5,3},{6,0},{7,1},{8,14},{9,15},{10,... | collective-permute-start | bytes 786440 | tf_op jit(solution)/shard_map/ppermute | solution.py:102
  202.3 74.4 %collective-permute-start.8 = (bf16[2,2,64,768]{3,2,1,0:T(8,128)(2,1)}, bf16[2,2,64,768]{3,2,1,0:T(8,128)(2,1)S(1)}, u32[]{:S(2)}, u32[]{:S(2)}) collective-permute-start(bf16[2,2,64,768]{3,2,1,0:T(8,128)(2,1)} %copy-done.56), channel_id=1, source_target_pairs={{0,8},{1,9},{2,10},{3,11},{4,12},{5,13},{6,14},{7,15},{8,0},{9,1},... | collective-permute-start | bytes 1179656 | tf_op jit(solution)/shard_map/ppermute | solution.py:102
  204.2 76.1 %collective-permute-start.10 = (bf16[2,2,64,768]{3,2,1,0:T(8,128)(2,1)}, bf16[2,2,64,768]{3,2,1,0:T(8,128)(2,1)S(1)}, u32[]{:S(2)}, u32[]{:S(2)}) collective-permute-start(bf16[2,2,64,768]{3,2,1,0:T(8,128)(2,1)} %collective-permute-done.9), channel_id=1, source_target_pairs={{0,8},{1,9},{2,10},{3,11},{4,12},{5,13},{6,14},{7,15},{8,0},{9,1},... | collective-permute-start | bytes 1179656 | tf_op jit(solution)/shard_map/ppermute | solution.py:102
  204.2 78.7 %collective-permute-start.12 = (bf16[2,2,64,768]{3,2,1,0:T(8,128)(2,1)}, bf16[2,2,64,768]{3,2,1,0:T(8,128)(2,1)S(1)}, u32[]{:S(2)}, u32[]{:S(2)}) collective-permute-start(bf16[2,2,64,768]{3,2,1,0:T(8,128)(2,1)} %collective-permute-done.11), channel_id=1, source_target_pairs={{0,8},{1,9},{2,10},{3,11},{4,12},{5,13},{6,14},{7,15},{8,0},{9,1},... | collective-permute-start | bytes 1179656 | tf_op jit(solution)/shard_map/ppermute | solution.py:102
  275.3 124.7 %collective-permute-start.74 = (bf16[128,2048]{1,0:T(8,128)(2,1)}, bf16[128,2048]{1,0:T(8,128)(2,1)}, u32[]{:S(2)}, u32[]{:S(2)}) collective-permute-start(bf16[128,2048]{1,0:T(8,128)(2,1)} %collective-permute-done.70), channel_id=1, source_target_pairs={{0,8},{1,9},{2,10},{3,11},{4,12},{5,13},{6,14},{7,15},{8,0},{9,1},... | collective-permute-start | bytes 1572872 | tf_op jit(solution)/shard_map/ppermute | solution.py:102
  276.7 127.4 %collective-permute-start.75 = (bf16[128,2048]{1,0:T(8,128)(2,1)}, bf16[128,2048]{1,0:T(8,128)(2,1)}, u32[]{:S(2)}, u32[]{:S(2)}) collective-permute-start(bf16[128,2048]{1,0:T(8,128)(2,1)} %collective-permute-done.71), channel_id=1, source_target_pairs={{0,8},{1,9},{2,10},{3,11},{4,12},{5,13},{6,14},{7,15},{8,0},{9,1},... | collective-permute-start | bytes 1572872 | tf_op jit(solution)/shard_map/ppermute | solution.py:102
  280.3 126.4 %collective-permute-start.76 = (bf16[128,2048]{1,0:T(8,128)(2,1)}, bf16[128,2048]{1,0:T(8,128)(2,1)}, u32[]{:S(2)}, u32[]{:S(2)}) collective-permute-start(bf16[128,2048]{1,0:T(8,128)(2,1)} %collective-permute-done.72), channel_id=1, source_target_pairs={{0,8},{1,9},{2,10},{3,11},{4,12},{5,13},{6,14},{7,15},{8,0},{9,1},... | collective-permute-start | bytes 1572872 | tf_op jit(solution)/shard_map/ppermute | solution.py:102
  426.2 65.3 %collective-permute-start.62 = (bf16[2,4,64,1024]{3,2,1,0:T(8,128)(2,1)}, bf16[2,4,64,1024]{3,2,1,0:T(8,128)(2,1)S(1)}, u32[]{:S(2)}, u32[]{:S(2)}) collective-permute-start(bf16[2,4,64,1024]{3,2,1,0:T(8,128)(2,1)} %bitcast_dynamic-update-slice_fusion.46), channel_id=1, source_target_pairs={{0,1},{1,0},{2,3},{3,2},{4,5},{5,4},{6,7},{7,6},{8,9},{9,8},{10,11... | collective-permute-start | bytes 3145736 | tf_op jit(solution)/shard_map/ppermute | solution.py:102
  616.8 115.6 %collective-permute-start.66 = (bf16[4,128,2048]{2,1,0:T(8,128)(2,1)S(1)}, bf16[4,128,2048]{2,1,0:T(8,128)(2,1)S(1)}, u32[]{:S(2)}, u32[]{:S(2)}) collective-permute-start(bf16[4,128,2048]{2,1,0:T(8,128)(2,1)S(1)} %bitcast.1005), channel_id=1, source_target_pairs={{0,8},{1,9},{2,10},{3,11},{4,12},{5,13},{6,14},{7,15},{8,0},{9,1},... | collective-permute-start | bytes 6291464 | tf_op jit(solution)/shard_map/ppermute | solution.py:102
  625.5 111.7 %collective-permute-start.77 = (bf16[4,128,2048]{2,1,0:T(8,128)(2,1)}, bf16[4,128,2048]{2,1,0:T(8,128)(2,1)S(1)}, u32[]{:S(2)}, u32[]{:S(2)}) collective-permute-start(bf16[4,128,2048]{2,1,0:T(8,128)(2,1)} %bitcast.168), channel_id=1, source_target_pairs={{0,8},{1,9},{2,10},{3,11},{4,12},{5,13},{6,14},{7,15},{8,0},{9,1},... | collective-permute-start | bytes 6291464 | tf_op jit(solution)/shard_map/ppermute | solution.py:102
  737.2 80.5 %collective-permute-start.69 = (bf16[128,2048]{1,0:T(8,128)(2,1)S(1)}, bf16[128,2048]{1,0:T(8,128)(2,1)S(1)}, u32[]{:S(2)}, u32[]{:S(2)}) collective-permute-start(bf16[128,2048]{1,0:T(8,128)(2,1)S(1)} %get-tuple-element.240), channel_id=1, source_target_pairs={{0,6},{1,7},{2,4},{3,5},{4,2},{5,3},{6,0},{7,1},{8,14},{9,15},{10,... | collective-permute-start | bytes 1572872 | tf_op jit(solution)/shard_map/ppermute | solution.py:102
  739.0 80.6 %collective-permute-start.78 = (bf16[128,2048]{1,0:T(8,128)(2,1)S(1)}, bf16[128,2048]{1,0:T(8,128)(2,1)S(1)}, u32[]{:S(2)}, u32[]{:S(2)}) collective-permute-start(bf16[128,2048]{1,0:T(8,128)(2,1)S(1)} %get-tuple-element.236), channel_id=1, source_target_pairs={{0,2},{1,3},{2,0},{3,1},{4,6},{5,7},{6,4},{7,5},{8,10},{9,11},{10,... | collective-permute-start | bytes 1572872 | tf_op jit(solution)/shard_map/ppermute | solution.py:102
  741.8 86.5 %collective-permute-start.79 = (bf16[128,2048]{1,0:T(8,128)(2,1)S(1)}, bf16[128,2048]{1,0:T(8,128)(2,1)S(1)}, u32[]{:S(2)}, u32[]{:S(2)}) collective-permute-start(bf16[128,2048]{1,0:T(8,128)(2,1)S(1)} %get-tuple-element.238), channel_id=1, source_target_pairs={{0,4},{1,5},{2,6},{3,7},{4,0},{5,1},{6,2},{7,3},{8,12},{9,13},{10,... | collective-permute-start | bytes 1572872 | tf_op jit(solution)/shard_map/ppermute | solution.py:102
  759.2 81.0 %collective-permute-start.80 = (bf16[128,2048]{1,0:T(8,128)(2,1)S(1)}, bf16[128,2048]{1,0:T(8,128)(2,1)S(1)}, u32[]{:S(2)}, u32[]{:S(2)}) collective-permute-start(bf16[128,2048]{1,0:T(8,128)(2,1)S(1)} %get-tuple-element.237), channel_id=1, source_target_pairs={{0,6},{1,7},{2,4},{3,5},{4,2},{5,3},{6,0},{7,1},{8,14},{9,15},{10,... | collective-permute-start | bytes 1572872 | tf_op jit(solution)/shard_map/ppermute | solution.py:102
  772.1 73.2 %collective-permute-start.131 = (bf16[2,64,1024]{2,1,0:T(8,128)(2,1)S(1)}, bf16[2,64,1024]{2,1,0:T(8,128)(2,1)S(1)}, u32[]{:S(2)}, u32[]{:S(2)}) collective-permute-start(bf16[2,64,1024]{2,1,0:T(8,128)(2,1)S(1)} %get-tuple-element.250), channel_id=1, source_target_pairs={{0,4},{1,5},{2,6},{3,7},{4,0},{5,1},{6,2},{7,3},{8,12},{9,13},{10,... | collective-permute-start | bytes 786440 | tf_op jit(solution)/shard_map/ppermute | solution.py:102
  819.6 95.7 %collective-permute-start.117 = (bf16[64,4,1024]{2,0,1:T(8,128)(2,1)}, bf16[64,4,1024]{2,0,1:T(8,128)(2,1)}, u32[]{:S(2)}, u32[]{:S(2)}) collective-permute-start(bf16[64,4,1024]{2,0,1:T(8,128)(2,1)} %get-tuple-element.256), channel_id=1, source_target_pairs={{0,8},{1,9},{2,10},{3,11},{4,12},{5,13},{6,14},{7,15},{8,0},{9,1},... | collective-permute-start | bytes 1572872 | tf_op jit(solution)/shard_map/ppermute | solution.py:102
  828.3 109.2 %collective-permute-start.125 = (bf16[64,4,1024]{2,0,1:T(8,128)(2,1)}, bf16[64,4,1024]{2,0,1:T(8,128)(2,1)}, u32[]{:S(2)}, u32[]{:S(2)}) collective-permute-start(bf16[64,4,1024]{2,0,1:T(8,128)(2,1)} %get-tuple-element.251), channel_id=1, source_target_pairs={{0,8},{1,9},{2,10},{3,11},{4,12},{5,13},{6,14},{7,15},{8,0},{9,1},... | collective-permute-start | bytes 1572872 | tf_op jit(solution)/shard_map/ppermute | solution.py:102
  843.7 118.4 %collective-permute-start.81 = (bf16[128,2048]{1,0:T(8,128)(2,1)}, bf16[128,2048]{1,0:T(8,128)(2,1)}, u32[]{:S(2)}, u32[]{:S(2)}) collective-permute-start(bf16[128,2048]{1,0:T(8,128)(2,1)} %get-tuple-element.186), channel_id=1, source_target_pairs={{0,1},{1,0},{2,3},{3,2},{4,5},{5,4},{6,7},{7,6},{8,9},{9,8},{10,11... | collective-permute-start | bytes 1572872 | tf_op jit(solution)/shard_map/ppermute | solution.py:102
  849.6 113.5 %collective-permute-start.82 = (bf16[128,2048]{1,0:T(8,128)(2,1)}, bf16[128,2048]{1,0:T(8,128)(2,1)}, u32[]{:S(2)}, u32[]{:S(2)}) collective-permute-start(bf16[128,2048]{1,0:T(8,128)(2,1)} %get-tuple-element.186), channel_id=1, source_target_pairs={{0,16},{1,17},{2,18},{3,19},{4,20},{5,21},{6,22},{7,23},{8,24},{9,... | collective-permute-start | bytes 1572872 | tf_op jit(solution)/shard_map/ppermute | solution.py:102
  852.1 252.6 %collective-permute-start.133 = (bf16[64,4,1024]{2,0,1:T(8,128)(2,1)}, bf16[64,4,1024]{2,0,1:T(8,128)(2,1)}, u32[]{:S(2)}, u32[]{:S(2)}) collective-permute-start(bf16[64,4,1024]{2,0,1:T(8,128)(2,1)} %get-tuple-element.246), channel_id=1, source_target_pairs={{0,8},{1,9},{2,10},{3,11},{4,12},{5,13},{6,14},{7,15},{8,0},{9,1},... | collective-permute-start | bytes 1572872 | tf_op jit(solution)/shard_map/ppermute | solution.py:102
  (213 other events, 3980.9 us)

commit v2 on v1

v2 whole, which is shorter than its diff:
```python
import functools
import math

import jax
import jax.numpy as jnp
import numpy as np
from jax import lax
from jax.experimental import pallas as pl
from jax.experimental.pallas import tpu as pltpu
from jax.sharding import Mesh, PartitionSpec as P

HEADS = 32
KV_HEADS = 8
HEAD_DIM = 64

epsilon = 1e-05
rope_base = 500000.0
rope_scale = 32.0
low_freq = 1.0
high_freq = 4.0
initial_context = 8192.0

BF = jnp.bfloat16
F32 = jnp.float32


def frequencies():
    half = HEAD_DIM // 2
    base_freqs = rope_base ** (-(jnp.arange(half, dtype=F32) * 2.0 / HEAD_DIM))
    wavelen = 2.0 * math.pi / base_freqs
    smooth = (initial_context / wavelen - low_freq) / (high_freq - low_freq)
    middle = (1.0 - smooth) * base_freqs / rope_scale + smooth * base_freqs
    return jnp.where(
        wavelen < initial_context / high_freq,
        base_freqs,
        jnp.where(wavelen > initial_context / low_freq, base_freqs / rope_scale, middle),
    )


def angles_of(positions):
    turned = positions.astype(F32)[:, None] * frequencies()[None, :]
    return (jnp.cos(turned), jnp.sin(turned))


def contract_rows(left, right):
    return jnp.einsum("ra,rb->ab", left, right, preferred_element_type=F32)


def product_t(left, right):
    return jnp.einsum("rc,dc->rd", left, right, preferred_element_type=F32)


def product(left, right):
    return jnp.dot(left, right, preferred_element_type=F32)


def norm_of(values):
    factor = lax.rsqrt(jnp.mean(values * values, axis=-1, keepdims=True) + epsilon)
    return (values * factor, factor)


def norm_backward(grad_hat, normed, factor):
    return factor * (grad_hat - normed * jnp.mean(grad_hat * normed, axis=-1, keepdims=True))


def pick(array, index, axis):
    return lax.dynamic_index_in_dim(array, index, axis, keepdims=False)


def put(buffer, block, *places):
    shape, start = list(buffer.shape), [0] * buffer.ndim
    for axis, index in places:
        shape[axis], start[axis] = 1, index
    return lax.dynamic_update_slice(buffer, block.reshape(shape), start)


def after(value, *others):
    zero = jnp.zeros((), value.dtype)
    for array in others:
        first = array[(0,) * array.ndim]
        zero = zero + (first != first).astype(value.dtype)
    corner = value[tuple(slice(0, min(n, 16 if i < value.ndim - 1 else 128)) if i >= value.ndim - 2
                         else slice(0, 1) for i, n in enumerate(value.shape))]
    return lax.dynamic_update_slice(value, corner + zero, (0,) * value.ndim)


PLANE = ("y", "x")
COLUMN = ("c", "z")


def place(axes):
    return lax.axis_index(axes), lax.axis_size(axes)


def trade(value, axes, step):
    count = lax.axis_size(axes)
    return lax.ppermute(value, axes, [(i, i ^ step) for i in range(count)])


def swap(blocks, axes, at=0):
    here, count = place(axes)
    return [pick(blocks, here, at)] + [
        trade(pick(blocks, here ^ k, at), axes, k) for k in range(1, count)
    ]


def spread(block, axes):
    count = lax.axis_size(axes)
    return [block] + [trade(block, axes, k) for k in range(1, count)]


def in_order(blocks, axes):
    here, count = place(axes)
    out = jnp.zeros((count,) + blocks[0].shape, blocks[0].dtype)
    for k, block in enumerate(blocks):
        out = put(out, block, (0, here ^ k))
    return out


def total(blocks):
    result = blocks[0].astype(F32)
    for block in blocks[1:]:
        result = result + block.astype(F32)
    return result


def order_kernel(order, group, in_ref, out_ref):
    wide = max(group, 128)
    for at in range(0, out_ref.shape[1], wide):
        first = at // group
        parts = [
            in_ref[:, j * group : (j + 1) * group] for j in order[first : first + wide // group]
        ]
        out_ref[:, at : at + wide] = jnp.concatenate(parts, axis=1).astype(out_ref.dtype)


def reorder(features, sizes, before, dtype):
    later = "yxcz" if before == "yczx" else "yczx"
    count = math.prod(sizes.values())
    axes = np.arange(count).reshape([sizes[axis] for axis in before])
    order = axes.transpose([before.index(axis) for axis in later]).reshape(-1).tolist()
    return in_vmem(
        functools.partial(order_kernel, order, features.shape[1] // count),
        [features],
        [jax.ShapeDtypeStruct(features.shape, dtype)],
        [],
        0,
    )[0]


def attention_weights(mine, sizes, splits):
    yn, cn, zn, xn = [sizes[axis] for axis in "yczx"]
    rows = mine.shape[1]
    core, column = lax.axis_index("c"), lax.axis_index("z")
    own = spread(mine, "z")
    results = []
    for start, end in splits:
        full = jnp.zeros((yn * xn, cn, zn, rows, end - start), BF)
        for k in range(zn):
            full = put(full, own[k][..., start:end], (1, core), (2, column ^ k))
        other = trade(pick(full, core, 1), "c", 1)
        results.append(put(full, other, (1, core ^ 1)).reshape(-1, end - start))
    return results, own[1:]


def attention_grads(partial, sizes, *earlier):
    yn, cn, zn, xn = [sizes[axis] for axis in "yczx"]
    cols = partial.shape[-1]
    blocks = partial.reshape(yn * xn, cn, zn, -1, cols)
    core = lax.axis_index("c")
    got = trade(pick(blocks, core ^ 1, 1).astype(BF), "c", 1)
    near = (pick(blocks, core, 1) + got.astype(F32)).astype(BF)
    there = swap(after(near, *earlier), "z", 1)
    mine = total(there).astype(BF)
    return in_order(swap(mine, PLANE), PLANE).astype(F32), there[1:]


def all_to_all(blocks, axes):
    return lax.all_to_all(blocks, axes, split_axis=0, concat_axis=0, tiled=True)


def ffn_weights_near(weights, sizes):
    slices = sizes["c"] * sizes["z"]
    split = [w.reshape(w.shape[0], slices, -1).transpose(1, 0, 2) for w in weights]
    return all_to_all(jnp.concatenate(split, axis=2), COLUMN)


def ffn_weights_far(near):
    full = lax.all_gather(near, PLANE, axis=0, tiled=False)
    return full.reshape(-1, near.shape[-1])


def ffn_grads(partial, sizes):
    cols = partial.shape[-1]
    blocks = partial.reshape(sizes["y"] * sizes["x"], -1, cols)
    mine = lax.psum_scatter(blocks, PLANE, scatter_dimension=0, tiled=False)
    return mine.reshape(sizes["c"], sizes["z"], -1, cols)


def ffn_grads_near(mine, *earlier):
    core, column = lax.axis_index("c"), lax.axis_index("z")
    own = pick(mine, core, 0)
    other = after(trade(pick(mine, core ^ 1, 0), "c", 1), *earlier)
    parts = []
    for k in range(mine.shape[1]):
        part = jnp.stack([pick(own, column ^ k, 0), pick(other, column ^ k, 0)])
        parts.append(trade(part, "z", k) if k else part)
    return parts


def ffn_slices(sizes):
    core, column = lax.axis_index("c"), lax.axis_index("z")
    spots = [
        other * sizes["z"] + (column ^ k) for k in range(sizes["z"]) for other in (core, core ^ 1)
    ]
    return jnp.stack(spots).astype(jnp.int32)


def scatter_plane(partial):
    return total(list(all_to_all(partial, PLANE)))


def gather(block, axes):
    copies = jnp.broadcast_to(block, (lax.axis_size(axes),) + block.shape)
    return all_to_all(copies, axes)


VMEM_BYTES = 56 * 1024 * 1024
TILE = 256
NT = (((1,), (1,)), ((), ()))


def mm(left, right):
    return jnp.dot(left, right, preferred_element_type=F32)


def mm_nt(left, right):
    return lax.dot_general(left, right, NT, preferred_element_type=F32)


def causal(scores, start, tile):
    keys = lax.broadcasted_iota(jnp.int32, (tile, tile), 0)
    queries = lax.broadcasted_iota(jnp.int32, (tile, tile), 1)
    last = jnp.where(keys <= queries, scores[start:], -1e30)
    return last if start == 0 else jnp.concatenate([scores[:start], last], axis=0)


def forward_kernel(q_cols, kv_cols, seq, result, logsums):
    length = seq.shape[0]
    tile = min(TILE, length)
    per_kv = q_cols // kv_cols
    for e in range(kv_cols // HEAD_DIM):
        at = q_cols + e * HEAD_DIM
        keys = seq[:, at : at + HEAD_DIM]
        at = q_cols + kv_cols + e * HEAD_DIM
        values_t = seq[:, at : at + HEAD_DIM].T
        for start in range(0, length, tile):
            end = start + tile
            turned = []
            for h in range(e * per_kv, (e + 1) * per_kv):
                queries = seq[start:end, h * HEAD_DIM : (h + 1) * HEAD_DIM]
                scores = causal(mm_nt(keys[:end], queries) * HEAD_DIM ** (-0.5), start, tile)
                peak = jnp.max(scores, axis=0, keepdims=True)
                expd = jnp.exp(scores - peak)
                sums = jnp.sum(expd, axis=0, keepdims=True)
                logsums[h : h + 1, start:end] = peak + jnp.log(sums)
                probs = (expd * (1.0 / sums)).astype(BF)
                turned.append(mm(values_t[:, :end], probs))
            at = e * per_kv * HEAD_DIM
            result[start:end, at : at + per_kv * HEAD_DIM] = (
                jnp.concatenate(turned, axis=0).T.astype(BF)
            )


def backward_kernel(q_cols, kv_cols, seq, grads, logsums, result, key_sum, value_sum):
    length = seq.shape[0]
    tile = min(TILE, length)
    per_kv = q_cols // kv_cols
    scale = HEAD_DIM ** (-0.5)
    for e in range(kv_cols // HEAD_DIM):
        key_at = q_cols + e * HEAD_DIM
        value_at = q_cols + kv_cols + e * HEAD_DIM
        keys = seq[:, key_at : key_at + HEAD_DIM]
        keys_t = keys.T
        values = seq[:, value_at : value_at + HEAD_DIM]
        key_sum[...] = jnp.zeros_like(key_sum)
        value_sum[...] = jnp.zeros_like(value_sum)
        for start in range(0, length, tile):
            end = start + tile
            turned = []
            for h in range(e * per_kv, (e + 1) * per_kv):
                at = h * HEAD_DIM
                queries = seq[start:end, at : at + HEAD_DIM]
                grad = grads[start:end, at : at + HEAD_DIM]
                scores = causal(mm_nt(keys[:end], queries) * scale, start, tile)
                probs = jnp.exp(scores - logsums[h : h + 1, start:end])
                grad_probs = mm_nt(values[:end], grad)
                centred = jnp.sum(probs * grad_probs, axis=0, keepdims=True)
                grad_scores = (probs * (grad_probs - centred)).astype(BF)
                value_sum[:end, :] += mm(probs.astype(BF), grad)
                key_sum[:end, :] += mm(grad_scores, queries)
                turned.append(mm(keys_t[:, :end], grad_scores))
            at = e * per_kv * HEAD_DIM
            result[start:end, at : at + per_kv * HEAD_DIM] = (
                jnp.concatenate(turned, axis=0).T * scale
            ).astype(BF)
        result[:, key_at : key_at + HEAD_DIM] = (key_sum[...] * scale).astype(BF)
        result[:, value_at : value_at + HEAD_DIM] = value_sum[...].astype(BF)


def turn(values, cosine, sine, rotated):
    lane = lax.broadcasted_iota(jnp.int32, cosine.shape, 1)
    first_half = lane % HEAD_DIM < HEAD_DIM // 2
    parts = []
    for tile in range(values.shape[1] // 128):
        part = values[:, tile * 128 : (tile + 1) * 128]
        low, high = rotated[2 * tile], rotated[2 * tile + 1]
        if low or high:
            left = pltpu.roll(part, 128 - HEAD_DIM // 2, 1)
            right = pltpu.roll(part, HEAD_DIM // 2, 1)
            moved = part * cosine + jnp.where(first_half, left, right) * sine
            if low and high:
                part = moved
            else:
                part = jnp.where((lane < HEAD_DIM) == low, moved, part)
        parts.append(part)
    return jnp.concatenate(parts, axis=1)


def qkv_kernel(halves, rotated, x_ref, w_ref, cosine, sine, out_ref):
    piece, part = out_ref.shape[1:]
    for y in range(out_ref.shape[0] // halves):
        rows = pl.ds(y * piece, piece)
        values = mm(x_ref[rows, : w_ref.shape[0]], w_ref[...])
        values = turn(values, cosine[rows, :], sine[rows, :], rotated).astype(BF)
        for h in range(halves):
            out_ref[y * halves + h] = values[:, h * part : (h + 1) * part]


def qkv_back_kernel(halves, rotated, blocks, w_ref, cosine, sine, grad_ref, out_ref):
    count, piece = blocks.shape[:2]
    for y in range(count // halves):
        rows = pl.ds(y * piece, piece)
        values = jnp.concatenate([blocks[y * halves + h] for h in range(halves)], axis=1)
        values = turn(values.astype(F32), cosine[rows, :], -sine[rows, :], rotated).astype(BF)
        grad_ref[rows, :] = values
        part = mm_nt(values, w_ref[...]).astype(BF)
        for x in range(piece // out_ref.shape[1]):
            out_ref[y * (piece // out_ref.shape[1]) + x] = part[
                x * out_ref.shape[1] : (x + 1) * out_ref.shape[1]
            ]


def o_kernel(halves, blocks, w_ref, tokens_ref, out_ref):
    count, piece = blocks.shape[:2]
    for y in range(count // halves):
        rows = pl.ds(y * piece, piece)
        values = jnp.concatenate([blocks[y * halves + h] for h in range(halves)], axis=1)
        tokens_ref[rows, :] = values
        part = mm_nt(values, w_ref[...]).astype(BF)
        for x in range(piece // out_ref.shape[1]):
            out_ref[y * (piece // out_ref.shape[1]) + x] = part[
                x * out_ref.shape[1] : (x + 1) * out_ref.shape[1]
            ]


def ffn_kernel(tiles, *refs):
    x_ref, dy_ref, gate_ref, up_ref, down_ref, gate_rows, up_rows = refs[:7]
    z_ref, dgate_ref, dup_ref, dx_ref, held_gate, held_up = refs[7:]
    step = pl.program_id(0)
    tile = gate_ref.shape[1]
    for i in range(tiles):

        @pl.when(step == i)
        def _():
            gate = mm(x_ref[...], gate_ref[...])
            up = mm(x_ref[...], up_ref[...])
            dz = mm(dy_ref[...], down_ref[...])
            sigmoid = jax.nn.sigmoid(gate)
            silu = gate * sigmoid
            z_ref[...] = (silu * up).astype(BF)
            dgate = (dz * up * sigmoid * (1.0 + gate * (1.0 - sigmoid))).astype(BF)
            dup = (dz * silu).astype(BF)
            dgate_ref[...] = dgate
            dup_ref[...] = dup
            held_gate[:, i * tile : (i + 1) * tile] = dgate
            held_up[:, i * tile : (i + 1) * tile] = dup

    @pl.when(step >= tiles)
    def _():
        part = mm_nt(held_gate[...], gate_rows[...]) + mm_nt(held_up[...], up_rows[...])
        dx_ref[...] = part.astype(dx_ref.dtype)


def ffn(tokens, grads, weights, out_dtype):
    count, width = tokens.shape
    units = weights.shape[1] // 3
    tile, row_tile = min(256, units), min(1024, width)
    tiles, row_tiles = units // tile, width // row_tile

    def first(i):
        return jnp.minimum(i, tiles - 1)

    def second(i):
        return jnp.maximum(i - tiles, 0)

    whole = pl.BlockSpec((count, width), lambda i: (0, 0))
    narrow = pl.BlockSpec((count, tile), lambda i: (0, first(i)))
    columns = [
        pl.BlockSpec((width, tile), lambda i, j=j: (0, j * tiles + first(i))) for j in range(3)
    ]
    across = [pl.BlockSpec((row_tile, units), lambda i, j=j: (second(i), j)) for j in range(2)]
    hidden = jax.ShapeDtypeStruct((count, units), BF)
    return pl.pallas_call(
        functools.partial(ffn_kernel, tiles),
        grid=(tiles + row_tiles,),
        out_shape=[hidden] * 3 + [jax.ShapeDtypeStruct((count, width), out_dtype)],
        in_specs=[whole, whole] + columns + across,
        out_specs=[narrow] * 3 + [pl.BlockSpec((count, row_tile), lambda i: (0, second(i)))],
        scratch_shapes=[pltpu.VMEM((count, units), BF)] * 2,
        compiler_params=pltpu.CompilerParams(vmem_limit_bytes=VMEM_BYTES),
        cost_estimate=pl.CostEstimate(flops=1, bytes_accessed=1, transcendentals=0),
    )(tokens, grads, *[weights] * 5)


def add_product_kernel(z_ref, down_ref, *refs):
    part = mm_nt(z_ref[...], down_ref[...])
    for held in refs[:-1]:
        part = part + held[...].astype(F32)
    refs[-1][...] = part.astype(BF)


def add_product(z, weights, *added):
    count, units = z.shape
    width = weights.shape[0]
    tile = min(512, width)
    part = pl.BlockSpec((count, tile), lambda i: (0, i))
    return pl.pallas_call(
        add_product_kernel,
        grid=(width // tile,),
        out_shape=jax.ShapeDtypeStruct((count, width), BF),
        in_specs=[
            pl.BlockSpec((count, units), lambda i: (0, 0)),
            pl.BlockSpec((tile, units), lambda i: (i, 2)),
        ]
        + [part] * len(added),
        out_specs=part,
        compiler_params=pltpu.CompilerParams(vmem_limit_bytes=VMEM_BYTES),
        cost_estimate=pl.CostEstimate(flops=1, bytes_accessed=1, transcendentals=0),
    )(z, weights, *added)


def outer_kernel(count, *refs):
    left_near, left_far = refs[0][...].T, refs[1][...].T
    outs = refs[2 + 2 * count :]
    for j in range(count):
        near, far = refs[2 + 2 * j], refs[3 + 2 * j]
        outs[0][:, j * near.shape[1] : (j + 1) * near.shape[1]] = (
            mm(left_near, near[...]) + mm(left_far, far[...])
        ).astype(BF)


def outer(left, rights):
    count, width = left[0].shape
    units = rights[0][0].shape[1]
    tile = min(512, width)
    flat = [array for pair in rights for array in pair]
    return pl.pallas_call(
        functools.partial(outer_kernel, len(rights)),
        grid=(width // tile,),
        out_shape=[jax.ShapeDtypeStruct((width, len(rights) * units), BF)],
        in_specs=[pl.BlockSpec((count, tile), lambda i: (0, i))] * 2
        + [pl.BlockSpec((count, units), lambda i: (0, 0))] * len(flat),
        out_specs=[pl.BlockSpec((tile, len(rights) * units), lambda i: (i, 0))],
        compiler_params=pltpu.CompilerParams(vmem_limit_bytes=VMEM_BYTES),
        cost_estimate=pl.CostEstimate(flops=1, bytes_accessed=1, transcendentals=0),
    )(*left, *flat)[0]


def finish_kernel(count, slices, *refs):
    pieces = len(refs) - 2 * count - 3
    spots, parts = refs[0], refs[1 : 1 + pieces]
    weights, gain = refs[1 + pieces : 1 + pieces + count], refs[1 + pieces + count]
    outs, gain_out = refs[2 + pieces + count : -1], refs[-1]
    width = outs[0].shape[1] // slices
    found = 0.0
    for k in range(pieces):
        for i in range(parts[k].shape[0]):
            spot = spots[k * parts[k].shape[0] + i]
            columns = pl.ds(pl.multiple_of(spot * width, width), width)
            for j in range(count):
                part = parts[k][i, :, j * width : (j + 1) * width].astype(F32)
                outs[j][:, columns] = part * gain[...]
                found = found + part * weights[j][:, columns].astype(F32)
    gain_out[...] = jnp.sum(found, axis=1, keepdims=True)


def finish(parts, spots, weights, gain):
    count, rows = len(weights), weights[0].shape[0]
    return in_vmem(
        functools.partial(finish_kernel, count, sum(part.shape[0] for part in parts)),
        list(parts) + list(weights) + [gain],
        [jax.ShapeDtypeStruct(weight.shape, F32) for weight in weights]
        + [jax.ShapeDtypeStruct((rows, 1), F32)],
        [],
        4 * math.prod(weights[0].shape) * count,
        spots,
    )


def in_vmem(kernel, operands, outs, scratch, flops, places=None):
    moved = sum(math.prod(array.shape) * 2 for array in list(operands) + outs)
    first = [] if places is None else [places]
    return pl.pallas_call(
        kernel,
        out_shape=outs,
        in_specs=[pl.BlockSpec(memory_space=pltpu.SMEM)] * len(first)
        + kernel_specs(len(operands)),
        out_specs=kernel_specs(len(outs)),
        scratch_shapes=scratch,
        compiler_params=pltpu.CompilerParams(vmem_limit_bytes=VMEM_BYTES),
        cost_estimate=pl.CostEstimate(flops=1, bytes_accessed=1, transcendentals=0),
    )(*first, *operands)


def kernel_specs(count):
    return [pl.BlockSpec(memory_space=pltpu.VMEM)] * count


def attention_forward(seq, q_cols, kv_cols):
    length = seq.shape[0]
    scores = (q_cols // HEAD_DIM) * length * length // 2
    return in_vmem(
        functools.partial(forward_kernel, q_cols, kv_cols),
        [seq],
        [
            jax.ShapeDtypeStruct((length, q_cols), BF),
            jax.ShapeDtypeStruct((q_cols // HEAD_DIM, length), F32),
        ],
        [],
        scores * HEAD_DIM * 16,
    )


def attention_backward(seq, grads, logsums, q_cols, kv_cols):
    length = seq.shape[0]
    scores = (q_cols // HEAD_DIM) * length * length // 2
    return in_vmem(
        functools.partial(backward_kernel, q_cols, kv_cols),
        [seq, grads, logsums],
        [jax.ShapeDtypeStruct(seq.shape, BF)],
        [pltpu.VMEM((length, HEAD_DIM), F32)] * 2,
        scores * HEAD_DIM * 40,
    )[0]


def body(
    inputs,
    positions,
    attn_gain,
    q_weight,
    k_weight,
    v_weight,
    o_weight,
    ffn_gain,
    gate_weight,
    up_weight,
    down_weight,
    cotangent,
):
    sizes = {axis: lax.axis_size(axis) for axis in "yczx"}
    yn, cn, zn, xn = [sizes[axis] for axis in "yczx"]
    _, span, width = inputs.shape
    slices = yn * xn
    expanded = max(KV_HEADS, 2 * slices)
    copies = expanded // KV_HEADS
    rows = q_weight.shape[0]
    halves = zn // yn
    q_cols = HEADS * HEAD_DIM // (slices * halves)
    kv_cols = expanded * HEAD_DIM // (slices * halves)
    part_cols = q_cols + 2 * kv_cols
    piece = xn * span
    length = zn * piece

    states = reorder(inputs.reshape(span, width), sizes, "yczx", F32)
    grad_low = reorder(cotangent.reshape(span, width), sizes, "yczx", BF)

    gain_one = attn_gain.astype(F32)[:, None]
    gain_two = ffn_gain.astype(F32)[:, None]

    def widen(weight):
        return jnp.repeat(weight.reshape(rows, KV_HEADS, HEAD_DIM), copies, axis=1)

    def parts(weight, cols):
        return weight.reshape(rows, slices, halves, cols)

    wide_k, wide_v = widen(k_weight), widen(v_weight)
    qkv_rows = (
        jnp.concatenate(
            [parts(q_weight, q_cols), parts(wide_k, kv_cols), parts(wide_v, kv_cols)], axis=3
        )
        .reshape(rows, slices, halves * part_cols)
        .transpose(1, 0, 2)
    )
    qkv_scaled = (qkv_rows.astype(F32) * gain_one[None]).astype(BF)
    gate_scaled = (gate_weight.astype(F32) * gain_two).astype(BF)
    up_scaled = (up_weight.astype(F32) * gain_two).astype(BF)

    unit_one, factor_one = norm_of(states)
    o_rows = o_weight.reshape(rows, slices, halves * q_cols).transpose(1, 0, 2)
    near_attn = in_order(swap(jnp.concatenate([qkv_scaled, o_rows], axis=2), PLANE), PLANE)
    ffn_near = ffn_weights_near((gate_scaled, up_scaled, down_weight), sizes)
    digits = jnp.stack([positions.reshape(span) // 128, positions.reshape(span) % 128], axis=1)
    digits = jnp.repeat(digits.astype(BF), HEAD_DIM, axis=1)
    tokens_one = lax.all_gather(
        jnp.concatenate([unit_one.astype(BF), digits], axis=1), PLANE, axis=0, tiled=True
    )
    ffn_full = ffn_weights_far(after(ffn_near, near_attn))
    qkv_width = halves * part_cols
    (qkv_full, o_full), qkv_there = attention_weights(
        after(near_attn, ffn_near), sizes, ((0, qkv_width), (qkv_width, near_attn.shape[-1]))
    )
    digits = tokens_one[:, width:].astype(F32)
    cosine, sine = angles_of(digits[:, 0] * 128.0 + digits[:, HEAD_DIM])
    cosine = jnp.concatenate([cosine] * 4, axis=1)
    sine = jnp.concatenate([-sine, sine] * 2, axis=1)
    rotated = ([True] * ((q_cols + kv_cols) // HEAD_DIM) + [False] * (kv_cols // HEAD_DIM)) * halves
    count = slices * span
    attn_flops = 2 * count * width * halves * part_cols

    (packed,) = in_vmem(
        functools.partial(qkv_kernel, halves, rotated),
        [tokens_one, qkv_full, cosine, sine],
        [jax.ShapeDtypeStruct((zn, piece, part_cols), BF)],
        [],
        attn_flops,
    )
    heads_in = all_to_all(packed, "z").reshape(length, part_cols)
    attended, logsums = attention_forward(heads_in, q_cols, kv_cols)
    grad_steps = [trade(after(grad_low, heads_in), "z", k) for k in range(1, zn)]
    attended = after(attended, grad_steps[0])
    attended = all_to_all(attended.reshape(zn, piece, q_cols), "z")

    attn_tokens, o_part = in_vmem(
        functools.partial(o_kernel, halves),
        [attended, o_full],
        [
            jax.ShapeDtypeStruct((count, halves * q_cols), BF),
            jax.ShapeDtypeStruct((slices, span, width), BF),
        ],
        [],
        2 * count * width * halves * q_cols,
    )
    hidden_one = after(states + scatter_plane(o_part), ffn_full, *grad_steps[1:])

    grad_out = grad_low.astype(F32)
    grad_near = in_order([after(grad_low, hidden_one)] + grad_steps, "z")
    grad_far = trade(grad_near, "c", 1)
    unit_two, factor_two = norm_of(hidden_one)
    tokens_near = gather(unit_two.astype(BF), "z")
    tokens_far = trade(tokens_near, "c", 1)
    tokens_near, tokens_far, grad_near, grad_far = [
        array.reshape(-1, width) for array in (tokens_near, tokens_far, grad_near, grad_far)
    ]
    z_near, dgate_near, dup_near, dx_near = ffn(tokens_near, grad_near, ffn_full, F32)
    z_far, dgate_far, dup_far, dx_far = ffn(tokens_far, grad_far, ffn_full, BF)
    blocks = (zn, span, width)
    down_part = outer((grad_near, grad_far), [(z_near, z_far)])
    grad_both = dx_near.reshape(blocks) + trade(dx_far.reshape(blocks), "c", 1).astype(F32)
    grad_both = grad_both.astype(BF)
    grad_there = all_to_all(grad_both, "z")
    grad_hat = total(list(grad_there))
    gate_up_part = outer(
        (tokens_near, tokens_far),
        [(dgate_near, dgate_far), (dup_near, dup_far)],
    )
    result_far = add_product(z_far, ffn_full)
    result_near = add_product(z_near, ffn_full, trade(result_far, "c", 1)).reshape(blocks)
    grad_hat = after(grad_hat, result_near, gate_up_part, down_part)
    grad_one = grad_out + norm_backward(grad_hat, unit_two, factor_two)
    result_there = swap(after(result_near, grad_one), "z")
    down_sum = ffn_grads(after(down_part, grad_both), sizes)
    branch_tokens = gather(grad_one.astype(BF), PLANE).reshape(-1, width)
    branch_tokens = after(branch_tokens, *result_there[1:3])
    gate_up_sum = ffn_grads(after(gate_up_part, branch_tokens), sizes)
    grad_attn = product(branch_tokens, o_full).astype(BF)
    grad_attn = grad_attn.reshape(yn, piece, halves, q_cols).transpose(0, 2, 1, 3)
    grad_heads = all_to_all(grad_attn.reshape(zn, piece, q_cols), "z")
    down_sum = ffn_grads_near(down_sum)
    grad_heads = grad_heads.reshape(length, q_cols)
    heads_out = attention_backward(heads_in, grad_heads, logsums, q_cols, kv_cols)
    heads_out = after(heads_out, *down_sum[1:3])
    back = all_to_all(heads_out.reshape(zn, piece, part_cols), "z")
    o_sum, o_sum_there = attention_grads(
        contract_rows(branch_tokens, after(attn_tokens, heads_out)), sizes, back
    )
    gate_up_sum = ffn_grads_near(gate_up_sum, heads_out)
    output = (after(hidden_one, grad_heads) + total(result_there)).astype(BF)
    grad_qkv, hat_part = in_vmem(
        functools.partial(qkv_back_kernel, halves, rotated),
        [back, qkv_full, cosine, sine],
        [
            jax.ShapeDtypeStruct((count, halves * part_cols), BF),
            jax.ShapeDtypeStruct((slices, span, width), BF),
        ],
        [],
        attn_flops,
    )
    grad_hat_one = after(scatter_plane(hat_part), result_there[3], down_sum[3])
    input_grad = grad_one + norm_backward(grad_hat_one, unit_one, factor_one)
    qkv_sum, _ = attention_grads(
        contract_rows(tokens_one[:, :width], grad_qkv), sizes
    )
    attn_gain_grad = jnp.sum(qkv_sum * qkv_rows.astype(F32), axis=(0, 2))
    qkv_grad = (qkv_sum * gain_one[None]).transpose(1, 0, 2)
    qkv_grad = qkv_grad.reshape(rows, slices, halves, part_cols)
    spots = ffn_slices(sizes)
    gate_grad, up_grad, ffn_gain_grad = finish(
        gate_up_sum, spots, (gate_weight, up_weight), gain_two
    )
    (down_grad, _) = finish(down_sum, spots, (down_weight,), jnp.ones_like(gain_two))

    def narrow(part):
        part = part.reshape(rows, KV_HEADS, copies, HEAD_DIM).sum(axis=2)
        return part.reshape(rows, KV_HEADS * HEAD_DIM)

    q_grad = qkv_grad[..., :q_cols].reshape(rows, HEADS * HEAD_DIM)
    k_grad = narrow(qkv_grad[..., q_cols : q_cols + kv_cols])
    v_grad = narrow(qkv_grad[..., q_cols + kv_cols :])
    return (
        reorder(output, sizes, "yxcz", BF).reshape(1, span, width),
        reorder(input_grad, sizes, "yxcz", F32).reshape(1, span, width),
        attn_gain_grad,
        q_grad,
        k_grad,
        v_grad,
        o_sum.transpose(1, 0, 2).reshape(rows, HEADS * HEAD_DIM),
        ffn_gain_grad.reshape(rows),
        gate_grad,
        up_grad,
        down_grad,
    )


def solution(mesh):
    batch, seq = mesh.devices.shape
    cores, column = 2, 4
    parts = mesh.devices.reshape(batch // cores, cores, column, seq // column)
    tokens = P(("y", "c"), ("z", "x"), None)
    rows = P(("y", "c", "z", "x"), None)
    gain = P(("y", "c", "z", "x"))
    return jax.shard_map(
        body,
        mesh=Mesh(parts, ("y", "c", "z", "x")),
        in_specs=(
            tokens, P(("y", "c"), ("z", "x")), gain, rows, rows, rows, rows, gain, rows, rows, rows,
            tokens,
        ),
        out_specs=(tokens, tokens, gain, rows, rows, rows, rows, gain, rows, rows, rows),
        check_vma=False,
    )
```

time: 1220 us -> 788 us (0.65)
  local copies, waits for them, and re-layouts: 342 us -> 95.5 us
  waiting for transfers between devices: 530 us -> 350 us
  Pallas kernels: 0 us -> 130 us
  matrix products: 136 us -> 9.6 us
  between operations: 3.74 us -> 45.4 us
  starting transfers between devices: 129 us -> 96.5 us
    ppermute x134 -> x40, waiting for transfers between devices: 530 us -> 235 us  [trade(): return lax.ppermute(value, axes, [(i, i ^ step) for i in range(count)])]
    pallas_call x0 -> x17, Pallas kernels: none -> 130 us  [the longest x11 55.6 us: in_vmem(): pl.pallas_call(kernel, out_shape=outs, in_specs=[pl.BlockSpec(memory_spac...]
    dynamic_update_slice x103 -> x24, local copies, waits for them, and re-layouts: 143 us -> 16.8 us  [put(): return lax.dynamic_update_slice(buffer, block.reshape(shape), start)]
    all_to_all x0 -> x10, waiting for transfers between devices: none -> 115 us  [all_to_all(): return lax.all_to_all(blocks, axes, split_axis=0, concat_axis=0, tiled=True)]
    ppermute x134 -> x40, starting transfers between devices: 129 us -> 44 us  [trade(): return lax.ppermute(value, axes, [(i, i ^ step) for i in range(count)])]
    dot_general x19 -> x0, matrix products: 79.3 us -> none  [the longest x5 30.3 us: product_t(): return jnp.einsum('rc,dc->rd', left, right, preferred_element_type=F32)]
    all_to_all x0 -> x10, starting transfers between devices: none -> 52.1 us  [all_to_all(): return lax.all_to_all(blocks, axes, split_axis=0, concat_axis=0, tiled=True)]
    dynamic_slice x22 -> x4, local copies, waits for them, and re-layouts: 34.6 us -> 3.82 us  [pick(): return lax.dynamic_index_in_dim(array, index, axis, keepdims=False)]
  transfers between devices with their start and end apart: 134 -> 54, of which waited for: 72 -> 30; matrix products, arithmetic and copies ran while one was open for 39% -> 16% of each run, Pallas kernels for 0% -> 14%
where the time goes in v2:
time: 788 us; the launch traced here: 776 us
  waiting for transfers between devices  350 us (44%)
  Pallas kernels  130 us (16%)
  starting transfers between devices  96.5 us (12%)
  local copies, waits for them, and re-layouts  95.5 us (12%)
  other arithmetic  49.4 us (6%)
  between operations  45.4 us (6%)
  matrix products  9.6 us (1%)
    ppermute x40, waiting for transfers between devices, trade(): return lax.ppermute(value, axes, [(i, i ^ step) for i in range(count)])  235 us
    all_to_all x10, waiting for transfers between devices, all_to_all(): return lax.all_to_all(blocks, axes, split_axis=0, concat_axis=0, tiled=True)  115 us
    pallas_call x11, Pallas kernels, in_vmem(): pl.pallas_call(kernel, out_shape=outs, in_specs=[pl.BlockSpec(memory_spac...  55.6 us
    all_to_all x10, starting transfers between devices, all_to_all(): return lax.all_to_all(blocks, axes, split_axis=0, concat_axis=0, tiled=True)  52.1 us
    ppermute x40, starting transfers between devices, trade(): return lax.ppermute(value, axes, [(i, i ^ step) for i in range(count)])  44 us
    pallas_call x2, Pallas kernels, ffn(): pl.pallas_call(functools.partial(ffn_kernel, tiles), grid=(tiles + row_ti...  38.5 us
    unnamed x105, local copies, waits for them, and re-layouts  24.4 us
    pallas_call x2, Pallas kernels, outer(): pl.pallas_call(functools.partial(outer_kernel, len(rights)), grid=(width...  22.1 us
  transfers between devices with their start and end apart: 54, of which 30 were waited for; matrix products, arithmetic and copies ran while one was open for 16% of the time, Pallas kernels for 14%

profile of v2, /device:TPU:8, one launch (start us, length us, event | category | flops | bytes accessed | tf_op | source)
XLA Modules:
  0.0 776.2 jit_solution(17716300497507257881)
XLA Ops:
  49.9 38.7 %all-to-all-done = bf16[8,64,3072]{2,1,0:T(8,128)(2,1)S(1)} async-done(((bf16[8,64,3072]{2,1,0:T(8,128)(2,1)}), bf16[8,64,3072]{2,1,0:T(8,128)(2,1)S(1)}, u32[]{:S(2)}, u32[]{:S(2)}) %all-to-all-start) | async-done | bytes 3145760 | tf_op jit(solution)/shard_map/all_to_all | solution.py:179
  99.2 25.9 %collective-permute-done.3 = bf16[4,64,1280]{2,1,0:T(8,128)(2,1)} collective-permute-done((bf16[4,64,1280]{2,1,0:T(8,128)(2,1)}, bf16[4,64,1280]{2,1,0:T(8,128)(2,1)}, u32[]{:S(2)}, u32[]{:S(2)}) %collective-permute-start.3) | collective-permute-done | bytes 655392 | tf_op jit(solution)/shard_map/ppermute | solution.py:97
  126.1 15.4 %collective-permute-done.4 = bf16[4,64,1280]{2,1,0:T(8,128)(2,1)} collective-permute-done((bf16[4,64,1280]{2,1,0:T(8,128)(2,1)}, bf16[4,64,1280]{2,1,0:T(8,128)(2,1)}, u32[]{:S(2)}, u32[]{:S(2)}) %collective-permute-start.4) | collective-permute-done | bytes 655392 | tf_op jit(solution)/shard_map/ppermute | solution.py:97
  142.5 13.3 %collective-permute-done.5 = bf16[4,64,1280]{2,1,0:T(8,128)(2,1)S(1)} collective-permute-done((bf16[4,64,1280]{2,1,0:T(8,128)(2,1)}, bf16[4,64,1280]{2,1,0:T(8,128)(2,1)S(1)}, u32[]{:S(2)}, u32[]{:S(2)}) %collective-permute-start.5) | collective-permute-done | bytes 655392 | tf_op jit(solution)/shard_map/ppermute | solution.py:97
  179.6 12.4 %all-to-all-done.1 = bf16[4,256,384]{2,1,0:T(8,128)(2,1)S(1)} async-done(((bf16[4,256,384]{2,1,0:T(8,128)(2,1)}), bf16[4,256,384]{2,1,0:T(8,128)(2,1)S(1)}, u32[]{:S(2)}, u32[]{:S(2)}) %all-to-all-start.1) | async-done | bytes 786464 | tf_op jit(solution)/shard_map/all_to_all | solution.py:179
  198.9 11.1 %shard_map.205 = (bf16[1024,256]{1,0:T(8,128)(2,1)}, f32[4,1024]{1,0:T(4,128)}) custom-call(bf16[1024,384]{1,0:T(8,128)(2,1)} %bitcast.311), custom_call_target="tpu_custom_call" | custom-call | flops 1 | bytes 1 | tf_op jit(solution)/shard_map/pallas_call | solution.py:514
  218.9 10.9 %all-to-all-done.2.blocks = bf16[4,256,256]{2,1,0:T(8,128)(2,1)S(1)} async-done(((bf16[4,256,256]{2,1,0:T(8,128)(2,1)}), bf16[4,256,256]{2,1,0:T(8,128)(2,1)S(1)}, u32[]{:S(2)}, u32[]{:S(2)}) %all-to-all-start.2) | async-done | bytes 524320 | tf_op jit(solution)/shard_map/all_to_all | solution.py:179
  244.0 31.7 %collective-permute-done.9 = bf16[128,2048]{1,0:T(8,128)(2,1)S(1)} collective-permute-done((bf16[128,2048]{1,0:T(8,128)(2,1)S(1)}, bf16[128,2048]{1,0:T(8,128)(2,1)S(1)}, u32[]{:S(2)}, u32[]{:S(2)}) %collective-permute-start.9) | collective-permute-done | bytes 524320 | tf_op jit(solution)/shard_map/ppermute | solution.py:97
  277.5 10.9 %collective-permute-done.10 = bf16[128,2048]{1,0:T(8,128)(2,1)S(1)} collective-permute-done((bf16[128,2048]{1,0:T(8,128)(2,1)S(1)}, bf16[128,2048]{1,0:T(8,128)(2,1)S(1)}, u32[]{:S(2)}, u32[]{:S(2)}) %collective-permute-start.10) | collective-permute-done | bytes 524320 | tf_op jit(solution)/shard_map/ppermute | solution.py:97
  308.2 38.6 %all-to-all-done.4 = bf16[4,128,2048]{2,1,0:T(8,128)(2,1)} async-done(((bf16[4,128,2048]{2,1,0:T(8,128)(2,1)}), bf16[4,128,2048]{2,1,0:T(8,128)(2,1)}, u32[]{:S(2)}, u32[]{:S(2)}) %all-to-all-start.4) | async-done | bytes 2097184 | tf_op jit(solution)/shard_map/all_to_all | solution.py:179
  352.5 19.0 %shard_map.209 = (bf16[512,1024]{1,0:T(8,128)(2,1)}, bf16[512,1024]{1,0:T(8,128)(2,1)}, bf16[512,1024]{1,0:T(8,128)(2,1)}, bf16[512,2048]{1,0:T(8,128)(2,1)}) custom-call(bf16[512,2048]{1,0:T(8,128)(2,1)} %bitcast.306, bf16[512,2048]{1,0:T(8,128)(2,1)} %bitcast.57.refs_1_, bf16[2048,3072]{1,0:T(8,128)(2,1)} %bitcast.281, bf16[2048,3072]{1,0:T(8,128)(2,1)} %bitcast.282, ...), custom_call_target="tpu_custom_call" | custom-call | flops 1 | bytes 1 | tf_op jit(solution)/shard_map/pallas_call | solution.py:414
  371.7 19.5 %shard_map.208 = (bf16[512,1024]{1,0:T(8,128)(2,1)}, bf16[512,1024]{1,0:T(8,128)(2,1)}, bf16[512,1024]{1,0:T(8,128)(2,1)}, f32[512,2048]{1,0:T(8,128)}) custom-call(bf16[512,2048]{1,0:T(8,128)(2,1)} %bitcast.47.refs_0_, bf16[512,2048]{1,0:T(8,128)(2,1)} %bitcast.54.refs_1_.refs_0_, bf16[2048,3072]{1,0:T(8,128)(2,1)} %bitcast.286, ...), custom_call_target="tpu_custom_call" | custom-call | flops 1 | bytes 1 | tf_op jit(solution)/shard_map/pallas_call | solution.py:414
  391.1 8.5 %shard_map.213 = bf16[2048,1024]{1,0:T(8,128)(2,1)} custom-call(bf16[512,2048]{1,0:T(8,128)(2,1)} %bitcast.54.refs_1_.refs_0_, bf16[512,2048]{1,0:T(8,128)(2,1)} %bitcast.57.refs_1_, bf16[512,1024]{1,0:T(8,128)(2,1)} %get-tuple-element.33.z_ref.refs_2_, bf16[512,1024]{1,0:T(8,128)(2,1)} %get-tuple-element.34.z_ref.refs_3_), custom_call_target="tpu_custom_call" | custom-call | flops 1 | bytes 1 | tf_op jit(solution)/shard_map/pallas_call | solution.py:468
  423.8 13.6 %shard_map.212 = bf16[2048,2048]{1,0:T(8,128)(2,1)} custom-call(bf16[512,2048]{1,0:T(8,128)(2,1)} %bitcast.47.refs_0_, bf16[512,2048]{1,0:T(8,128)(2,1)} %bitcast.307, bf16[512,1024]{1,0:T(8,128)(2,1)} %get-tuple-element.35.refs_2_, bf16[512,1024]{1,0:T(8,128)(2,1)} %get-tuple-element.36.refs_3_, bf16[512,1024]{1,0:T(8,128)(2,1)} %get-tuple-element.37.refs_4_, ...), custom_call_target="tpu_custom_call" | custom-call | flops 1 | bytes 1 | tf_op jit(solution)/shard_map/pallas_call | solution.py:468
  453.1 10.0 %all-to-all-done.5 = bf16[4,128,2048]{2,1,0:T(8,128)(2,1)} async-done(((bf16[4,128,2048]{2,1,0:T(8,128)(2,1)}), bf16[4,128,2048]{2,1,0:T(8,128)(2,1)}, u32[]{:S(2)}, u32[]{:S(2)}) %all-to-all-start.5) | async-done | bytes 2097184 | tf_op jit(solution)/shard_map/all_to_all | solution.py:179
  482.1 21.0 %collective-permute-done.15 = bf16[128,2048]{1,0:T(8,128)(2,1)S(1)} collective-permute-done((bf16[128,2048]{1,0:T(8,128)(2,1)S(1)}, bf16[128,2048]{1,0:T(8,128)(2,1)S(1)}, u32[]{:S(2)}, u32[]{:S(2)}) %collective-permute-start.15) | collective-permute-done | bytes 524320 | tf_op jit(solution)/shard_map/ppermute | solution.py:97
  537.6 11.4 %shard_map.215 = bf16[1024,384]{1,0:T(8,128)(2,1)} custom-call(bf16[1024,384]{1,0:T(8,128)(2,1)} %bitcast.312, bf16[1024,256]{1,0:T(8,128)(2,1)} %bitcast.325, f32[4,1024]{1,0:T(4,128)} %get-tuple-element.39.logsums), custom_call_target="tpu_custom_call" | custom-call | flops 1 | bytes 1 | tf_op jit(solution)/shard_map/pallas_call | solution.py:514
  550.9 8.4 %collective-permute-done.20.refs_3_ = bf16[2,64,1024]{2,1,0:T(8,128)(2,1)S(1)} collective-permute-done((bf16[2,64,1024]{2,1,0:T(8,128)(2,1)}, bf16[2,64,1024]{2,1,0:T(8,128)(2,1)S(1)}, u32[]{:S(2)}, u32[]{:S(2)}) %collective-permute-start.20) | collective-permute-done | bytes 262176 | tf_op jit(solution)/shard_map/ppermute | solution.py:97
  619.3 9.5 %collective-permute-done.32 = bf16[4,64,512]{2,1,0:T(8,128)(2,1)S(1)} collective-permute-done((bf16[4,64,512]{2,1,0:T(8,128)(2,1)S(1)}, bf16[4,64,512]{2,1,0:T(8,128)(2,1)S(1)}, u32[]{:S(2)}, u32[]{:S(2)}) %collective-permute-start.32) | collective-permute-done | bytes 262176 | tf_op jit(solution)/shard_map/ppermute | solution.py:97
  628.8 10.2 %collective-permute-done.31 = bf16[4,64,512]{2,1,0:T(8,128)(2,1)S(1)} collective-permute-done((bf16[4,64,512]{2,1,0:T(8,128)(2,1)S(1)}, bf16[4,64,512]{2,1,0:T(8,128)(2,1)S(1)}, u32[]{:S(2)}, u32[]{:S(2)}) %collective-permute-start.31) | collective-permute-done | bytes 262176 | tf_op jit(solution)/shard_map/ppermute | solution.py:97
  666.0 20.6 %collective-permute-done.25 = bf16[4,64,768]{2,1,0:T(8,128)(2,1)} collective-permute-done((bf16[4,64,768]{2,1,0:T(8,128)(2,1)S(1)}, bf16[4,64,768]{2,1,0:T(8,128)(2,1)}, u32[]{:S(2)}, u32[]{:S(2)}) %collective-permute-start.25) | collective-permute-done | bytes 393248 | tf_op jit(solution)/shard_map/ppermute | solution.py:97
  724.4 11.3 %collective-permute-done.37.refs_2_ = bf16[2,64,2048]{2,1,0:T(8,128)(2,1)} collective-permute-done((bf16[2,64,2048]{2,1,0:T(8,128)(2,1)}, bf16[2,64,2048]{2,1,0:T(8,128)(2,1)}, u32[]{:S(2)}, u32[]{:S(2)}) %collective-permute-start.37) | collective-permute-done | bytes 524320 | tf_op jit(solution)/shard_map/ppermute | solution.py:97
  735.6 16.5 %collective-permute-done.38.refs_3_ = bf16[2,64,2048]{2,1,0:T(8,128)(2,1)S(1)} collective-permute-done((bf16[2,64,2048]{2,1,0:T(8,128)(2,1)}, bf16[2,64,2048]{2,1,0:T(8,128)(2,1)S(1)}, u32[]{:S(2)}, u32[]{:S(2)}) %collective-permute-start.38) | collective-permute-done | bytes 524320 | tf_op jit(solution)/shard_map/ppermute | solution.py:97
  752.1 10.6 %collective-permute-done.39.refs_4_ = bf16[2,64,2048]{2,1,0:T(8,128)(2,1)} collective-permute-done((bf16[2,64,2048]{2,1,0:T(8,128)(2,1)}, bf16[2,64,2048]{2,1,0:T(8,128)(2,1)}, u32[]{:S(2)}, u32[]{:S(2)}) %collective-permute-start.39) | collective-permute-done | bytes 524320 | tf_op jit(solution)/shard_map/ppermute | solution.py:97
  (377 shorter events, 332.0 us)
Async XLA Ops:
  15.1 73.6 %all-to-all-start = ((bf16[8,64,3072]{2,1,0:T(8,128)(2,1)}), bf16[8,64,3072]{2,1,0:T(8,128)(2,1)S(1)}, u32[]{:S(2)}, u32[]{:S(2)}) async-start(bf16[8,64,3072]{2,1,0:T(8,128)(2,1)} %copy.210), calls=%async_computation | async-start | bytes 6291456 | tf_op jit(solution)/shard_map/all_to_all | solution.py:179
  20.5 137.4 %all-gather.3.cloned.1.call-start = ((), (), s32[]{:S(2)}) async-start(), calls=%async_computation.12 | async-start | bytes 2785280 | tf_op jit(solution)/shard_map/all_gather | solution.py:615
  26.6 265.6 %all-gather.5.cloned.1.call-start = ((), (), s32[]{:S(2)}) async-start(), calls=%async_computation.13 | async-start | bytes 15728640 | tf_op jit(solution)/shard_map/all_gather | solution.py:189
  94.1 31.0 %collective-permute-start.3 = (bf16[4,64,1280]{2,1,0:T(8,128)(2,1)}, bf16[4,64,1280]{2,1,0:T(8,128)(2,1)}, u32[]{:S(2)}, u32[]{:S(2)}) collective-permute-start(bf16[4,64,1280]{2,1,0:T(8,128)(2,1)} %constant_dynamic-update-slice_fusion.19), channel_id=1, source_target_pairs={{0,2},{2,0},{4,6},{6,4},{1,3},{3,1},{5,7},{7,5},{8,10},{10,8},{12,... | collective-permute-start | bytes 1966088 | tf_op jit(solution)/shard_map/ppermute | solution.py:97
  97.0 44.4 %collective-permute-start.4 = (bf16[4,64,1280]{2,1,0:T(8,128)(2,1)}, bf16[4,64,1280]{2,1,0:T(8,128)(2,1)}, u32[]{:S(2)}, u32[]{:S(2)}) collective-permute-start(bf16[4,64,1280]{2,1,0:T(8,128)(2,1)} %constant_dynamic-update-slice_fusion.19), channel_id=1, source_target_pairs={{0,4},{2,6},{4,0},{6,2},{1,5},{3,7},{5,1},{7,3},{8,12},{10,14},{12... | collective-permute-start | bytes 1966088 | tf_op jit(solution)/shard_map/ppermute | solution.py:97
  97.9 57.9 %collective-permute-start.5 = (bf16[4,64,1280]{2,1,0:T(8,128)(2,1)}, bf16[4,64,1280]{2,1,0:T(8,128)(2,1)S(1)}, u32[]{:S(2)}, u32[]{:S(2)}) collective-permute-start(bf16[4,64,1280]{2,1,0:T(8,128)(2,1)} %constant_dynamic-update-slice_fusion.19), channel_id=1, source_target_pairs={{0,6},{2,4},{4,2},{6,0},{1,7},{3,5},{5,3},{7,1},{8,14},{10,12},{12... | collective-permute-start | bytes 1966088 | tf_op jit(solution)/shard_map/ppermute | solution.py:97
  234.9 55.4 %all-to-all-start.3 = ((bf16[4,128,2048]{2,1,0:T(8,128)(2,1)}), bf16[4,128,2048]{2,1,0:T(8,128)(2,1)}, u32[]{:S(2)}, u32[]{:S(2)}) async-start(bf16[4,128,2048]{2,1,0:T(8,128)(2,1)} %get-tuple-element.30), calls=%async_computation.3 | async-start | bytes 4194304 | tf_op jit(solution)/shard_map/all_to_all | solution.py:179
  239.5 36.2 %collective-permute-start.9 = (bf16[128,2048]{1,0:T(8,128)(2,1)S(1)}, bf16[128,2048]{1,0:T(8,128)(2,1)S(1)}, u32[]{:S(2)}, u32[]{:S(2)}) collective-permute-start(bf16[128,2048]{1,0:T(8,128)(2,1)S(1)} %constant_dynamic-update-slice_fusion.18), channel_id=1, source_target_pairs={{0,4},{2,6},{4,0},{6,2},{1,5},{3,7},{5,1},{7,3},{8,12},{10,14},{12... | collective-permute-start | bytes 1572872 | tf_op jit(solution)/shard_map/ppermute | solution.py:97
  242.8 45.6 %collective-permute-start.10 = (bf16[128,2048]{1,0:T(8,128)(2,1)S(1)}, bf16[128,2048]{1,0:T(8,128)(2,1)S(1)}, u32[]{:S(2)}, u32[]{:S(2)}) collective-permute-start(bf16[128,2048]{1,0:T(8,128)(2,1)S(1)} %constant_dynamic-update-slice_fusion.18), channel_id=1, source_target_pairs={{0,6},{2,4},{4,2},{6,0},{1,7},{3,5},{5,3},{7,1},{8,14},{10,12},{12... | collective-permute-start | bytes 1572872 | tf_op jit(solution)/shard_map/ppermute | solution.py:97
  296.6 50.2 %all-to-all-start.4 = ((bf16[4,128,2048]{2,1,0:T(8,128)(2,1)}), bf16[4,128,2048]{2,1,0:T(8,128)(2,1)}, u32[]{:S(2)}, u32[]{:S(2)}) async-start(bf16[4,128,2048]{2,1,0:T(8,128)(2,1)} %broadcast_in_dim.43), calls=%async_computation.4 | async-start | bytes 4194304 | tf_op jit(solution)/shard_map/all_to_all | solution.py:179
  301.2 210.6 %reduce-scatter.7.cloned.1.call-start = ((), (), s32[]{:S(2)}) async-start(), calls=%async_computation.14 | async-start | bytes 5242880
  308.2 38.6 %collective-permute-start.12 = (bf16[4,128,2048]{2,1,0:T(8,128)(2,1)}, bf16[4,128,2048]{2,1,0:T(8,128)(2,1)}, u32[]{:S(2)}, u32[]{:S(2)}) collective-permute-start(bf16[4,128,2048]{2,1,0:T(8,128)(2,1)} %bitcast_dynamic-update-slice_fusion.2), channel_id=1, source_target_pairs={{0,8},{8,0},{1,9},{9,1},{2,10},{10,2},{3,11},{11,3},{4,12},{12,4},... | collective-permute-start | bytes 6291464 | tf_op jit(solution)/shard_map/ppermute | solution.py:97
  371.5 32.9 %collective-permute-start.13 = (bf16[4,128,2048]{2,1,0:T(8,128)(2,1)}, bf16[4,128,2048]{2,1,0:T(8,128)(2,1)S(1)}, u32[]{:S(2)}, u32[]{:S(2)}) collective-permute-start(bf16[4,128,2048]{2,1,0:T(8,128)(2,1)} %bitcast.341), channel_id=1, source_target_pairs={{0,8},{8,0},{1,9},{9,1},{2,10},{10,2},{3,11},{11,3},{4,12},{12,4},... | collective-permute-start | bytes 6291464 | tf_op jit(solution)/shard_map/ppermute | solution.py:97
  409.7 53.5 %all-to-all-start.5 = ((bf16[4,128,2048]{2,1,0:T(8,128)(2,1)}), bf16[4,128,2048]{2,1,0:T(8,128)(2,1)}, u32[]{:S(2)}, u32[]{:S(2)}) async-start(bf16[4,128,2048]{2,1,0:T(8,128)(2,1)} %copy-done.9), calls=%async_computation.5 | async-start | bytes 4194304 | tf_op jit(solution)/shard_map/all_to_all | solution.py:179
  468.2 39.1 %all-to-all-start.6 = ((bf16[4,128,2048]{2,1,0:T(8,128)(2,1)}), bf16[4,128,2048]{2,1,0:T(8,128)(2,1)}, u32[]{:S(2)}, u32[]{:S(2)}) async-start(bf16[4,128,2048]{2,1,0:T(8,128)(2,1)} %broadcast_in_dim.45), calls=%async_computation.6 | async-start | bytes 4194304 | tf_op jit(solution)/shard_map/all_to_all | solution.py:179
  472.6 225.4 %reduce-scatter.9.cloned.1.call-start = ((), (), s32[]{:S(2)}) async-start(), calls=%async_computation.15 | async-start | bytes 10485760
  533.5 46.5 %collective-permute-start.17 = (bf16[128,2048]{1,0:T(8,128)(2,1)}, bf16[128,2048]{1,0:T(8,128)(2,1)}, u32[]{:S(2)}, u32[]{:S(2)}) collective-permute-start(bf16[128,2048]{1,0:T(8,128)(2,1)} %get-tuple-element.59), channel_id=1, source_target_pairs={{0,6},{2,4},{4,2},{6,0},{1,7},{3,5},{5,3},{7,1},{8,14},{10,12},{12... | collective-permute-start | bytes 1572872 | tf_op jit(solution)/shard_map/ppermute | solution.py:97
  598.5 57.3 %collective-permute-start.22 = (bf16[4,4,64,768]{3,2,0,1:T(8,128)(2,1)}, bf16[4,4,64,768]{3,2,0,1:T(8,128)(2,1)}, u32[]{:S(2)}, u32[]{:S(2)}) collective-permute-start(bf16[4,4,64,768]{3,2,0,1:T(8,128)(2,1)} %fusion.4), channel_id=1, source_target_pairs={{0,8},{8,0},{1,9},{9,1},{2,10},{10,2},{3,11},{11,3},{4,12},{12,4},... | collective-permute-start | bytes 4718600 | tf_op jit(solution)/shard_map/ppermute | solution.py:97
  600.9 63.0 %all-to-all-start.9 = ((bf16[4,128,2048]{2,1,0:T(8,128)(2,1)}), bf16[4,128,2048]{2,1,0:T(8,128)(2,1)}, u32[]{:S(2)}, u32[]{:S(2)}) async-start(bf16[4,128,2048]{2,1,0:T(8,128)(2,1)} %get-tuple-element.40), calls=%async_computation.9 | async-start | bytes 4194304 | tf_op jit(solution)/shard_map/all_to_all | solution.py:179
  609.8 29.2 %collective-permute-start.31 = (bf16[4,64,512]{2,1,0:T(8,128)(2,1)S(1)}, bf16[4,64,512]{2,1,0:T(8,128)(2,1)S(1)}, u32[]{:S(2)}, u32[]{:S(2)}) collective-permute-start(bf16[4,64,512]{2,1,0:T(8,128)(2,1)S(1)} %get-tuple-element.75), channel_id=1, source_target_pairs={{0,4},{2,6},{4,0},{6,2},{1,5},{3,7},{5,1},{7,3},{8,12},{10,14},{12... | collective-permute-start | bytes 786440 | tf_op jit(solution)/shard_map/ppermute | solution.py:97
  661.6 32.8 %collective-permute-start.24 = (bf16[4,64,768]{2,1,0:T(8,128)(2,1)S(1)}, bf16[4,64,768]{2,1,0:T(8,128)(2,1)}, u32[]{:S(2)}, u32[]{:S(2)}) collective-permute-start(bf16[4,64,768]{2,1,0:T(8,128)(2,1)S(1)} %get-tuple-element.64), channel_id=1, source_target_pairs={{0,4},{2,6},{4,0},{6,2},{1,5},{3,7},{5,1},{7,3},{8,12},{10,14},{12... | collective-permute-start | bytes 1179656 | tf_op jit(solution)/shard_map/ppermute | solution.py:97
  663.9 30.4 %collective-permute-start.23 = (bf16[4,64,768]{2,1,0:T(8,128)(2,1)S(1)}, bf16[4,64,768]{2,1,0:T(8,128)(2,1)}, u32[]{:S(2)}, u32[]{:S(2)}) collective-permute-start(bf16[4,64,768]{2,1,0:T(8,128)(2,1)S(1)} %get-tuple-element.62), channel_id=1, source_target_pairs={{0,2},{2,0},{4,6},{6,4},{1,3},{3,1},{5,7},{7,5},{8,10},{10,8},{12,... | collective-permute-start | bytes 1179656 | tf_op jit(solution)/shard_map/ppermute | solution.py:97
  715.6 36.6 %collective-permute-start.38 = (bf16[2,64,2048]{2,1,0:T(8,128)(2,1)}, bf16[2,64,2048]{2,1,0:T(8,128)(2,1)S(1)}, u32[]{:S(2)}, u32[]{:S(2)}) collective-permute-start(bf16[2,64,2048]{2,1,0:T(8,128)(2,1)} %pad_maximum_fusion.4), channel_id=1, source_target_pairs={{0,4},{2,6},{4,0},{6,2},{1,5},{3,7},{5,1},{7,3},{8,12},{10,14},{12... | collective-permute-start | bytes 1572872 | tf_op jit(solution)/shard_map/ppermute | solution.py:97
  717.8 44.9 %collective-permute-start.39 = (bf16[2,64,2048]{2,1,0:T(8,128)(2,1)}, bf16[2,64,2048]{2,1,0:T(8,128)(2,1)}, u32[]{:S(2)}, u32[]{:S(2)}) collective-permute-start(bf16[2,64,2048]{2,1,0:T(8,128)(2,1)} %pad_maximum_fusion.5), channel_id=1, source_target_pairs={{0,6},{2,4},{4,2},{6,0},{1,7},{3,5},{5,3},{7,1},{8,14},{10,12},{12... | collective-permute-start | bytes 1572872 | tf_op jit(solution)/shard_map/ppermute | solution.py:97
  (79 other events, 755.5 us)
Sparse Core Ops, SparseCore 0:
  26.7 42.4 all-gather.2
  91.1 123.4 all-gather.4
  409.8 54.7 reduce-scatter.6
  511.8 88.3 reduce-scatter.8

commit v3 on v2

--- a/solution.py
+++ b/solution.py
@@ -144,7 +144,6 @@
         [features],
         [jax.ShapeDtypeStruct(features.shape, dtype)],
         [],
-        0,
     )[0]
 
 
@@ -337,6 +336,39 @@
             out_ref[y * halves + h] = values[:, h * part : (h + 1) * part]
 
 
+def heads_kernel(halves, x_ref, w_ref, out_ref):
+    piece, cols = out_ref.shape[1:]
+    for y in range(out_ref.shape[0] // halves):
+        values = mm(x_ref[pl.ds(y * piece, piece), :], w_ref[...]).astype(BF)
+        for h in range(halves):
+            out_ref[y * halves + h] = values[:, h * cols : (h + 1) * cols]
+
+
+def summed(parts):
+    result = parts[0].astype(F32)
+    for i in range(1, parts.shape[0]):
+        result = result + parts[i].astype(F32)
+    return result
+
+
+def hidden_norm_kernel(parts, states, hidden_ref, unit_ref, factor_ref, copies):
+    hidden = states[...] + summed(parts)
+    unit, factor = norm_of(hidden)
+    hidden_ref[...] = hidden
+    unit_ref[...] = unit
+    factor_ref[...] = factor
+    for i in range(copies.shape[0]):
+        copies[i] = unit.astype(BF)
+
+
+def norm_back_kernel(parts, grad_out, unit, factor, grad_ref, copies):
+    back = norm_backward(summed(parts), unit[...], factor[...])
+    grad = grad_out[...].astype(F32) + back
+    grad_ref[...] = grad
+    for i in range(copies.shape[0]):
+        copies[i] = grad.astype(BF)
+
+
 def qkv_back_kernel(halves, rotated, blocks, w_ref, cosine, sine, grad_ref, out_ref):
     count, piece = blocks.shape[:2]
     for y in range(count // halves):
@@ -392,7 +424,7 @@
         dx_ref[...] = part.astype(dx_ref.dtype)
 
 
-def ffn(tokens, grads, weights, out_dtype):
+def ffn(tokens, grads, weights, out_dtype, ties=()):
     count, width = tokens.shape
     units = weights.shape[1] // 3
     tile, row_tile = min(256, units), min(1024, width)
@@ -412,15 +444,18 @@
     across = [pl.BlockSpec((row_tile, units), lambda i, j=j: (second(i), j)) for j in range(2)]
     hidden = jax.ShapeDtypeStruct((count, units), BF)
     return pl.pallas_call(
-        functools.partial(ffn_kernel, tiles),
+        skipping(functools.partial(ffn_kernel, tiles), 7, len(ties)),
         grid=(tiles + row_tiles,),
         out_shape=[hidden] * 3 + [jax.ShapeDtypeStruct((count, width), out_dtype)],
-        in_specs=[whole, whole] + columns + across,
+        in_specs=[whole, whole]
+        + columns
+        + across
+        + [pl.BlockSpec(memory_space=pl.ANY)] * len(ties),
         out_specs=[narrow] * 3 + [pl.BlockSpec((count, row_tile), lambda i: (0, second(i)))],
         scratch_shapes=[pltpu.VMEM((count, units), BF)] * 2,
         compiler_params=pltpu.CompilerParams(vmem_limit_bytes=VMEM_BYTES),
         cost_estimate=pl.CostEstimate(flops=1, bytes_accessed=1, transcendentals=0),
-    )(tokens, grads, *[weights] * 5)
+    )(tokens, grads, *[weights] * 5, *ties)
 
 
 def add_product_kernel(z_ref, down_ref, *refs):
@@ -460,21 +495,22 @@
         ).astype(BF)
 
 
-def outer(left, rights):
+def outer(left, rights, ties=()):
     count, width = left[0].shape
     units = rights[0][0].shape[1]
     tile = min(512, width)
     flat = [array for pair in rights for array in pair]
     return pl.pallas_call(
-        functools.partial(outer_kernel, len(rights)),
+        skipping(functools.partial(outer_kernel, len(rights)), 2 + len(flat), len(ties)),
         grid=(width // tile,),
         out_shape=[jax.ShapeDtypeStruct((width, len(rights) * units), BF)],
         in_specs=[pl.BlockSpec((count, tile), lambda i: (0, i))] * 2
-        + [pl.BlockSpec((count, units), lambda i: (0, 0))] * len(flat),
+        + [pl.BlockSpec((count, units), lambda i: (0, 0))] * len(flat)
+        + [pl.BlockSpec(memory_space=pl.ANY)] * len(ties),
         out_specs=[pl.BlockSpec((tile, len(rights) * units), lambda i: (i, 0))],
         compiler_params=pltpu.CompilerParams(vmem_limit_bytes=VMEM_BYTES),
         cost_estimate=pl.CostEstimate(flops=1, bytes_accessed=1, transcendentals=0),
-    )(*left, *flat)[0]
+    )(*left, *flat, *ties)[0]
 
 
 def finish_kernel(count, slices, *refs):
@@ -503,24 +539,28 @@
         [jax.ShapeDtypeStruct(weight.shape, F32) for weight in weights]
         + [jax.ShapeDtypeStruct((rows, 1), F32)],
         [],
-        4 * math.prod(weights[0].shape) * count,
         spots,
     )
 
 
-def in_vmem(kernel, operands, outs, scratch, flops, places=None):
-    moved = sum(math.prod(array.shape) * 2 for array in list(operands) + outs)
+def skipping(kernel, at, count):
+    return lambda *refs: kernel(*refs[:at], *refs[at + count :])
+
+
+def in_vmem(kernel, operands, outs, scratch, places=None, ties=()):
     first = [] if places is None else [places]
+    kernel = skipping(kernel, len(first) + len(operands), len(ties))
     return pl.pallas_call(
         kernel,
         out_shape=outs,
         in_specs=[pl.BlockSpec(memory_space=pltpu.SMEM)] * len(first)
-        + kernel_specs(len(operands)),
+        + kernel_specs(len(operands))
+        + [pl.BlockSpec(memory_space=pl.ANY)] * len(ties),
         out_specs=kernel_specs(len(outs)),
         scratch_shapes=scratch,
         compiler_params=pltpu.CompilerParams(vmem_limit_bytes=VMEM_BYTES),
         cost_estimate=pl.CostEstimate(flops=1, bytes_accessed=1, transcendentals=0),
-    )(*first, *operands)
+    )(*first, *operands, *ties)
 
 
 def kernel_specs(count):
@@ -529,7 +569,6 @@
 
 def attention_forward(seq, q_cols, kv_cols):
     length = seq.shape[0]
-    scores = (q_cols // HEAD_DIM) * length * length // 2
     return in_vmem(
         functools.partial(forward_kernel, q_cols, kv_cols),
         [seq],
@@ -538,19 +577,16 @@
             jax.ShapeDtypeStruct((q_cols // HEAD_DIM, length), F32),
         ],
         [],
-        scores * HEAD_DIM * 16,
     )
 
 
 def attention_backward(seq, grads, logsums, q_cols, kv_cols):
     length = seq.shape[0]
-    scores = (q_cols // HEAD_DIM) * length * length // 2
     return in_vmem(
         functools.partial(backward_kernel, q_cols, kv_cols),
         [seq, grads, logsums],
         [jax.ShapeDtypeStruct(seq.shape, BF)],
         [pltpu.VMEM((length, HEAD_DIM), F32)] * 2,
-        scores * HEAD_DIM * 40,
     )[0]
 
 
@@ -626,19 +662,16 @@
     sine = jnp.concatenate([-sine, sine] * 2, axis=1)
     rotated = ([True] * ((q_cols + kv_cols) // HEAD_DIM) + [False] * (kv_cols // HEAD_DIM)) * halves
     count = slices * span
-    attn_flops = 2 * count * width * halves * part_cols
 
     (packed,) = in_vmem(
         functools.partial(qkv_kernel, halves, rotated),
         [tokens_one, qkv_full, cosine, sine],
         [jax.ShapeDtypeStruct((zn, piece, part_cols), BF)],
         [],
-        attn_flops,
     )
     heads_in = all_to_all(packed, "z").reshape(length, part_cols)
     attended, logsums = attention_forward(heads_in, q_cols, kv_cols)
-    grad_steps = [trade(after(grad_low, heads_in), "z", k) for k in range(1, zn)]
-    attended = after(attended, grad_steps[0])
+    grad_near = lax.all_gather(after(grad_low, attended), "z", axis=0, tiled=False)
     attended = all_to_all(attended.reshape(zn, piece, q_cols), "z")
 
     attn_tokens, o_part = in_vmem(
@@ -649,52 +682,70 @@
             jax.ShapeDtypeStruct((slices, span, width), BF),
         ],
         [],
-        2 * count * width * halves * q_cols,
-    )
-    hidden_one = after(states + scatter_plane(o_part), ffn_full, *grad_steps[1:])
-
-    grad_out = grad_low.astype(F32)
-    grad_near = in_order([after(grad_low, hidden_one)] + grad_steps, "z")
+    )
+    square = jax.ShapeDtypeStruct((span, width), F32)
+    hidden_one, unit_two, factor_two, tokens_near = in_vmem(
+        hidden_norm_kernel,
+        [all_to_all(o_part, PLANE), states],
+        [
+            square,
+            square,
+            jax.ShapeDtypeStruct((span, 1), F32),
+            jax.ShapeDtypeStruct((zn, span, width), BF),
+        ],
+        [],
+        ties=[ffn_full],
+    )
+
     grad_far = trade(grad_near, "c", 1)
-    unit_two, factor_two = norm_of(hidden_one)
-    tokens_near = gather(unit_two.astype(BF), "z")
+    tokens_near = all_to_all(tokens_near, "z")
     tokens_far = trade(tokens_near, "c", 1)
     tokens_near, tokens_far, grad_near, grad_far = [
         array.reshape(-1, width) for array in (tokens_near, tokens_far, grad_near, grad_far)
     ]
-    z_near, dgate_near, dup_near, dx_near = ffn(tokens_near, grad_near, ffn_full, F32)
     z_far, dgate_far, dup_far, dx_far = ffn(tokens_far, grad_far, ffn_full, BF)
+    z_near, dgate_near, dup_near, dx_near = ffn(
+        tokens_near, grad_near, ffn_full, F32, [dx_far]
+    )
     blocks = (zn, span, width)
-    down_part = outer((grad_near, grad_far), [(z_near, z_far)])
     grad_both = dx_near.reshape(blocks) + trade(dx_far.reshape(blocks), "c", 1).astype(F32)
     grad_both = grad_both.astype(BF)
     grad_there = all_to_all(grad_both, "z")
-    grad_hat = total(list(grad_there))
     gate_up_part = outer(
         (tokens_near, tokens_far),
         [(dgate_near, dgate_far), (dup_near, dup_far)],
     )
     result_far = add_product(z_far, ffn_full)
     result_near = add_product(z_near, ffn_full, trade(result_far, "c", 1)).reshape(blocks)
-    grad_hat = after(grad_hat, result_near, gate_up_part, down_part)
-    grad_one = grad_out + norm_backward(grad_hat, unit_two, factor_two)
-    result_there = swap(after(result_near, grad_one), "z")
-    down_sum = ffn_grads(after(down_part, grad_both), sizes)
-    branch_tokens = gather(grad_one.astype(BF), PLANE).reshape(-1, width)
-    branch_tokens = after(branch_tokens, *result_there[1:3])
-    gate_up_sum = ffn_grads(after(gate_up_part, branch_tokens), sizes)
-    grad_attn = product(branch_tokens, o_full).astype(BF)
-    grad_attn = grad_attn.reshape(yn, piece, halves, q_cols).transpose(0, 2, 1, 3)
-    grad_heads = all_to_all(grad_attn.reshape(zn, piece, q_cols), "z")
+    down_part = outer((grad_near, grad_far), [(z_near, z_far)])
+    grad_one, branch_tokens = in_vmem(
+        norm_back_kernel,
+        [grad_there, grad_low, unit_two, factor_two],
+        [square, jax.ShapeDtypeStruct((slices, span, width), BF)],
+        [],
+        ties=[result_near, gate_up_part],
+    )
+    result_there = swap(result_near, "z")
+    down_sum = ffn_grads(down_part, sizes)
+
+    branch_tokens = all_to_all(branch_tokens, PLANE).reshape(-1, width)
+    (grad_attn,) = in_vmem(
+        functools.partial(heads_kernel, halves),
+        [branch_tokens, o_full],
+        [jax.ShapeDtypeStruct((zn, piece, q_cols), BF)],
+        [],
+        ties=result_there[1:3],
+    )
+    gate_up_sum = ffn_grads(after(gate_up_part, grad_attn), sizes)
+    grad_heads = all_to_all(grad_attn, "z")
     down_sum = ffn_grads_near(down_sum)
     grad_heads = grad_heads.reshape(length, q_cols)
     heads_out = attention_backward(heads_in, grad_heads, logsums, q_cols, kv_cols)
-    heads_out = after(heads_out, *down_sum[1:3])
     back = all_to_all(heads_out.reshape(zn, piece, part_cols), "z")
     o_sum, o_sum_there = attention_grads(
-        contract_rows(branch_tokens, after(attn_tokens, heads_out)), sizes, back
-    )
-    gate_up_sum = ffn_grads_near(gate_up_sum, heads_out)
+        contract_rows(branch_tokens, attn_tokens), sizes, back
+    )
+    gate_up_sum = ffn_grads_near(gate_up_sum)
     output = (after(hidden_one, grad_heads) + total(result_there)).astype(BF)
     grad_qkv, hat_part = in_vmem(
         functools.partial(qkv_back_kernel, halves, rotated),
@@ -704,9 +755,9 @@
             jax.ShapeDtypeStruct((slices, span, width), BF),
         ],
         [],
-        attn_flops,
-    )
-    grad_hat_one = after(scatter_plane(hat_part), result_there[3], down_sum[3])
+        ties=down_sum[1:],
+    )
+    grad_hat_one = after(scatter_plane(hat_part), result_there[3])
     input_grad = grad_one + norm_backward(grad_hat_one, unit_one, factor_one)
     qkv_sum, _ = attention_grads(
         contract_rows(tokens_one[:, :width], grad_qkv), sizes

time: 788 us -> 765 us (0.971)
  between operations: 45.4 us -> 24.1 us
  local copies, waits for them, and re-layouts: 95.5 us -> 81.6 us
  Pallas kernels: 130 us -> 142 us
  waiting for transfers between devices: 350 us -> 362 us
    ppermute x40 -> x37, waiting for transfers between devices: 235 us -> 201 us  [trade(): return lax.ppermute(value, axes, [(i, i ^ step) for i in range(count)])]
    all_gather x0 -> x1, waiting for transfers between devices: none -> 31.5 us  [body(): lax.all_gather(after(grad_low, attended), 'z', axis=0, tiled=False)]
    all_to_all x10, waiting for transfers between devices: 115 us -> 130 us  [all_to_all(): return lax.all_to_all(blocks, axes, split_axis=0, concat_axis=0, tiled=True)]
    pallas_call x11 -> x14, Pallas kernels: 55.6 us -> 68.1 us  [in_vmem(): pl.pallas_call(kernel, out_shape=outs, in_specs=[pl.BlockSpec(memory_spac...]
    slice x23 -> x7, local copies, waits for them, and re-layouts: 18 us -> 7.02 us  [after(): first = array[(0,) * array.ndim]]
    ppermute x40 -> x37, starting transfers between devices: 44 us -> 36.1 us  [trade(): return lax.ppermute(value, axes, [(i, i ^ step) for i in range(count)])]
    unnamed x105 -> x96, local copies, waits for them, and re-layouts: 24.4 us -> 21.8 us
    dynamic_update_slice x24 -> x20, local copies, waits for them, and re-layouts: 16.8 us -> 17.3 us  [put(): return lax.dynamic_update_slice(buffer, block.reshape(shape), start)]
  transfers between devices with their start and end apart: 54 -> 52, of which waited for: 30 -> 30; matrix products, arithmetic and copies ran while one was open for 16% -> 14% of each run, Pallas kernels for 14% -> 12%
where the time goes in v3:
time: 765 us; the launch traced here: 754 us
  waiting for transfers between devices  362 us (47%)
  Pallas kernels  142 us (19%)
  starting transfers between devices  93.9 us (12%)
  local copies, waits for them, and re-layouts  81.6 us (11%)
  other arithmetic  42.2 us (6%)
  between operations  24.1 us (3%)
  matrix products  8.07 us (1%)
    ppermute x37, waiting for transfers between devices, trade(): return lax.ppermute(value, axes, [(i, i ^ step) for i in range(count)])  201 us
    all_to_all x10, waiting for transfers between devices, all_to_all(): return lax.all_to_all(blocks, axes, split_axis=0, concat_axis=0, tiled=True)  130 us
    pallas_call x14, Pallas kernels, in_vmem(): pl.pallas_call(kernel, out_shape=outs, in_specs=[pl.BlockSpec(memory_spac...  68.1 us
    all_to_all x10, starting transfers between devices, all_to_all(): return lax.all_to_all(blocks, axes, split_axis=0, concat_axis=0, tiled=True)  57.3 us
    pallas_call x2, Pallas kernels, ffn(): pl.pallas_call(skipping(functools.partial(ffn_kernel, tiles), 7, len(ties...  38.6 us
    ppermute x37, starting transfers between devices, trade(): return lax.ppermute(value, axes, [(i, i ^ step) for i in range(count)])  36.1 us
    all_gather x1, waiting for transfers between devices, body(): lax.all_gather(after(grad_low, attended), 'z', axis=0, tiled=False)  31.5 us
    pallas_call x2, Pallas kernels, outer(): pl.pallas_call(skipping(functools.partial(outer_kernel, len(rights)), 2 +...  21.8 us
  transfers between devices with their start and end apart: 52, of which 30 were waited for; matrix products, arithmetic and copies ran while one was open for 14% of the time, Pallas kernels for 12%

profile of v3, /device:TPU:8, one launch (start us, length us, event | category | flops | bytes accessed | tf_op | source)
XLA Modules:
  0.0 754.2 jit_solution(13962574167473093922)
XLA Ops:
  49.5 38.7 %all-to-all-done = bf16[8,64,3072]{2,1,0:T(8,128)(2,1)S(1)} async-done(((bf16[8,64,3072]{2,1,0:T(8,128)(2,1)}), bf16[8,64,3072]{2,1,0:T(8,128)(2,1)S(1)}, u32[]{:S(2)}, u32[]{:S(2)}) %all-to-all-start) | async-done | bytes 3145760 | tf_op jit(solution)/shard_map/all_to_all | solution.py:178
  98.6 25.9 %collective-permute-done.3 = bf16[4,64,1280]{2,1,0:T(8,128)(2,1)} collective-permute-done((bf16[4,64,1280]{2,1,0:T(8,128)(2,1)}, bf16[4,64,1280]{2,1,0:T(8,128)(2,1)}, u32[]{:S(2)}, u32[]{:S(2)}) %collective-permute-start.3) | collective-permute-done | bytes 655392 | tf_op jit(solution)/shard_map/ppermute | solution.py:97
  125.5 15.4 %collective-permute-done.4 = bf16[4,64,1280]{2,1,0:T(8,128)(2,1)} collective-permute-done((bf16[4,64,1280]{2,1,0:T(8,128)(2,1)}, bf16[4,64,1280]{2,1,0:T(8,128)(2,1)}, u32[]{:S(2)}, u32[]{:S(2)}) %collective-permute-start.4) | collective-permute-done | bytes 655392 | tf_op jit(solution)/shard_map/ppermute | solution.py:97
  141.9 13.3 %collective-permute-done.5 = bf16[4,64,1280]{2,1,0:T(8,128)(2,1)S(1)} collective-permute-done((bf16[4,64,1280]{2,1,0:T(8,128)(2,1)}, bf16[4,64,1280]{2,1,0:T(8,128)(2,1)S(1)}, u32[]{:S(2)}, u32[]{:S(2)}) %collective-permute-start.5) | collective-permute-done | bytes 655392 | tf_op jit(solution)/shard_map/ppermute | solution.py:97
  183.4 10.1 %all-to-all-done.1 = bf16[4,256,384]{2,1,0:T(8,128)(2,1)S(1)} async-done(((bf16[4,256,384]{2,1,0:T(8,128)(2,1)}), bf16[4,256,384]{2,1,0:T(8,128)(2,1)S(1)}, u32[]{:S(2)}, u32[]{:S(2)}) %all-to-all-start.1) | async-done | bytes 786464 | tf_op jit(solution)/shard_map/all_to_all | solution.py:178
  194.4 11.1 %shard_map.205 = (bf16[1024,256]{1,0:T(8,128)(2,1)}, f32[4,1024]{1,0:T(4,128)}) custom-call(bf16[1024,384]{1,0:T(8,128)(2,1)} %bitcast.296), custom_call_target="tpu_custom_call" | custom-call | flops 1 | bytes 1 | tf_op jit(solution)/shard_map/pallas_call | solution.py:553
  213.1 9.8 %all-to-all-done.2.refs_0_ = bf16[4,256,256]{2,1,0:T(8,128)(2,1)S(1)} async-done(((bf16[4,256,256]{2,1,0:T(8,128)(2,1)}), bf16[4,256,256]{2,1,0:T(8,128)(2,1)S(1)}, u32[]{:S(2)}, u32[]{:S(2)}) %all-to-all-start.2) | async-done | bytes 524320 | tf_op jit(solution)/shard_map/all_to_all | solution.py:178
  238.9 16.6 %all-to-all-done.3.refs_0_ = bf16[4,128,2048]{2,1,0:T(8,128)(2,1)S(1)} async-done(((bf16[4,128,2048]{2,1,0:T(8,128)(2,1)}), bf16[4,128,2048]{2,1,0:T(8,128)(2,1)S(1)}, u32[]{:S(2)}, u32[]{:S(2)}) %all-to-all-start.3) | async-done | bytes 2097184 | tf_op jit(solution)/shard_map/all_to_all | solution.py:178
  268.8 31.5 %all-gather.8.cloned.1.call-done = bf16[4,128,2048]{2,1,0:T(8,128)(2,1)} async-done(((bf16[1,128,2048]{2,1,0:T(8,128)(2,1)}), bf16[4,128,2048]{2,1,0:T(8,128)(2,1)}) %all-gather.8.cloned.1.call-update) | async-done | bytes 2097168 | tf_op jit(solution)/shard_map/all_gather | solution.py:674
  300.3 28.3 %all-to-all-done.4 = bf16[4,128,2048]{2,1,0:T(8,128)(2,1)S(1)} async-done(((bf16[4,128,2048]{2,1,0:T(8,128)(2,1)}), bf16[4,128,2048]{2,1,0:T(8,128)(2,1)S(1)}, u32[]{:S(2)}, u32[]{:S(2)}) %all-to-all-start.4) | async-done | bytes 2097184 | tf_op jit(solution)/shard_map/all_to_all | solution.py:178
  334.0 19.0 %shard_map.209 = (bf16[512,1024]{1,0:T(8,128)(2,1)}, bf16[512,1024]{1,0:T(8,128)(2,1)}, bf16[512,1024]{1,0:T(8,128)(2,1)}, bf16[512,2048]{1,0:T(8,128)(2,1)}) custom-call(bf16[512,2048]{1,0:T(8,128)(2,1)} %bitcast.292, bf16[512,2048]{1,0:T(8,128)(2,1)} %bitcast.49.refs_1_, bf16[2048,3072]{1,0:T(8,128)(2,1)} %bitcast.263, bf16[2048,3072]{1,0:T(8,128)(2,1)} %bitcast.264, ...), custom_call_target="tpu_custom_call" | custom-call | flops 1 | bytes 1 | tf_op jit(solution)/shard_map/pallas_call | solution.py:446
  353.0 19.6 %shard_map.210 = (bf16[512,1024]{1,0:T(8,128)(2,1)}, bf16[512,1024]{1,0:T(8,128)(2,1)}, bf16[512,1024]{1,0:T(8,128)(2,1)}, f32[512,2048]{1,0:T(8,128)}) custom-call(bf16[512,2048]{1,0:T(8,128)(2,1)} %bitcast.285, bf16[512,2048]{1,0:T(8,128)(2,1)} %bitcast.289, bf16[2048,3072]{1,0:T(8,128)(2,1)} %bitcast.268, bf16[2048,3072]{1,0:T(8,128)(2,1)} %bitcast.269, ...), custom_call_target="tpu_custom_call" | custom-call | flops 1 | bytes 1 | tf_op jit(solution)/shard_map/pallas_call | solution.py:446
  372.7 8.4 %shard_map.218 = bf16[2048,1024]{1,0:T(8,128)(2,1)} custom-call(bf16[512,2048]{1,0:T(8,128)(2,1)} %bitcast.290, bf16[512,2048]{1,0:T(8,128)(2,1)} %bitcast.49.refs_1_, bf16[512,1024]{1,0:T(8,128)(2,1)} %get-tuple-element.43.z_ref.refs_2_, bf16[512,1024]{1,0:T(8,128)(2,1)} %get-tuple-element.44.z_ref.refs_3_), custom_call_target="tpu_custom_call" | custom-call | flops 1 | bytes 1 | tf_op jit(solution)/shard_map/pallas_call | solution.py:503
  404.8 13.4 %shard_map.213.refs_5_ = bf16[2048,2048]{1,0:T(8,128)(2,1)} custom-call(bf16[512,2048]{1,0:T(8,128)(2,1)} %bitcast.286, bf16[512,2048]{1,0:T(8,128)(2,1)} %bitcast.293, bf16[512,1024]{1,0:T(8,128)(2,1)} %get-tuple-element.45.refs_2_, bf16[512,1024]{1,0:T(8,128)(2,1)} %get-tuple-element.46.refs_3_, bf16[512,1024]{1,0:T(8,128)(2,1)} %get-tuple-element.47.refs_4_, ...), custom_call_target="tpu_custom_call" | custom-call | flops 1 | bytes 1 | tf_op jit(solution)/shard_map/pallas_call | solution.py:503
  426.6 17.4 %all-to-all-done.5.refs_0_ = bf16[4,128,2048]{2,1,0:T(8,128)(2,1)S(1)} async-done(((bf16[4,128,2048]{2,1,0:T(8,128)(2,1)}), bf16[4,128,2048]{2,1,0:T(8,128)(2,1)S(1)}, u32[]{:S(2)}, u32[]{:S(2)}) %all-to-all-start.5) | async-done | bytes 2097184 | tf_op jit(solution)/shard_map/all_to_all | solution.py:178
  458.5 20.8 %collective-permute-done.12.refs_2_ = bf16[128,2048]{1,0:T(8,128)(2,1)S(1)} collective-permute-done((bf16[128,2048]{1,0:T(8,128)(2,1)S(1)}, bf16[128,2048]{1,0:T(8,128)(2,1)S(1)}, u32[]{:S(2)}, u32[]{:S(2)}) %collective-permute-start.12) | collective-permute-done | bytes 524320 | tf_op jit(solution)/shard_map/ppermute | solution.py:97
  509.1 9.1 %all-to-all-done.7 = bf16[4,256,256]{2,1,0:T(8,128)(2,1)S(1)} async-done(((bf16[4,256,256]{2,1,0:T(8,128)(2,1)}), bf16[4,256,256]{2,1,0:T(8,128)(2,1)S(1)}, u32[]{:S(2)}, u32[]{:S(2)}) %all-to-all-start.7) | async-done | bytes 524320 | tf_op jit(solution)/shard_map/all_to_all | solution.py:178
  518.9 11.3 %shard_map.217 = bf16[1024,384]{1,0:T(8,128)(2,1)} custom-call(bf16[1024,384]{1,0:T(8,128)(2,1)} %bitcast.297, bf16[1024,256]{1,0:T(8,128)(2,1)} %bitcast.311, f32[4,1024]{1,0:T(4,128)} %get-tuple-element.51.refs_2_), custom_call_target="tpu_custom_call" | custom-call | flops 1 | bytes 1 | tf_op jit(solution)/shard_map/pallas_call | solution.py:553
  530.2 7.8 %all-to-all-start.8 = ((bf16[4,256,384]{2,1,0:T(8,128)(2,1)}), bf16[4,256,384]{2,1,0:T(8,128)(2,1)S(1)}, u32[]{:S(2)}, u32[]{:S(2)}) async-start(bf16[4,256,384]{2,1,0:T(8,128)(2,1)} %bitcast.306), calls=%async_computation.8 | async-start | bytes 1572864 | tf_op jit(solution)/shard_map/all_to_all | solution.py:178
  557.3 11.0 %collective-permute-done.17.refs_5_.refs_3_ = bf16[2,64,1024]{2,1,0:T(8,128)(2,1)S(1)} collective-permute-done((bf16[2,64,1024]{2,1,0:T(8,128)(2,1)}, bf16[2,64,1024]{2,1,0:T(8,128)(2,1)S(1)}, u32[]{:S(2)}, u32[]{:S(2)}) %collective-permute-start.17) | collective-permute-done | bytes 262176 | tf_op jit(solution)/shard_map/ppermute | solution.py:97
  640.8 21.3 %collective-permute-done.22 = bf16[4,64,768]{2,1,0:T(8,128)(2,1)} collective-permute-done((bf16[4,64,768]{2,1,0:T(8,128)(2,1)S(1)}, bf16[4,64,768]{2,1,0:T(8,128)(2,1)}, u32[]{:S(2)}, u32[]{:S(2)}) %collective-permute-start.22) | collective-permute-done | bytes 393248 | tf_op jit(solution)/shard_map/ppermute | solution.py:97
  702.2 11.0 %collective-permute-done.34.refs_2_ = bf16[2,64,2048]{2,1,0:T(8,128)(2,1)S(1)} collective-permute-done((bf16[2,64,2048]{2,1,0:T(8,128)(2,1)}, bf16[2,64,2048]{2,1,0:T(8,128)(2,1)S(1)}, u32[]{:S(2)}, u32[]{:S(2)}) %collective-permute-start.34) | collective-permute-done | bytes 524320 | tf_op jit(solution)/shard_map/ppermute | solution.py:97
  713.2 15.9 %collective-permute-done.35.refs_3_ = bf16[2,64,2048]{2,1,0:T(8,128)(2,1)} collective-permute-done((bf16[2,64,2048]{2,1,0:T(8,128)(2,1)}, bf16[2,64,2048]{2,1,0:T(8,128)(2,1)}, u32[]{:S(2)}, u32[]{:S(2)}) %collective-permute-start.35) | collective-permute-done | bytes 524320 | tf_op jit(solution)/shard_map/ppermute | solution.py:97
  729.1 11.9 %collective-permute-done.36.refs_4_ = bf16[2,64,2048]{2,1,0:T(8,128)(2,1)} collective-permute-done((bf16[2,64,2048]{2,1,0:T(8,128)(2,1)}, bf16[2,64,2048]{2,1,0:T(8,128)(2,1)}, u32[]{:S(2)}, u32[]{:S(2)}) %collective-permute-start.36) | collective-permute-done | bytes 524320 | tf_op jit(solution)/shard_map/ppermute | solution.py:97
  (327 shorter events, 331.8 us)
Async XLA Ops:
  14.6 73.6 %all-to-all-start = ((bf16[8,64,3072]{2,1,0:T(8,128)(2,1)}), bf16[8,64,3072]{2,1,0:T(8,128)(2,1)S(1)}, u32[]{:S(2)}, u32[]{:S(2)}) async-start(bf16[8,64,3072]{2,1,0:T(8,128)(2,1)} %copy.210), calls=%async_computation | async-start | bytes 6291456 | tf_op jit(solution)/shard_map/all_to_all | solution.py:178
  20.0 137.3 %all-gather.4.cloned.1.call-start = ((), (), s32[]{:S(2)}) async-start(), calls=%async_computation.12 | async-start | bytes 2785280 | tf_op jit(solution)/shard_map/all_gather | solution.py:651
  26.1 229.5 %all-gather.6.cloned.1.call-start = ((), (), s32[]{:S(2)}) async-start(), calls=%async_computation.13 | async-start | bytes 15728640 | tf_op jit(solution)/shard_map/all_gather | solution.py:188
  93.5 31.0 %collective-permute-start.3 = (bf16[4,64,1280]{2,1,0:T(8,128)(2,1)}, bf16[4,64,1280]{2,1,0:T(8,128)(2,1)}, u32[]{:S(2)}, u32[]{:S(2)}) collective-permute-start(bf16[4,64,1280]{2,1,0:T(8,128)(2,1)} %constant_dynamic-update-slice_fusion.9), channel_id=1, source_target_pairs={{0,2},{2,0},{4,6},{6,4},{1,3},{3,1},{5,7},{7,5},{8,10},{10,8},{12,... | collective-permute-start | bytes 1966088 | tf_op jit(solution)/shard_map/ppermute | solution.py:97
  96.4 44.4 %collective-permute-start.4 = (bf16[4,64,1280]{2,1,0:T(8,128)(2,1)}, bf16[4,64,1280]{2,1,0:T(8,128)(2,1)}, u32[]{:S(2)}, u32[]{:S(2)}) collective-permute-start(bf16[4,64,1280]{2,1,0:T(8,128)(2,1)} %constant_dynamic-update-slice_fusion.9), channel_id=1, source_target_pairs={{0,4},{2,6},{4,0},{6,2},{1,5},{3,7},{5,1},{7,3},{8,12},{10,14},{12... | collective-permute-start | bytes 1966088 | tf_op jit(solution)/shard_map/ppermute | solution.py:97
  97.3 57.9 %collective-permute-start.5 = (bf16[4,64,1280]{2,1,0:T(8,128)(2,1)}, bf16[4,64,1280]{2,1,0:T(8,128)(2,1)S(1)}, u32[]{:S(2)}, u32[]{:S(2)}) collective-permute-start(bf16[4,64,1280]{2,1,0:T(8,128)(2,1)} %constant_dynamic-update-slice_fusion.9), channel_id=1, source_target_pairs={{0,6},{2,4},{4,2},{6,0},{1,7},{3,5},{5,3},{7,1},{8,14},{10,12},{12... | collective-permute-start | bytes 1966088 | tf_op jit(solution)/shard_map/ppermute | solution.py:97
  183.0 28.7 %collective-permute-start.7 = (bf16[4,4,64,512]{3,2,1,0:T(8,128)(2,1)}, bf16[4,4,64,512]{3,2,1,0:T(8,128)(2,1)}, u32[]{:S(2)}, u32[]{:S(2)}) collective-permute-start(bf16[4,4,64,512]{3,2,1,0:T(8,128)(2,1)} %dynamic-slice_bitcast_fusion.2), channel_id=1, source_target_pairs={{0,8},{8,0},{1,9},{9,1},{2,10},{10,2},{3,11},{11,3},{4,12},{12,4},... | collective-permute-start | bytes 3145736 | tf_op jit(solution)/shard_map/ppermute | solution.py:97
  231.8 68.5 %all-gather.8.cloned.1.call-start = ((), (), s32[]{:S(2)}) async-start(), calls=%async_computation.14 | async-start | bytes 2621440 | tf_op jit(solution)/shard_map/all_gather | solution.py:674
  261.1 67.4 %all-to-all-start.4 = ((bf16[4,128,2048]{2,1,0:T(8,128)(2,1)}), bf16[4,128,2048]{2,1,0:T(8,128)(2,1)S(1)}, u32[]{:S(2)}, u32[]{:S(2)}) async-start(bf16[4,128,2048]{2,1,0:T(8,128)(2,1)} %get-tuple-element.38), calls=%async_computation.4 | async-start | bytes 4194304 | tf_op jit(solution)/shard_map/all_to_all | solution.py:178
  268.4 233.9 %reduce-scatter.7.cloned.1.call-start = ((), (), s32[]{:S(2)}) async-start(), calls=%async_computation.15 | async-start | bytes 5242880
  300.3 28.3 %collective-permute-start.9 = (bf16[4,128,2048]{2,1,0:T(8,128)(2,1)}, bf16[4,128,2048]{2,1,0:T(8,128)(2,1)}, u32[]{:S(2)}, u32[]{:S(2)}) collective-permute-start(bf16[4,128,2048]{2,1,0:T(8,128)(2,1)} %all-gather.8.cloned.1.call-done), channel_id=1, source_target_pairs={{0,8},{8,0},{1,9},{9,1},{2,10},{10,2},{3,11},{11,3},{4,12},{12,4},... | collective-permute-start | bytes 6291464 | tf_op jit(solution)/shard_map/ppermute | solution.py:97
  391.1 52.9 %all-to-all-start.5 = ((bf16[4,128,2048]{2,1,0:T(8,128)(2,1)}), bf16[4,128,2048]{2,1,0:T(8,128)(2,1)S(1)}, u32[]{:S(2)}, u32[]{:S(2)}) async-start(bf16[4,128,2048]{2,1,0:T(8,128)(2,1)} %add_convert_fusion), calls=%async_computation.5 | async-start | bytes 4194304 | tf_op jit(solution)/shard_map/all_to_all | solution.py:178
  449.6 31.6 %all-to-all-start.6 = ((bf16[4,128,2048]{2,1,0:T(8,128)(2,1)}), bf16[4,128,2048]{2,1,0:T(8,128)(2,1)}, u32[]{:S(2)}, u32[]{:S(2)}) async-start(bf16[4,128,2048]{2,1,0:T(8,128)(2,1)} %get-tuple-element.49), calls=%async_computation.6 | async-start | bytes 4194304 | tf_op jit(solution)/shard_map/all_to_all | solution.py:178
  454.2 217.6 %reduce-scatter.9.cloned.1.call-start = ((), (), s32[]{:S(2)}) async-start(), calls=%async_computation.16 | async-start | bytes 10485760
  490.1 28.1 %all-to-all-start.7 = ((bf16[4,256,256]{2,1,0:T(8,128)(2,1)}), bf16[4,256,256]{2,1,0:T(8,128)(2,1)S(1)}, u32[]{:S(2)}, u32[]{:S(2)}) async-start(bf16[4,256,256]{2,1,0:T(8,128)(2,1)} %shard_map.215), calls=%async_computation.7 | async-start | bytes 1048576 | tf_op jit(solution)/shard_map/all_to_all | solution.py:178
  496.5 54.4 %collective-permute-start.14 = (bf16[128,2048]{1,0:T(8,128)(2,1)}, bf16[128,2048]{1,0:T(8,128)(2,1)}, u32[]{:S(2)}, u32[]{:S(2)}) collective-permute-start(bf16[128,2048]{1,0:T(8,128)(2,1)} %get-tuple-element.63), channel_id=1, source_target_pairs={{0,6},{2,4},{4,2},{6,0},{1,7},{3,5},{5,3},{7,1},{8,14},{10,12},{12... | collective-permute-start | bytes 1572872 | tf_op jit(solution)/shard_map/ppermute | solution.py:97
  504.1 36.8 %collective-permute-start.15 = (bf16[4,64,1024]{2,1,0:T(8,128)(2,1)}, bf16[4,64,1024]{2,1,0:T(8,128)(2,1)}, u32[]{:S(2)}, u32[]{:S(2)}) collective-permute-start(bf16[4,64,1024]{2,1,0:T(8,128)(2,1)} %dynamic-slice_bitcast_fusion.3), channel_id=1, source_target_pairs={{0,8},{8,0},{1,9},{9,1},{2,10},{10,2},{3,11},{11,3},{4,12},{12,4},... | collective-permute-start | bytes 1572872 | tf_op jit(solution)/shard_map/ppermute | solution.py:97
  540.8 44.0 %collective-permute-start.26 = (bf16[4,4,64,512]{3,2,1,0:T(8,128)(2,1)}, bf16[4,4,64,512]{3,2,1,0:T(8,128)(2,1)}, u32[]{:S(2)}, u32[]{:S(2)}) collective-permute-start(bf16[4,4,64,512]{3,2,1,0:T(8,128)(2,1)} %fusion.5), channel_id=1, source_target_pairs={{0,8},{8,0},{1,9},{9,1},{2,10},{10,2},{3,11},{11,3},{4,12},{12,4},... | collective-permute-start | bytes 3145736 | tf_op jit(solution)/shard_map/ppermute | solution.py:97
  584.8 46.3 %collective-permute-start.19 = (bf16[4,4,64,768]{3,2,0,1:T(8,128)(2,1)}, bf16[4,4,64,768]{3,2,0,1:T(8,128)(2,1)}, u32[]{:S(2)}, u32[]{:S(2)}) collective-permute-start(bf16[4,4,64,768]{3,2,0,1:T(8,128)(2,1)} %fusion.4), channel_id=1, source_target_pairs={{0,8},{8,0},{1,9},{9,1},{2,10},{10,2},{3,11},{11,3},{4,12},{12,4},... | collective-permute-start | bytes 4718600 | tf_op jit(solution)/shard_map/ppermute | solution.py:97
  594.1 44.5 %all-to-all-start.9 = ((bf16[4,128,2048]{2,1,0:T(8,128)(2,1)}), bf16[4,128,2048]{2,1,0:T(8,128)(2,1)}, u32[]{:S(2)}, u32[]{:S(2)}) async-start(bf16[4,128,2048]{2,1,0:T(8,128)(2,1)} %get-tuple-element.52), calls=%async_computation.9 | async-start | bytes 4194304 | tf_op jit(solution)/shard_map/all_to_all | solution.py:178
  635.7 31.5 %collective-permute-start.21 = (bf16[4,64,768]{2,1,0:T(8,128)(2,1)S(1)}, bf16[4,64,768]{2,1,0:T(8,128)(2,1)}, u32[]{:S(2)}, u32[]{:S(2)}) collective-permute-start(bf16[4,64,768]{2,1,0:T(8,128)(2,1)S(1)} %get-tuple-element.68), channel_id=1, source_target_pairs={{0,4},{2,6},{4,0},{6,2},{1,5},{3,7},{5,1},{7,3},{8,12},{10,14},{12... | collective-permute-start | bytes 1179656 | tf_op jit(solution)/shard_map/ppermute | solution.py:97
  637.8 29.5 %collective-permute-start.20 = (bf16[4,64,768]{2,1,0:T(8,128)(2,1)S(1)}, bf16[4,64,768]{2,1,0:T(8,128)(2,1)}, u32[]{:S(2)}, u32[]{:S(2)}) collective-permute-start(bf16[4,64,768]{2,1,0:T(8,128)(2,1)S(1)} %get-tuple-element.66), channel_id=1, source_target_pairs={{0,2},{2,0},{4,6},{6,4},{1,3},{3,1},{5,7},{7,5},{8,10},{10,8},{12,... | collective-permute-start | bytes 1179656 | tf_op jit(solution)/shard_map/ppermute | solution.py:97
  693.9 35.2 %collective-permute-start.35 = (bf16[2,64,2048]{2,1,0:T(8,128)(2,1)}, bf16[2,64,2048]{2,1,0:T(8,128)(2,1)}, u32[]{:S(2)}, u32[]{:S(2)}) collective-permute-start(bf16[2,64,2048]{2,1,0:T(8,128)(2,1)} %pad_maximum_fusion.4), channel_id=1, source_target_pairs={{0,4},{2,6},{4,0},{6,2},{1,5},{3,7},{5,1},{7,3},{8,12},{10,14},{12... | collective-permute-start | bytes 1572872 | tf_op jit(solution)/shard_map/ppermute | solution.py:97
  694.8 46.2 %collective-permute-start.36 = (bf16[2,64,2048]{2,1,0:T(8,128)(2,1)}, bf16[2,64,2048]{2,1,0:T(8,128)(2,1)}, u32[]{:S(2)}, u32[]{:S(2)}) collective-permute-start(bf16[2,64,2048]{2,1,0:T(8,128)(2,1)} %pad_maximum_fusion.5), channel_id=1, source_target_pairs={{0,6},{2,4},{4,2},{6,0},{1,7},{3,5},{5,3},{7,1},{8,14},{10,12},{12... | collective-permute-start | bytes 1572872 | tf_op jit(solution)/shard_map/ppermute | solution.py:97
  (73 other events, 731.0 us)
Sparse Core Ops, SparseCore 0:
  26.2 42.4 all-gather.3
  90.5 123.4 all-gather.5
  239.0 61.2 all-gather.7
  381.2 54.5 reduce-scatter.6
  490.2 87.6 reduce-scatter.8

commit v4 on v3

--- a/solution.py
+++ b/solution.py
@@ -147,22 +147,18 @@
     )[0]
 
 
-def attention_weights(mine, sizes, splits):
+def attention_weights(own, sizes):
     yn, cn, zn, xn = [sizes[axis] for axis in "yczx"]
-    rows = mine.shape[1]
+    rows, cols = own[0].shape[1:]
     core, column = lax.axis_index("c"), lax.axis_index("z")
-    own = spread(mine, "z")
-    results = []
-    for start, end in splits:
-        full = jnp.zeros((yn * xn, cn, zn, rows, end - start), BF)
-        for k in range(zn):
-            full = put(full, own[k][..., start:end], (1, core), (2, column ^ k))
-        other = trade(pick(full, core, 1), "c", 1)
-        results.append(put(full, other, (1, core ^ 1)).reshape(-1, end - start))
-    return results, own[1:]
-
-
-def attention_grads(partial, sizes, *earlier):
+    full = jnp.zeros((yn * xn, cn, zn, rows, cols), BF)
+    for k in range(zn):
+        full = put(full, own[k], (1, core), (2, column ^ k))
+    other = trade(pick(full, core, 1), "c", 1)
+    return put(full, other, (1, core ^ 1)).reshape(-1, cols)
+
+
+def attention_grads(partial, sizes, earlier, later):
     yn, cn, zn, xn = [sizes[axis] for axis in "yczx"]
     cols = partial.shape[-1]
     blocks = partial.reshape(yn * xn, cn, zn, -1, cols)
@@ -170,7 +166,7 @@
     got = trade(pick(blocks, core ^ 1, 1).astype(BF), "c", 1)
     near = (pick(blocks, core, 1) + got.astype(F32)).astype(BF)
     there = swap(after(near, *earlier), "z", 1)
-    mine = total(there).astype(BF)
+    mine = after(total(there).astype(BF), *later)
     return in_order(swap(mine, PLANE), PLANE).astype(F32), there[1:]
 
 
@@ -196,15 +192,15 @@
     return mine.reshape(sizes["c"], sizes["z"], -1, cols)
 
 
-def ffn_grads_near(mine, *earlier):
+def ffn_grads_near(mine):
     core, column = lax.axis_index("c"), lax.axis_index("z")
     own = pick(mine, core, 0)
-    other = after(trade(pick(mine, core ^ 1, 0), "c", 1), *earlier)
+    other = trade(pick(mine, core ^ 1, 0), "c", 1)
     parts = []
     for k in range(mine.shape[1]):
         part = jnp.stack([pick(own, column ^ k, 0), pick(other, column ^ k, 0)])
         parts.append(trade(part, "z", k) if k else part)
-    return parts
+    return parts, other
 
 
 def ffn_slices(sizes):
@@ -454,7 +450,11 @@
         out_specs=[narrow] * 3 + [pl.BlockSpec((count, row_tile), lambda i: (0, second(i)))],
         scratch_shapes=[pltpu.VMEM((count, units), BF)] * 2,
         compiler_params=pltpu.CompilerParams(vmem_limit_bytes=VMEM_BYTES),
-        cost_estimate=pl.CostEstimate(flops=1, bytes_accessed=1, transcendentals=0),
+        cost_estimate=pl.CostEstimate(
+            flops=10 * count * width * units,
+            bytes_accessed=10 * width * units,
+            transcendentals=count * units,
+        ),
     )(tokens, grads, *[weights] * 5, *ties)
 
 
@@ -485,59 +485,59 @@
     )(z, weights, *added)
 
 
-def outer_kernel(count, *refs):
-    left_near, left_far = refs[0][...].T, refs[1][...].T
-    outs = refs[2 + 2 * count :]
-    for j in range(count):
-        near, far = refs[2 + 2 * j], refs[3 + 2 * j]
-        outs[0][:, j * near.shape[1] : (j + 1) * near.shape[1]] = (
-            mm(left_near, near[...]) + mm(left_far, far[...])
-        ).astype(BF)
-
-
-def outer(left, rights, ties=()):
-    count, width = left[0].shape
-    units = rights[0][0].shape[1]
+def outer_kernel(*refs):
+    tokens, grads = refs[0:2], refs[2:4]
+    dgate, dup, hidden, out_ref = refs[4:6], refs[6:8], refs[8:10], refs[10]
+    units = hidden[0].shape[1]
+    tokens_t = [half[...].T for half in tokens]
+    grads_t = [half[...].T for half in grads]
+    for j, (left, right) in enumerate(((tokens_t, dgate), (tokens_t, dup), (grads_t, hidden))):
+        part = mm(left[0], right[0][...]) + mm(left[1], right[1][...])
+        out_ref[:, j * units : (j + 1) * units] = part.astype(BF)
+
+
+def outer(tokens, grads, dgate, dup, hidden):
+    count, width = tokens[0].shape
+    units = hidden[0].shape[1]
     tile = min(512, width)
-    flat = [array for pair in rights for array in pair]
+    narrow = pl.BlockSpec((count, tile), lambda i: (0, i))
+    whole = pl.BlockSpec((count, units), lambda i: (0, 0))
     return pl.pallas_call(
-        skipping(functools.partial(outer_kernel, len(rights)), 2 + len(flat), len(ties)),
+        outer_kernel,
         grid=(width // tile,),
-        out_shape=[jax.ShapeDtypeStruct((width, len(rights) * units), BF)],
-        in_specs=[pl.BlockSpec((count, tile), lambda i: (0, i))] * 2
-        + [pl.BlockSpec((count, units), lambda i: (0, 0))] * len(flat)
-        + [pl.BlockSpec(memory_space=pl.ANY)] * len(ties),
-        out_specs=[pl.BlockSpec((tile, len(rights) * units), lambda i: (i, 0))],
+        out_shape=jax.ShapeDtypeStruct((width, 3 * units), BF),
+        in_specs=[narrow] * 4 + [whole] * 6,
+        out_specs=pl.BlockSpec((tile, 3 * units), lambda i: (i, 0)),
         compiler_params=pltpu.CompilerParams(vmem_limit_bytes=VMEM_BYTES),
         cost_estimate=pl.CostEstimate(flops=1, bytes_accessed=1, transcendentals=0),
-    )(*left, *flat, *ties)[0]
-
-
-def finish_kernel(count, slices, *refs):
-    pieces = len(refs) - 2 * count - 3
+    )(*tokens, *grads, *dgate, *dup, *hidden)
+
+
+def finish_kernel(slices, *refs):
+    pieces = len(refs) - 8
     spots, parts = refs[0], refs[1 : 1 + pieces]
-    weights, gain = refs[1 + pieces : 1 + pieces + count], refs[1 + pieces + count]
-    outs, gain_out = refs[2 + pieces + count : -1], refs[-1]
+    weights, gain = refs[1 + pieces : 3 + pieces], refs[3 + pieces]
+    outs, gain_out = refs[4 + pieces : 7 + pieces], refs[7 + pieces]
     width = outs[0].shape[1] // slices
     found = 0.0
     for k in range(pieces):
         for i in range(parts[k].shape[0]):
             spot = spots[k * parts[k].shape[0] + i]
             columns = pl.ds(pl.multiple_of(spot * width, width), width)
-            for j in range(count):
+            for j in range(2):
                 part = parts[k][i, :, j * width : (j + 1) * width].astype(F32)
                 outs[j][:, columns] = part * gain[...]
                 found = found + part * weights[j][:, columns].astype(F32)
+            outs[2][:, columns] = parts[k][i, :, 2 * width :].astype(F32)
     gain_out[...] = jnp.sum(found, axis=1, keepdims=True)
 
 
 def finish(parts, spots, weights, gain):
-    count, rows = len(weights), weights[0].shape[0]
+    rows = gain.shape[0]
     return in_vmem(
-        functools.partial(finish_kernel, count, sum(part.shape[0] for part in parts)),
+        functools.partial(finish_kernel, sum(part.shape[0] for part in parts)),
         list(parts) + list(weights) + [gain],
-        [jax.ShapeDtypeStruct(weight.shape, F32) for weight in weights]
-        + [jax.ShapeDtypeStruct((rows, 1), F32)],
+        [jax.ShapeDtypeStruct(weights[0].shape, F32)] * 3 + [jax.ShapeDtypeStruct((rows, 1), F32)],
         [],
         spots,
     )
@@ -567,7 +567,7 @@
     return [pl.BlockSpec(memory_space=pltpu.VMEM)] * count
 
 
-def attention_forward(seq, q_cols, kv_cols):
+def attention_forward(seq, q_cols, kv_cols, ties):
     length = seq.shape[0]
     return in_vmem(
         functools.partial(forward_kernel, q_cols, kv_cols),
@@ -577,6 +577,7 @@
             jax.ShapeDtypeStruct((q_cols // HEAD_DIM, length), F32),
         ],
         [],
+        ties=ties,
     )
 
 
@@ -653,9 +654,9 @@
     )
     ffn_full = ffn_weights_far(after(ffn_near, near_attn))
     qkv_width = halves * part_cols
-    (qkv_full, o_full), qkv_there = attention_weights(
-        after(near_attn, ffn_near), sizes, ((0, qkv_width), (qkv_width, near_attn.shape[-1]))
-    )
+    qkv_own = spread(after(near_attn[..., :qkv_width], ffn_near), "z")
+    o_own = spread(after(near_attn[..., qkv_width:], *qkv_own[1:]), "z")
+    qkv_full = attention_weights(qkv_own, sizes)
     digits = tokens_one[:, width:].astype(F32)
     cosine, sine = angles_of(digits[:, 0] * 128.0 + digits[:, HEAD_DIM])
     cosine = jnp.concatenate([cosine] * 4, axis=1)
@@ -670,7 +671,8 @@
         [],
     )
     heads_in = all_to_all(packed, "z").reshape(length, part_cols)
-    attended, logsums = attention_forward(heads_in, q_cols, kv_cols)
+    attended, logsums = attention_forward(heads_in, q_cols, kv_cols, o_own[1:])
+    o_full = attention_weights(o_own, sizes)
     grad_near = lax.all_gather(after(grad_low, attended), "z", axis=0, tiled=False)
     attended = all_to_all(attended.reshape(zn, piece, q_cols), "z")
 
@@ -711,22 +713,23 @@
     grad_both = dx_near.reshape(blocks) + trade(dx_far.reshape(blocks), "c", 1).astype(F32)
     grad_both = grad_both.astype(BF)
     grad_there = all_to_all(grad_both, "z")
-    gate_up_part = outer(
+    ffn_part = outer(
         (tokens_near, tokens_far),
-        [(dgate_near, dgate_far), (dup_near, dup_far)],
+        (grad_near, grad_far),
+        (dgate_near, dgate_far),
+        (dup_near, dup_far),
+        (z_near, z_far),
     )
     result_far = add_product(z_far, ffn_full)
     result_near = add_product(z_near, ffn_full, trade(result_far, "c", 1)).reshape(blocks)
-    down_part = outer((grad_near, grad_far), [(z_near, z_far)])
     grad_one, branch_tokens = in_vmem(
         norm_back_kernel,
         [grad_there, grad_low, unit_two, factor_two],
         [square, jax.ShapeDtypeStruct((slices, span, width), BF)],
         [],
-        ties=[result_near, gate_up_part],
+        ties=[result_near, ffn_part],
     )
     result_there = swap(result_near, "z")
-    down_sum = ffn_grads(down_part, sizes)
 
     branch_tokens = all_to_all(branch_tokens, PLANE).reshape(-1, width)
     (grad_attn,) = in_vmem(
@@ -736,16 +739,12 @@
         [],
         ties=result_there[1:3],
     )
-    gate_up_sum = ffn_grads(after(gate_up_part, grad_attn), sizes)
+    ffn_sum = ffn_grads(after(ffn_part, grad_attn), sizes)
     grad_heads = all_to_all(grad_attn, "z")
-    down_sum = ffn_grads_near(down_sum)
     grad_heads = grad_heads.reshape(length, q_cols)
     heads_out = attention_backward(heads_in, grad_heads, logsums, q_cols, kv_cols)
     back = all_to_all(heads_out.reshape(zn, piece, part_cols), "z")
-    o_sum, o_sum_there = attention_grads(
-        contract_rows(branch_tokens, attn_tokens), sizes, back
-    )
-    gate_up_sum = ffn_grads_near(gate_up_sum)
+    ffn_sum, _ = ffn_grads_near(ffn_sum)
     output = (after(hidden_one, grad_heads) + total(result_there)).astype(BF)
     grad_qkv, hat_part = in_vmem(
         functools.partial(qkv_back_kernel, halves, rotated),
@@ -755,21 +754,19 @@
             jax.ShapeDtypeStruct((slices, span, width), BF),
         ],
         [],
-        ties=down_sum[1:],
     )
     grad_hat_one = after(scatter_plane(hat_part), result_there[3])
     input_grad = grad_one + norm_backward(grad_hat_one, unit_one, factor_one)
-    qkv_sum, _ = attention_grads(
-        contract_rows(tokens_one[:, :width], grad_qkv), sizes
-    )
+    qkv_part = contract_rows(tokens_one[:, :width], grad_qkv)
+    qkv_sum, qkv_there = attention_grads(qkv_part, sizes, [], [])
+    o_sum, _ = attention_grads(contract_rows(branch_tokens, attn_tokens), sizes, qkv_there, [])
     attn_gain_grad = jnp.sum(qkv_sum * qkv_rows.astype(F32), axis=(0, 2))
     qkv_grad = (qkv_sum * gain_one[None]).transpose(1, 0, 2)
     qkv_grad = qkv_grad.reshape(rows, slices, halves, part_cols)
     spots = ffn_slices(sizes)
-    gate_grad, up_grad, ffn_gain_grad = finish(
-        gate_up_sum, spots, (gate_weight, up_weight), gain_two
-    )
-    (down_grad, _) = finish(down_sum, spots, (down_weight,), jnp.ones_like(gain_two))
+    gate_grad, up_grad, down_grad, ffn_gain_grad = finish(
+        ffn_sum, spots, (gate_weight, up_weight), gain_two
+    )
 
     def narrow(part):
         part = part.reshape(rows, KV_HEADS, copies, HEAD_DIM).sum(axis=2)

time: 765 us -> 749 us (0.979)
  waiting for transfers between devices: 362 us -> 341 us
  blocking collectives: 0 us -> 16.7 us
  other arithmetic: 42.2 us -> 34.5 us
    ppermute x37 -> x36, waiting for transfers between devices: 201 us -> 152 us  [trade(): return lax.ppermute(value, axes, [(i, i ^ step) for i in range(count)])]
    all_to_all x10 -> x9, waiting for transfers between devices: 130 us -> 158 us  [all_to_all(): return lax.all_to_all(blocks, axes, split_axis=0, concat_axis=0, tiled=True)]
    all_to_all x0 -> x1, blocking collectives: none -> 16.7 us  [all_to_all(): return lax.all_to_all(blocks, axes, split_axis=0, concat_axis=0, tiled=True)]
    all_to_all x10 -> x9, starting transfers between devices: 57.3 us -> 50.2 us  [all_to_all(): return lax.all_to_all(blocks, axes, split_axis=0, concat_axis=0, tiled=True)]
    unnamed x96 -> x94, local copies, waits for them, and re-layouts: 21.8 us -> 24.9 us
    ppermute x37 -> x36, starting transfers between devices: 36.1 us -> 39 us  [trade(): return lax.ppermute(value, axes, [(i, i ^ step) for i in range(count)])]
    pallas_call x2 -> x1, Pallas kernels: 21.8 us -> 19.2 us  [outer(): pl.pallas_call(outer_kernel, grid=(width // tile,), out_shape=jax.ShapeDt...]
    pallas_call x14 -> x13, Pallas kernels: 68.1 us -> 65.7 us  [in_vmem(): pl.pallas_call(kernel, out_shape=outs, in_specs=[pl.BlockSpec(memory_spac...]
  transfers between devices with their start and end apart: 52 -> 49, of which waited for: 30 -> 25; matrix products, arithmetic and copies ran while one was open for 14% -> 13% of each run, Pallas kernels for 12% -> 14%
where the time goes in v4:
time: 749 us; the launch traced here: 742 us
  waiting for transfers between devices  341 us (46%)
  Pallas kernels  136 us (18%)
  starting transfers between devices  89.6 us (12%)
  local copies, waits for them, and re-layouts  87.1 us (12%)
  other arithmetic  34.5 us (5%)
  between operations  30.7 us (4%)
  blocking collectives  16.7 us (2%)
    all_to_all x9, waiting for transfers between devices, all_to_all(): return lax.all_to_all(blocks, axes, split_axis=0, concat_axis=0, tiled=True)  158 us
    ppermute x36, waiting for transfers between devices, trade(): return lax.ppermute(value, axes, [(i, i ^ step) for i in range(count)])  152 us
    pallas_call x13, Pallas kernels, in_vmem(): pl.pallas_call(kernel, out_shape=outs, in_specs=[pl.BlockSpec(memory_spac...  65.7 us
    all_to_all x9, starting transfers between devices, all_to_all(): return lax.all_to_all(blocks, axes, split_axis=0, concat_axis=0, tiled=True)  50.2 us
    ppermute x36, starting transfers between devices, trade(): return lax.ppermute(value, axes, [(i, i ^ step) for i in range(count)])  39 us
    pallas_call x2, Pallas kernels, ffn(): pl.pallas_call(skipping(functools.partial(ffn_kernel, tiles), 7, len(ties...  38.3 us
    all_gather x1, waiting for transfers between devices, body(): lax.all_gather(after(grad_low, attended), 'z', axis=0, tiled=False)  31.6 us
    unnamed x94, local copies, waits for them, and re-layouts  24.9 us
  transfers between devices with their start and end apart: 49, of which 25 were waited for; matrix products, arithmetic and copies ran while one was open for 13% of the time, Pallas kernels for 14%

profile of v4, /device:TPU:8, one launch (start us, length us, event | category | flops | bytes accessed | tf_op | source)
XLA Modules:
  0.0 741.8 jit_solution(7201095820825214066)
XLA Ops:
  53.2 34.9 %all-to-all-done = bf16[8,64,3072]{2,1,0:T(8,128)(2,1)S(1)} async-done(((bf16[8,64,3072]{2,1,0:T(8,128)(2,1)}), bf16[8,64,3072]{2,1,0:T(8,128)(2,1)S(1)}, u32[]{:S(2)}, u32[]{:S(2)}) %all-to-all-start) | async-done | bytes 3145760 | tf_op jit(solution)/shard_map/all_to_all | solution.py:174
  98.7 14.6 %collective-permute-done.3 = bf16[4,64,768]{2,1,0:T(8,128)(2,1)} collective-permute-done((bf16[4,64,768]{2,1,0:T(8,128)(2,1)S(1)}, bf16[4,64,768]{2,1,0:T(8,128)(2,1)}, u32[]{:S(2)}, u32[]{:S(2)}) %collective-permute-start.3) | collective-permute-done | bytes 393248 | tf_op jit(solution)/shard_map/ppermute | solution.py:97
  114.4 9.7 %collective-permute-done.4 = bf16[4,64,768]{2,1,0:T(8,128)(2,1)S(1)} collective-permute-done((bf16[4,64,768]{2,1,0:T(8,128)(2,1)S(1)}, bf16[4,64,768]{2,1,0:T(8,128)(2,1)S(1)}, u32[]{:S(2)}, u32[]{:S(2)}) %collective-permute-start.4) | collective-permute-done | bytes 393248 | tf_op jit(solution)/shard_map/ppermute | solution.py:97
  124.2 8.8 %collective-permute-done.5 = bf16[4,64,768]{2,1,0:T(8,128)(2,1)S(1)} collective-permute-done((bf16[4,64,768]{2,1,0:T(8,128)(2,1)S(1)}, bf16[4,64,768]{2,1,0:T(8,128)(2,1)S(1)}, u32[]{:S(2)}, u32[]{:S(2)}) %collective-permute-start.5) | collective-permute-done | bytes 393248 | tf_op jit(solution)/shard_map/ppermute | solution.py:97
  169.7 14.0 %collective-permute-done.9.refs_3_ = bf16[4,64,512]{2,1,0:T(8,128)(2,1)} collective-permute-done((bf16[4,64,512]{2,1,0:T(8,128)(2,1)S(1)}, bf16[4,64,512]{2,1,0:T(8,128)(2,1)}, u32[]{:S(2)}, u32[]{:S(2)}) %collective-permute-start.9) | collective-permute-done | bytes 262176 | tf_op jit(solution)/shard_map/ppermute | solution.py:97
  190.8 11.1 %shard_map.205 = (bf16[1024,256]{1,0:T(8,128)(2,1)}, f32[4,1024]{1,0:T(4,128)}) custom-call(bf16[1024,384]{1,0:T(8,128)(2,1)} %bitcast.269, bf16[4,64,512]{2,1,0:T(8,128)(2,1)} %collective-permute-done.7.refs_1_, bf16[4,64,512]{2,1,0:T(8,128)(2,1)} %collective-permute-done.8.refs_2_, bf16[4,64,512]{2,1,0:T(8,128)(2,1)} %collective-permute-done.9.refs_3_), custom_call_target="tpu_custom_call" | custom-call | flops 1 | bytes 1 | tf_op jit(solution)/shard_map/pallas_call | solution.py:553
  209.6 9.8 %all-to-all-done.2.refs_0_ = bf16[4,256,256]{2,1,0:T(8,128)(2,1)S(1)} async-done(((bf16[4,256,256]{2,1,0:T(8,128)(2,1)}), bf16[4,256,256]{2,1,0:T(8,128)(2,1)S(1)}, u32[]{:S(2)}, u32[]{:S(2)}) %all-to-all-start.2) | async-done | bytes 524320 | tf_op jit(solution)/shard_map/all_to_all | solution.py:174
  235.3 16.7 %all-to-all-done.3.refs_0_ = bf16[4,128,2048]{2,1,0:T(8,128)(2,1)S(1)} async-done(((bf16[4,128,2048]{2,1,0:T(8,128)(2,1)}), bf16[4,128,2048]{2,1,0:T(8,128)(2,1)S(1)}, u32[]{:S(2)}, u32[]{:S(2)}) %all-to-all-start.3) | async-done | bytes 2097184 | tf_op jit(solution)/shard_map/all_to_all | solution.py:174
  265.0 31.6 %all-gather.8.cloned.1.call-done = bf16[4,128,2048]{2,1,0:T(8,128)(2,1)} async-done(((bf16[1,128,2048]{2,1,0:T(8,128)(2,1)}), bf16[4,128,2048]{2,1,0:T(8,128)(2,1)}) %all-gather.8.cloned.1.call-update) | async-done | bytes 2097168 | tf_op jit(solution)/shard_map/all_gather | solution.py:676
  296.6 28.4 %all-to-all-done.4 = bf16[4,128,2048]{2,1,0:T(8,128)(2,1)S(1)} async-done(((bf16[4,128,2048]{2,1,0:T(8,128)(2,1)}), bf16[4,128,2048]{2,1,0:T(8,128)(2,1)S(1)}, u32[]{:S(2)}, u32[]{:S(2)}) %all-to-all-start.4) | async-done | bytes 2097184 | tf_op jit(solution)/shard_map/all_to_all | solution.py:174
  330.4 18.9 %shard_map.209 = (bf16[512,1024]{1,0:T(8,128)(2,1)}, bf16[512,1024]{1,0:T(8,128)(2,1)}, bf16[512,1024]{1,0:T(8,128)(2,1)}, bf16[512,2048]{1,0:T(8,128)(2,1)}) custom-call(bf16[512,2048]{1,0:T(8,128)(2,1)} %bitcast.267, bf16[512,2048]{1,0:T(8,128)(2,1)} %bitcast.51.refs_1_.refs_3_, bf16[2048,3072]{1,0:T(8,128)(2,1)} %bitcast.237, ...), custom_call_target="tpu_custom_call" | custom-call | flops 10737418240 | bytes 20971520 | tf_op jit(solution)/shard_map/pallas_call | solution.py:442
  349.6 19.4 %shard_map.210 = (bf16[512,1024]{1,0:T(8,128)(2,1)}, bf16[512,1024]{1,0:T(8,128)(2,1)}, bf16[512,1024]{1,0:T(8,128)(2,1)}, f32[512,2048]{1,0:T(8,128)}) custom-call(bf16[512,2048]{1,0:T(8,128)(2,1)} %bitcast.261, bf16[512,2048]{1,0:T(8,128)(2,1)} %bitcast.265, bf16[2048,3072]{1,0:T(8,128)(2,1)} %bitcast.242, bf16[2048,3072]{1,0:T(8,128)(2,1)} %bitcast.243, ...), custom_call_target="tpu_custom_call" | custom-call | flops 10737418240 | bytes 20971520 | tf_op jit(solution)/shard_map/pallas_call | solution.py:442
  373.2 7.6 %all-to-all-start.5 = ((bf16[4,128,2048]{2,1,0:T(8,128)(2,1)}), bf16[4,128,2048]{2,1,0:T(8,128)(2,1)S(1)}, u32[]{:S(2)}, u32[]{:S(2)}) async-start(bf16[4,128,2048]{2,1,0:T(8,128)(2,1)} %add_convert_fusion), calls=%async_computation.5 | async-start | bytes 4194304 | tf_op jit(solution)/shard_map/all_to_all | solution.py:174
  387.1 19.2 %shard_map.213.refs_5_ = bf16[2048,3072]{1,0:T(8,128)(2,1)} custom-call(bf16[512,2048]{1,0:T(8,128)(2,1)} %bitcast.262, bf16[512,2048]{1,0:T(8,128)(2,1)} %bitcast.268, bf16[512,2048]{1,0:T(8,128)(2,1)} %bitcast.266, bf16[512,2048]{1,0:T(8,128)(2,1)} %bitcast.51.refs_1_.refs_3_, bf16[512,1024]{1,0:T(8,128)(2,1)} %get-tuple-element.45.refs_4_, ...), custom_call_target="tpu_custom_call" | custom-call | flops 1 | bytes 1 | tf_op jit(solution)/shard_map/pallas_call | solution.py:505
  414.4 12.1 %all-to-all-done.5.refs_0_ = bf16[4,128,2048]{2,1,0:T(8,128)(2,1)S(1)} async-done(((bf16[4,128,2048]{2,1,0:T(8,128)(2,1)}), bf16[4,128,2048]{2,1,0:T(8,128)(2,1)S(1)}, u32[]{:S(2)}, u32[]{:S(2)}) %all-to-all-start.5) | async-done | bytes 2097184 | tf_op jit(solution)/shard_map/all_to_all | solution.py:174
  441.0 21.0 %collective-permute-done.15.refs_2_ = bf16[128,2048]{1,0:T(8,128)(2,1)S(1)} collective-permute-done((bf16[128,2048]{1,0:T(8,128)(2,1)S(1)}, bf16[128,2048]{1,0:T(8,128)(2,1)S(1)}, u32[]{:S(2)}, u32[]{:S(2)}) %collective-permute-start.15) | collective-permute-done | bytes 524320 | tf_op jit(solution)/shard_map/ppermute | solution.py:97
  473.9 16.7 %all_to_all.50 = bf16[4,256,256]{2,1,0:T(8,128)(2,1)} all-to-all(bf16[4,256,256]{2,1,0:T(8,128)(2,1)S(1)} %copy-done.25), channel_id=1, replica_groups=mesh['y'=2,'c'=2,'z'=4,'x'=2] {'z'}, dimensions={0} | all-to-all | bytes 1048576 | tf_op jit(solution)/shard_map/all_to_all | solution.py:174
  490.6 11.3 %shard_map.217 = bf16[1024,384]{1,0:T(8,128)(2,1)} custom-call(bf16[1024,384]{1,0:T(8,128)(2,1)} %bitcast.270, bf16[1024,256]{1,0:T(8,128)(2,1)} %bitcast.283, f32[4,1024]{1,0:T(4,128)} %get-tuple-element.51.refs_2_), custom_call_target="tpu_custom_call" | custom-call | flops 1 | bytes 1 | tf_op jit(solution)/shard_map/pallas_call | solution.py:553
  508.7 27.1 %all-to-all-done.8.refs_0_ = bf16[4,256,384]{2,1,0:T(8,128)(2,1)S(1)} async-done(((bf16[4,256,384]{2,1,0:T(8,128)(2,1)}), bf16[4,256,384]{2,1,0:T(8,128)(2,1)S(1)}, u32[]{:S(2)}, u32[]{:S(2)}) %all-to-all-start.8) | async-done | bytes 786464 | tf_op jit(solution)/shard_map/all_to_all | solution.py:174
  583.4 26.9 %all-to-all-done.9 = bf16[4,128,2048]{2,1,0:T(8,128)(2,1)} async-done(((bf16[4,128,2048]{2,1,0:T(8,128)(2,1)}), bf16[4,128,2048]{2,1,0:T(8,128)(2,1)}, u32[]{:S(2)}, u32[]{:S(2)}) %all-to-all-start.9) | async-done | bytes 2097184 | tf_op jit(solution)/shard_map/all_to_all | solution.py:174
  637.5 13.8 %collective-permute-done.28 = bf16[4,64,512]{2,1,0:T(8,128)(2,1)S(1)} collective-permute-done((bf16[4,64,512]{2,1,0:T(8,128)(2,1)S(1)}, bf16[4,64,512]{2,1,0:T(8,128)(2,1)S(1)}, u32[]{:S(2)}, u32[]{:S(2)}) %collective-permute-start.28) | collective-permute-done | bytes 262176 | tf_op jit(solution)/shard_map/ppermute | solution.py:97
  677.6 10.3 %collective-permute-done.33.refs_2_ = bf16[2,64,3072]{2,1,0:T(8,128)(2,1)} collective-permute-done((bf16[2,64,3072]{2,1,0:T(8,128)(2,1)S(1)}, bf16[2,64,3072]{2,1,0:T(8,128)(2,1)}, u32[]{:S(2)}, u32[]{:S(2)}) %collective-permute-start.33) | collective-permute-done | bytes 786464 | tf_op jit(solution)/shard_map/ppermute | solution.py:97
  687.9 24.1 %collective-permute-done.34.refs_3_ = bf16[2,64,3072]{2,1,0:T(8,128)(2,1)} collective-permute-done((bf16[2,64,3072]{2,1,0:T(8,128)(2,1)}, bf16[2,64,3072]{2,1,0:T(8,128)(2,1)}, u32[]{:S(2)}, u32[]{:S(2)}) %collective-permute-start.34) | collective-permute-done | bytes 786464 | tf_op jit(solution)/shard_map/ppermute | solution.py:97
  712.0 15.5 %collective-permute-done.35.refs_4_ = bf16[2,64,3072]{2,1,0:T(8,128)(2,1)} collective-permute-done((bf16[2,64,3072]{2,1,0:T(8,128)(2,1)}, bf16[2,64,3072]{2,1,0:T(8,128)(2,1)}, u32[]{:S(2)}, u32[]{:S(2)}) %collective-permute-start.35) | collective-permute-done | bytes 786464 | tf_op jit(solution)/shard_map/ppermute | solution.py:97
  (315 shorter events, 287.6 us)
Async XLA Ops:
  14.6 73.6 %all-to-all-start = ((bf16[8,64,3072]{2,1,0:T(8,128)(2,1)}), bf16[8,64,3072]{2,1,0:T(8,128)(2,1)S(1)}, u32[]{:S(2)}, u32[]{:S(2)}) async-start(bf16[8,64,3072]{2,1,0:T(8,128)(2,1)} %copy.177), calls=%async_computation | async-start | bytes 6291456 | tf_op jit(solution)/shard_map/all_to_all | solution.py:174
  20.0 116.0 %all-gather.4.cloned.1.call-start = ((), (), s32[]{:S(2)}) async-start(), calls=%async_computation.11 | async-start | bytes 2785280 | tf_op jit(solution)/shard_map/all_gather | solution.py:652
  26.1 225.9 %all-gather.6.cloned.1.call-start = ((), (), s32[]{:S(2)}) async-start(), calls=%async_computation.12 | async-start | bytes 15728640 | tf_op jit(solution)/shard_map/all_gather | solution.py:184
  96.9 27.3 %collective-permute-start.4 = (bf16[4,64,768]{2,1,0:T(8,128)(2,1)S(1)}, bf16[4,64,768]{2,1,0:T(8,128)(2,1)S(1)}, u32[]{:S(2)}, u32[]{:S(2)}) collective-permute-start(bf16[4,64,768]{2,1,0:T(8,128)(2,1)S(1)} %constant_dynamic-update-slice_fusion.10), channel_id=1, source_target_pairs={{0,4},{2,6},{4,0},{6,2},{1,5},{3,7},{5,1},{7,3},{8,12},{10,14},{12... | collective-permute-start | bytes 1179656 | tf_op jit(solution)/shard_map/ppermute | solution.py:97
  97.8 35.2 %collective-permute-start.5 = (bf16[4,64,768]{2,1,0:T(8,128)(2,1)S(1)}, bf16[4,64,768]{2,1,0:T(8,128)(2,1)S(1)}, u32[]{:S(2)}, u32[]{:S(2)}) collective-permute-start(bf16[4,64,768]{2,1,0:T(8,128)(2,1)S(1)} %constant_dynamic-update-slice_fusion.10), channel_id=1, source_target_pairs={{0,6},{2,4},{4,2},{6,0},{1,7},{3,5},{5,3},{7,1},{8,14},{10,12},{12... | collective-permute-start | bytes 1179656 | tf_op jit(solution)/shard_map/ppermute | solution.py:97
  150.0 33.6 %collective-permute-start.9 = (bf16[4,64,512]{2,1,0:T(8,128)(2,1)S(1)}, bf16[4,64,512]{2,1,0:T(8,128)(2,1)}, u32[]{:S(2)}, u32[]{:S(2)}) collective-permute-start(bf16[4,64,512]{2,1,0:T(8,128)(2,1)S(1)} %constant_dynamic-update-slice_fusion.9), channel_id=1, source_target_pairs={{0,6},{2,4},{4,2},{6,0},{1,7},{3,5},{5,3},{7,1},{8,14},{10,12},{12... | collective-permute-start | bytes 786440 | tf_op jit(solution)/shard_map/ppermute | solution.py:97
  161.1 28.7 %all-to-all-start.1 = ((bf16[4,256,384]{2,1,0:T(8,128)(2,1)}), bf16[4,256,384]{2,1,0:T(8,128)(2,1)S(1)}, u32[]{:S(2)}, u32[]{:S(2)}) async-start(bf16[4,256,384]{2,1,0:T(8,128)(2,1)} %shard_map.204), calls=%async_computation.1 | async-start | bytes 1572864 | tf_op jit(solution)/shard_map/all_to_all | solution.py:174
  224.5 27.5 %all-to-all-start.3 = ((bf16[4,128,2048]{2,1,0:T(8,128)(2,1)}), bf16[4,128,2048]{2,1,0:T(8,128)(2,1)S(1)}, u32[]{:S(2)}, u32[]{:S(2)}) async-start(bf16[4,128,2048]{2,1,0:T(8,128)(2,1)} %get-tuple-element.36), calls=%async_computation.3 | async-start | bytes 4194304 | tf_op jit(solution)/shard_map/all_to_all | solution.py:174
  228.2 68.4 %all-gather.8.cloned.1.call-start = ((), (), s32[]{:S(2)}) async-start(), calls=%async_computation.13 | async-start | bytes 2621440 | tf_op jit(solution)/shard_map/all_gather | solution.py:676
  257.6 67.4 %all-to-all-start.4 = ((bf16[4,128,2048]{2,1,0:T(8,128)(2,1)}), bf16[4,128,2048]{2,1,0:T(8,128)(2,1)S(1)}, u32[]{:S(2)}, u32[]{:S(2)}) async-start(bf16[4,128,2048]{2,1,0:T(8,128)(2,1)} %get-tuple-element.38), calls=%async_computation.4 | async-start | bytes 4194304 | tf_op jit(solution)/shard_map/all_to_all | solution.py:174
  296.6 28.4 %collective-permute-start.12 = (bf16[4,128,2048]{2,1,0:T(8,128)(2,1)}, bf16[4,128,2048]{2,1,0:T(8,128)(2,1)}, u32[]{:S(2)}, u32[]{:S(2)}) collective-permute-start(bf16[4,128,2048]{2,1,0:T(8,128)(2,1)} %all-gather.8.cloned.1.call-done), channel_id=1, source_target_pairs={{0,8},{8,0},{1,9},{9,1},{2,10},{10,2},{3,11},{11,3},{4,12},{12,4},... | collective-permute-start | bytes 6291464 | tf_op jit(solution)/shard_map/ppermute | solution.py:97
  373.2 53.3 %all-to-all-start.5 = ((bf16[4,128,2048]{2,1,0:T(8,128)(2,1)}), bf16[4,128,2048]{2,1,0:T(8,128)(2,1)S(1)}, u32[]{:S(2)}, u32[]{:S(2)}) async-start(bf16[4,128,2048]{2,1,0:T(8,128)(2,1)} %add_convert_fusion), calls=%async_computation.5 | async-start | bytes 4194304 | tf_op jit(solution)/shard_map/all_to_all | solution.py:174
  432.1 31.9 %all-to-all-start.6 = ((bf16[4,128,2048]{2,1,0:T(8,128)(2,1)}), bf16[4,128,2048]{2,1,0:T(8,128)(2,1)}, u32[]{:S(2)}, u32[]{:S(2)}) async-start(bf16[4,128,2048]{2,1,0:T(8,128)(2,1)} %get-tuple-element.49), calls=%async_computation.6 | async-start | bytes 4194304 | tf_op jit(solution)/shard_map/all_to_all | solution.py:174
  436.8 198.8 %reduce-scatter.4.cloned.1.call-start = ((), (), s32[]{:S(2)}) async-start(), calls=%async_computation.14 | async-start | bytes 15728640
  501.9 33.8 %all-to-all-start.8 = ((bf16[4,256,384]{2,1,0:T(8,128)(2,1)}), bf16[4,256,384]{2,1,0:T(8,128)(2,1)S(1)}, u32[]{:S(2)}, u32[]{:S(2)}) async-start(bf16[4,256,384]{2,1,0:T(8,128)(2,1)} %bitcast.278), calls=%async_computation.8 | async-start | bytes 1572864 | tf_op jit(solution)/shard_map/all_to_all | solution.py:174
  507.2 43.1 %collective-permute-start.17 = (bf16[128,2048]{1,0:T(8,128)(2,1)S(1)}, bf16[128,2048]{1,0:T(8,128)(2,1)}, u32[]{:S(2)}, u32[]{:S(2)}) collective-permute-start(bf16[128,2048]{1,0:T(8,128)(2,1)S(1)} %copy-done.32), channel_id=1, source_target_pairs={{0,6},{2,4},{4,2},{6,0},{1,7},{3,5},{5,3},{7,1},{8,14},{10,12},{12... | collective-permute-start | bytes 1572872 | tf_op jit(solution)/shard_map/ppermute | solution.py:97
  556.8 53.5 %all-to-all-start.9 = ((bf16[4,128,2048]{2,1,0:T(8,128)(2,1)}), bf16[4,128,2048]{2,1,0:T(8,128)(2,1)}, u32[]{:S(2)}, u32[]{:S(2)}) async-start(bf16[4,128,2048]{2,1,0:T(8,128)(2,1)} %get-tuple-element.52), calls=%async_computation.9 | async-start | bytes 4194304 | tf_op jit(solution)/shard_map/all_to_all | solution.py:174
  572.0 41.7 %collective-permute-start.25 = (bf16[4,4,64,512]{3,2,1,0:T(8,128)(2,1)}, bf16[4,4,64,512]{3,2,1,0:T(8,128)(2,1)S(1)}, u32[]{:S(2)}, u32[]{:S(2)}) collective-permute-start(bf16[4,4,64,512]{3,2,1,0:T(8,128)(2,1)} %fusion.5), channel_id=1, source_target_pairs={{0,8},{8,0},{1,9},{9,1},{2,10},{10,2},{3,11},{11,3},{4,12},{12,4},... | collective-permute-start | bytes 3145736 | tf_op jit(solution)/shard_map/ppermute | solution.py:97
  578.5 39.5 %collective-permute-start.21 = (bf16[4,64,768]{2,1,0:T(8,128)(2,1)}, bf16[4,64,768]{2,1,0:T(8,128)(2,1)}, u32[]{:S(2)}, u32[]{:S(2)}) collective-permute-start(bf16[4,64,768]{2,1,0:T(8,128)(2,1)} %get-tuple-element.71), channel_id=1, source_target_pairs={{0,6},{2,4},{4,2},{6,0},{1,7},{3,5},{5,3},{7,1},{8,14},{10,12},{12... | collective-permute-start | bytes 1179656 | tf_op jit(solution)/shard_map/ppermute | solution.py:97
  579.0 39.0 %collective-permute-start.20 = (bf16[4,64,768]{2,1,0:T(8,128)(2,1)}, bf16[4,64,768]{2,1,0:T(8,128)(2,1)}, u32[]{:S(2)}, u32[]{:S(2)}) collective-permute-start(bf16[4,64,768]{2,1,0:T(8,128)(2,1)} %get-tuple-element.72), channel_id=1, source_target_pairs={{0,4},{2,6},{4,0},{6,2},{1,5},{3,7},{5,1},{7,3},{8,12},{10,14},{12... | collective-permute-start | bytes 1179656 | tf_op jit(solution)/shard_map/ppermute | solution.py:97
  583.4 34.6 %collective-permute-start.19 = (bf16[4,64,768]{2,1,0:T(8,128)(2,1)S(1)}, bf16[4,64,768]{2,1,0:T(8,128)(2,1)}, u32[]{:S(2)}, u32[]{:S(2)}) collective-permute-start(bf16[4,64,768]{2,1,0:T(8,128)(2,1)S(1)} %get-tuple-element.70), channel_id=1, source_target_pairs={{0,2},{2,0},{4,6},{6,4},{1,3},{3,1},{5,7},{7,5},{8,10},{10,8},{12,... | collective-permute-start | bytes 1179656 | tf_op jit(solution)/shard_map/ppermute | solution.py:97
  655.4 32.5 %collective-permute-start.33 = (bf16[2,64,3072]{2,1,0:T(8,128)(2,1)S(1)}, bf16[2,64,3072]{2,1,0:T(8,128)(2,1)}, u32[]{:S(2)}, u32[]{:S(2)}) collective-permute-start(bf16[2,64,3072]{2,1,0:T(8,128)(2,1)S(1)} %pad_maximum_fusion.2), channel_id=1, source_target_pairs={{0,2},{2,0},{4,6},{6,4},{1,3},{3,1},{5,7},{7,5},{8,10},{10,8},{12,... | collective-permute-start | bytes 2359304 | tf_op jit(solution)/shard_map/ppermute | solution.py:97
  660.0 52.0 %collective-permute-start.34 = (bf16[2,64,3072]{2,1,0:T(8,128)(2,1)}, bf16[2,64,3072]{2,1,0:T(8,128)(2,1)}, u32[]{:S(2)}, u32[]{:S(2)}) collective-permute-start(bf16[2,64,3072]{2,1,0:T(8,128)(2,1)} %pad_maximum_fusion.3), channel_id=1, source_target_pairs={{0,4},{2,6},{4,0},{6,2},{1,5},{3,7},{5,1},{7,3},{8,12},{10,14},{12... | collective-permute-start | bytes 2359304 | tf_op jit(solution)/shard_map/ppermute | solution.py:97
  660.9 66.6 %collective-permute-start.35 = (bf16[2,64,3072]{2,1,0:T(8,128)(2,1)}, bf16[2,64,3072]{2,1,0:T(8,128)(2,1)}, u32[]{:S(2)}, u32[]{:S(2)}) collective-permute-start(bf16[2,64,3072]{2,1,0:T(8,128)(2,1)} %pad_maximum_fusion.4), channel_id=1, source_target_pairs={{0,6},{2,4},{4,2},{6,0},{1,7},{3,5},{5,3},{7,1},{8,14},{10,12},{12... | collective-permute-start | bytes 2359304 | tf_op jit(solution)/shard_map/ppermute | solution.py:97
  (69 other events, 742.2 us)
Sparse Core Ops, SparseCore 0:
  26.2 44.3 all-gather.3
  90.5 123.4 all-gather.5
  235.5 61.0 all-gather.7
  473.0 144.4 reduce-scatter.3

commit v5 on v4

--- a/solution.py
+++ b/solution.py
@@ -165,9 +165,10 @@
     core = lax.axis_index("c")
     got = trade(pick(blocks, core ^ 1, 1).astype(BF), "c", 1)
     near = (pick(blocks, core, 1) + got.astype(F32)).astype(BF)
-    there = swap(after(near, *earlier), "z", 1)
+    near = after(near, *earlier)
+    there = swap(near, "z", 1)
     mine = after(total(there).astype(BF), *later)
-    return in_order(swap(mine, PLANE), PLANE).astype(F32), there[1:]
+    return in_order(swap(mine, PLANE), PLANE).astype(F32), there[1:], near
 
 
 def all_to_all(blocks, axes):
@@ -745,7 +746,6 @@
     heads_out = attention_backward(heads_in, grad_heads, logsums, q_cols, kv_cols)
     back = all_to_all(heads_out.reshape(zn, piece, part_cols), "z")
     ffn_sum, _ = ffn_grads_near(ffn_sum)
-    output = (after(hidden_one, grad_heads) + total(result_there)).astype(BF)
     grad_qkv, hat_part = in_vmem(
         functools.partial(qkv_back_kernel, halves, rotated),
         [back, qkv_full, cosine, sine],
@@ -758,8 +758,10 @@
     grad_hat_one = after(scatter_plane(hat_part), result_there[3])
     input_grad = grad_one + norm_backward(grad_hat_one, unit_one, factor_one)
     qkv_part = contract_rows(tokens_one[:, :width], grad_qkv)
-    qkv_sum, qkv_there = attention_grads(qkv_part, sizes, [], [])
-    o_sum, _ = attention_grads(contract_rows(branch_tokens, attn_tokens), sizes, qkv_there, [])
+    qkv_sum, qkv_there, qkv_near = attention_grads(qkv_part, sizes, [], [])
+    attn_tokens = after(attn_tokens, qkv_near)
+    output = (after(hidden_one, qkv_near) + total(result_there)).astype(BF)
+    o_sum, _, _ = attention_grads(contract_rows(branch_tokens, attn_tokens), sizes, qkv_there, [])
     attn_gain_grad = jnp.sum(qkv_sum * qkv_rows.astype(F32), axis=(0, 2))
     qkv_grad = (qkv_sum * gain_one[None]).transpose(1, 0, 2)
     qkv_grad = qkv_grad.reshape(rows, slices, halves, part_cols)

time: 749 us -> 747 us (level)
  blocking collectives: 16.7 us -> 39.4 us
  waiting for transfers between devices: 341 us -> 327 us
  starting transfers between devices: 89.6 us -> 81.3 us
    all_to_all x9 -> x8, waiting for transfers between devices: 158 us -> 104 us  [all_to_all(): return lax.all_to_all(blocks, axes, split_axis=0, concat_axis=0, tiled=True)]
    ppermute x36, waiting for transfers between devices: 152 us -> 192 us  [trade(): return lax.ppermute(value, axes, [(i, i ^ step) for i in range(count)])]
    all_to_all x1 -> x2, blocking collectives: 16.7 us -> 39.4 us  [all_to_all(): return lax.all_to_all(blocks, axes, split_axis=0, concat_axis=0, tiled=True)]
    all_to_all x9 -> x8, starting transfers between devices: 50.2 us -> 44.6 us  [all_to_all(): return lax.all_to_all(blocks, axes, split_axis=0, concat_axis=0, tiled=True)]
    unnamed x94 -> x90, local copies, waits for them, and re-layouts: 24.9 us -> 23.8 us
  transfers between devices with their start and end apart: 49 -> 48, of which waited for: 25 -> 26; matrix products, arithmetic and copies ran while one was open for 13% -> 12% of each run, Pallas kernels for 14% -> 14%
where the time goes in v5:
time: 747 us; the launch traced here: 740 us
  waiting for transfers between devices  327 us (44%)
  Pallas kernels  136 us (18%)
  local copies, waits for them, and re-layouts  82 us (11%)
  starting transfers between devices  81.3 us (11%)
  blocking collectives  39.4 us (5%)
  other arithmetic  37.6 us (5%)
  between operations  31.5 us (4%)
    ppermute x36, waiting for transfers between devices, trade(): return lax.ppermute(value, axes, [(i, i ^ step) for i in range(count)])  192 us
    all_to_all x8, waiting for transfers between devices, all_to_all(): return lax.all_to_all(blocks, axes, split_axis=0, concat_axis=0, tiled=True)  104 us
    pallas_call x13, Pallas kernels, in_vmem(): pl.pallas_call(kernel, out_shape=outs, in_specs=[pl.BlockSpec(memory_spac...  65.8 us
    all_to_all x8, starting transfers between devices, all_to_all(): return lax.all_to_all(blocks, axes, split_axis=0, concat_axis=0, tiled=True)  44.6 us
    all_to_all x2, blocking collectives, all_to_all(): return lax.all_to_all(blocks, axes, split_axis=0, concat_axis=0, tiled=True)  39.4 us
    pallas_call x2, Pallas kernels, ffn(): pl.pallas_call(skipping(functools.partial(ffn_kernel, tiles), 7, len(ties...  38.4 us
    ppermute x36, starting transfers between devices, trade(): return lax.ppermute(value, axes, [(i, i ^ step) for i in range(count)])  36.3 us
    all_gather x1, waiting for transfers between devices, body(): lax.all_gather(after(grad_low, attended), 'z', axis=0, tiled=False)  31.6 us
  transfers between devices with their start and end apart: 48, of which 26 were waited for; matrix products, arithmetic and copies ran while one was open for 12% of the time, Pallas kernels for 14%

profile of v5, /device:TPU:8, one launch (start us, length us, event | category | flops | bytes accessed | tf_op | source)
XLA Modules:
  0.0 739.8 jit_solution(15538190028032845042)
XLA Ops:
  53.2 34.9 %all-to-all-done = bf16[8,64,3072]{2,1,0:T(8,128)(2,1)S(1)} async-done(((bf16[8,64,3072]{2,1,0:T(8,128)(2,1)}), bf16[8,64,3072]{2,1,0:T(8,128)(2,1)S(1)}, u32[]{:S(2)}, u32[]{:S(2)}) %all-to-all-start) | async-done | bytes 3145760 | tf_op jit(solution)/shard_map/all_to_all | solution.py:175
  98.7 14.6 %collective-permute-done.3 = bf16[4,64,768]{2,1,0:T(8,128)(2,1)} collective-permute-done((bf16[4,64,768]{2,1,0:T(8,128)(2,1)S(1)}, bf16[4,64,768]{2,1,0:T(8,128)(2,1)}, u32[]{:S(2)}, u32[]{:S(2)}) %collective-permute-start.3) | collective-permute-done | bytes 393248 | tf_op jit(solution)/shard_map/ppermute | solution.py:97
  114.4 9.7 %collective-permute-done.4 = bf16[4,64,768]{2,1,0:T(8,128)(2,1)S(1)} collective-permute-done((bf16[4,64,768]{2,1,0:T(8,128)(2,1)S(1)}, bf16[4,64,768]{2,1,0:T(8,128)(2,1)S(1)}, u32[]{:S(2)}, u32[]{:S(2)}) %collective-permute-start.4) | collective-permute-done | bytes 393248 | tf_op jit(solution)/shard_map/ppermute | solution.py:97
  124.2 8.8 %collective-permute-done.5 = bf16[4,64,768]{2,1,0:T(8,128)(2,1)S(1)} collective-permute-done((bf16[4,64,768]{2,1,0:T(8,128)(2,1)S(1)}, bf16[4,64,768]{2,1,0:T(8,128)(2,1)S(1)}, u32[]{:S(2)}, u32[]{:S(2)}) %collective-permute-start.5) | collective-permute-done | bytes 393248 | tf_op jit(solution)/shard_map/ppermute | solution.py:97
  169.7 14.0 %collective-permute-done.9.refs_3_ = bf16[4,64,512]{2,1,0:T(8,128)(2,1)} collective-permute-done((bf16[4,64,512]{2,1,0:T(8,128)(2,1)S(1)}, bf16[4,64,512]{2,1,0:T(8,128)(2,1)}, u32[]{:S(2)}, u32[]{:S(2)}) %collective-permute-start.9) | collective-permute-done | bytes 262176 | tf_op jit(solution)/shard_map/ppermute | solution.py:97
  190.8 11.1 %shard_map.205 = (bf16[1024,256]{1,0:T(8,128)(2,1)}, f32[4,1024]{1,0:T(4,128)}) custom-call(bf16[1024,384]{1,0:T(8,128)(2,1)} %bitcast.268, bf16[4,64,512]{2,1,0:T(8,128)(2,1)} %collective-permute-done.7.refs_1_, bf16[4,64,512]{2,1,0:T(8,128)(2,1)} %collective-permute-done.8.refs_2_, bf16[4,64,512]{2,1,0:T(8,128)(2,1)} %collective-permute-done.9.refs_3_), custom_call_target="tpu_custom_call" | custom-call | flops 1 | bytes 1 | tf_op jit(solution)/shard_map/pallas_call | solution.py:554
  209.6 9.8 %all-to-all-done.2.refs_0_ = bf16[4,256,256]{2,1,0:T(8,128)(2,1)S(1)} async-done(((bf16[4,256,256]{2,1,0:T(8,128)(2,1)}), bf16[4,256,256]{2,1,0:T(8,128)(2,1)S(1)}, u32[]{:S(2)}, u32[]{:S(2)}) %all-to-all-start.2) | async-done | bytes 524320 | tf_op jit(solution)/shard_map/all_to_all | solution.py:175
  235.4 16.7 %all-to-all-done.3.refs_0_ = bf16[4,128,2048]{2,1,0:T(8,128)(2,1)S(1)} async-done(((bf16[4,128,2048]{2,1,0:T(8,128)(2,1)}), bf16[4,128,2048]{2,1,0:T(8,128)(2,1)S(1)}, u32[]{:S(2)}, u32[]{:S(2)}) %all-to-all-start.3) | async-done | bytes 2097184 | tf_op jit(solution)/shard_map/all_to_all | solution.py:175
  265.0 31.6 %all-gather.8.cloned.1.call-done = bf16[4,128,2048]{2,1,0:T(8,128)(2,1)} async-done(((bf16[1,128,2048]{2,1,0:T(8,128)(2,1)}), bf16[4,128,2048]{2,1,0:T(8,128)(2,1)}) %all-gather.8.cloned.1.call-update) | async-done | bytes 2097168 | tf_op jit(solution)/shard_map/all_gather | solution.py:677
  296.6 28.3 %all-to-all-done.4 = bf16[4,128,2048]{2,1,0:T(8,128)(2,1)S(1)} async-done(((bf16[4,128,2048]{2,1,0:T(8,128)(2,1)}), bf16[4,128,2048]{2,1,0:T(8,128)(2,1)S(1)}, u32[]{:S(2)}, u32[]{:S(2)}) %all-to-all-start.4) | async-done | bytes 2097184 | tf_op jit(solution)/shard_map/all_to_all | solution.py:175
  330.5 18.9 %shard_map.209 = (bf16[512,1024]{1,0:T(8,128)(2,1)}, bf16[512,1024]{1,0:T(8,128)(2,1)}, bf16[512,1024]{1,0:T(8,128)(2,1)}, bf16[512,2048]{1,0:T(8,128)(2,1)}) custom-call(bf16[512,2048]{1,0:T(8,128)(2,1)} %bitcast.266, bf16[512,2048]{1,0:T(8,128)(2,1)} %bitcast.51.refs_1_.refs_3_, bf16[2048,3072]{1,0:T(8,128)(2,1)} %bitcast.238, ...), custom_call_target="tpu_custom_call" | custom-call | flops 10737418240 | bytes 20971520 | tf_op jit(solution)/shard_map/pallas_call | solution.py:443
  349.6 19.4 %shard_map.210 = (bf16[512,1024]{1,0:T(8,128)(2,1)}, bf16[512,1024]{1,0:T(8,128)(2,1)}, bf16[512,1024]{1,0:T(8,128)(2,1)}, f32[512,2048]{1,0:T(8,128)}) custom-call(bf16[512,2048]{1,0:T(8,128)(2,1)} %bitcast.260, bf16[512,2048]{1,0:T(8,128)(2,1)} %bitcast.264, bf16[2048,3072]{1,0:T(8,128)(2,1)} %bitcast.243, bf16[2048,3072]{1,0:T(8,128)(2,1)} %bitcast.244, ...), custom_call_target="tpu_custom_call" | custom-call | flops 10737418240 | bytes 20971520 | tf_op jit(solution)/shard_map/pallas_call | solution.py:443
  387.2 19.2 %shard_map.213.refs_5_ = bf16[2048,3072]{1,0:T(8,128)(2,1)} custom-call(bf16[512,2048]{1,0:T(8,128)(2,1)} %bitcast.261, bf16[512,2048]{1,0:T(8,128)(2,1)} %bitcast.267, bf16[512,2048]{1,0:T(8,128)(2,1)} %bitcast.265, bf16[512,2048]{1,0:T(8,128)(2,1)} %bitcast.51.refs_1_.refs_3_, bf16[512,1024]{1,0:T(8,128)(2,1)} %get-tuple-element.45.refs_4_, ...), custom_call_target="tpu_custom_call" | custom-call | flops 1 | bytes 1 | tf_op jit(solution)/shard_map/pallas_call | solution.py:506
  414.5 12.1 %all-to-all-done.5.refs_0_ = bf16[4,128,2048]{2,1,0:T(8,128)(2,1)S(1)} async-done(((bf16[4,128,2048]{2,1,0:T(8,128)(2,1)}), bf16[4,128,2048]{2,1,0:T(8,128)(2,1)S(1)}, u32[]{:S(2)}, u32[]{:S(2)}) %all-to-all-start.5) | async-done | bytes 2097184 | tf_op jit(solution)/shard_map/all_to_all | solution.py:175
  441.1 21.0 %collective-permute-done.15.refs_2_ = bf16[128,2048]{1,0:T(8,128)(2,1)S(1)} collective-permute-done((bf16[128,2048]{1,0:T(8,128)(2,1)S(1)}, bf16[128,2048]{1,0:T(8,128)(2,1)S(1)}, u32[]{:S(2)}, u32[]{:S(2)}) %collective-permute-start.15) | collective-permute-done | bytes 524320 | tf_op jit(solution)/shard_map/ppermute | solution.py:97
  474.0 16.7 %all_to_all.50 = bf16[4,256,256]{2,1,0:T(8,128)(2,1)} all-to-all(bf16[4,256,256]{2,1,0:T(8,128)(2,1)S(1)} %copy-done.24), channel_id=1, replica_groups=mesh['y'=2,'c'=2,'z'=4,'x'=2] {'z'}, dimensions={0} | all-to-all | bytes 1048576 | tf_op jit(solution)/shard_map/all_to_all | solution.py:175
  490.7 11.3 %shard_map.216 = bf16[1024,384]{1,0:T(8,128)(2,1)} custom-call(bf16[1024,384]{1,0:T(8,128)(2,1)} %bitcast.269, bf16[1024,256]{1,0:T(8,128)(2,1)} %bitcast.282, f32[4,1024]{1,0:T(4,128)} %get-tuple-element.50.refs_2_), custom_call_target="tpu_custom_call" | custom-call | flops 1 | bytes 1 | tf_op jit(solution)/shard_map/pallas_call | solution.py:554
  501.9 22.8 %all_to_all.51.refs_0_ = bf16[4,256,384]{2,1,0:T(8,128)(2,1)} all-to-all(bf16[4,256,384]{2,1,0:T(8,128)(2,1)} %bitcast.277), channel_id=1, replica_groups=mesh['y'=2,'c'=2,'z'=4,'x'=2] {'z'}, dimensions={0} | all-to-all | bytes 1572864 | tf_op jit(solution)/shard_map/all_to_all | solution.py:175
  543.1 19.9 %collective-permute-done.18 = bf16[128,2048]{1,0:T(8,128)(2,1)S(1)} collective-permute-done((bf16[128,2048]{1,0:T(8,128)(2,1)S(1)}, bf16[128,2048]{1,0:T(8,128)(2,1)S(1)}, u32[]{:S(2)}, u32[]{:S(2)}) %collective-permute-start.18) | collective-permute-done | bytes 524320 | tf_op jit(solution)/shard_map/ppermute | solution.py:97
  587.4 8.4 %collective-permute-done.21 = bf16[4,64,768]{2,1,0:T(8,128)(2,1)} collective-permute-done((bf16[4,64,768]{2,1,0:T(8,128)(2,1)}, bf16[4,64,768]{2,1,0:T(8,128)(2,1)}, u32[]{:S(2)}, u32[]{:S(2)}) %collective-permute-start.21) | collective-permute-done | bytes 393248 | tf_op jit(solution)/shard_map/ppermute | solution.py:97
  631.2 14.1 %collective-permute-done.28 = bf16[4,64,512]{2,1,0:T(8,128)(2,1)S(1)} collective-permute-done((bf16[4,64,512]{2,1,0:T(8,128)(2,1)S(1)}, bf16[4,64,512]{2,1,0:T(8,128)(2,1)S(1)}, u32[]{:S(2)}, u32[]{:S(2)}) %collective-permute-start.28) | collective-permute-done | bytes 262176 | tf_op jit(solution)/shard_map/ppermute | solution.py:97
  672.9 14.3 %collective-permute-done.33.refs_2_ = bf16[2,64,3072]{2,1,0:T(8,128)(2,1)} collective-permute-done((bf16[2,64,3072]{2,1,0:T(8,128)(2,1)}, bf16[2,64,3072]{2,1,0:T(8,128)(2,1)}, u32[]{:S(2)}, u32[]{:S(2)}) %collective-permute-start.33) | collective-permute-done | bytes 786464 | tf_op jit(solution)/shard_map/ppermute | solution.py:97
  687.3 21.9 %collective-permute-done.34.refs_3_ = bf16[2,64,3072]{2,1,0:T(8,128)(2,1)} collective-permute-done((bf16[2,64,3072]{2,1,0:T(8,128)(2,1)}, bf16[2,64,3072]{2,1,0:T(8,128)(2,1)}, u32[]{:S(2)}, u32[]{:S(2)}) %collective-permute-start.34) | collective-permute-done | bytes 786464 | tf_op jit(solution)/shard_map/ppermute | solution.py:97
  709.2 16.3 %collective-permute-done.35.refs_4_ = bf16[2,64,3072]{2,1,0:T(8,128)(2,1)} collective-permute-done((bf16[2,64,3072]{2,1,0:T(8,128)(2,1)}, bf16[2,64,3072]{2,1,0:T(8,128)(2,1)}, u32[]{:S(2)}, u32[]{:S(2)}) %collective-permute-start.35) | collective-permute-done | bytes 786464 | tf_op jit(solution)/shard_map/ppermute | solution.py:97
  (310 shorter events, 292.4 us)
Async XLA Ops:
  14.6 73.6 %all-to-all-start = ((bf16[8,64,3072]{2,1,0:T(8,128)(2,1)}), bf16[8,64,3072]{2,1,0:T(8,128)(2,1)S(1)}, u32[]{:S(2)}, u32[]{:S(2)}) async-start(bf16[8,64,3072]{2,1,0:T(8,128)(2,1)} %copy.177), calls=%async_computation | async-start | bytes 6291456 | tf_op jit(solution)/shard_map/all_to_all | solution.py:175
  20.0 116.0 %all-gather.4.cloned.1.call-start = ((), (), s32[]{:S(2)}) async-start(), calls=%async_computation.11 | async-start | bytes 2785280 | tf_op jit(solution)/shard_map/all_gather | solution.py:653
  26.1 225.9 %all-gather.6.cloned.1.call-start = ((), (), s32[]{:S(2)}) async-start(), calls=%async_computation.12 | async-start | bytes 15728640 | tf_op jit(solution)/shard_map/all_gather | solution.py:185
  96.9 27.3 %collective-permute-start.4 = (bf16[4,64,768]{2,1,0:T(8,128)(2,1)S(1)}, bf16[4,64,768]{2,1,0:T(8,128)(2,1)S(1)}, u32[]{:S(2)}, u32[]{:S(2)}) collective-permute-start(bf16[4,64,768]{2,1,0:T(8,128)(2,1)S(1)} %constant_dynamic-update-slice_fusion.11), channel_id=1, source_target_pairs={{0,4},{2,6},{4,0},{6,2},{1,5},{3,7},{5,1},{7,3},{8,12},{10,14},{12... | collective-permute-start | bytes 1179656 | tf_op jit(solution)/shard_map/ppermute | solution.py:97
  97.8 35.2 %collective-permute-start.5 = (bf16[4,64,768]{2,1,0:T(8,128)(2,1)S(1)}, bf16[4,64,768]{2,1,0:T(8,128)(2,1)S(1)}, u32[]{:S(2)}, u32[]{:S(2)}) collective-permute-start(bf16[4,64,768]{2,1,0:T(8,128)(2,1)S(1)} %constant_dynamic-update-slice_fusion.11), channel_id=1, source_target_pairs={{0,6},{2,4},{4,2},{6,0},{1,7},{3,5},{5,3},{7,1},{8,14},{10,12},{12... | collective-permute-start | bytes 1179656 | tf_op jit(solution)/shard_map/ppermute | solution.py:97
  150.1 33.6 %collective-permute-start.9 = (bf16[4,64,512]{2,1,0:T(8,128)(2,1)S(1)}, bf16[4,64,512]{2,1,0:T(8,128)(2,1)}, u32[]{:S(2)}, u32[]{:S(2)}) collective-permute-start(bf16[4,64,512]{2,1,0:T(8,128)(2,1)S(1)} %constant_dynamic-update-slice_fusion.10), channel_id=1, source_target_pairs={{0,6},{2,4},{4,2},{6,0},{1,7},{3,5},{5,3},{7,1},{8,14},{10,12},{12... | collective-permute-start | bytes 786440 | tf_op jit(solution)/shard_map/ppermute | solution.py:97
  161.1 28.8 %all-to-all-start.1 = ((bf16[4,256,384]{2,1,0:T(8,128)(2,1)}), bf16[4,256,384]{2,1,0:T(8,128)(2,1)S(1)}, u32[]{:S(2)}, u32[]{:S(2)}) async-start(bf16[4,256,384]{2,1,0:T(8,128)(2,1)} %shard_map.204), calls=%async_computation.1 | async-start | bytes 1572864 | tf_op jit(solution)/shard_map/all_to_all | solution.py:175
  224.5 27.5 %all-to-all-start.3 = ((bf16[4,128,2048]{2,1,0:T(8,128)(2,1)}), bf16[4,128,2048]{2,1,0:T(8,128)(2,1)S(1)}, u32[]{:S(2)}, u32[]{:S(2)}) async-start(bf16[4,128,2048]{2,1,0:T(8,128)(2,1)} %get-tuple-element.36), calls=%async_computation.3 | async-start | bytes 4194304 | tf_op jit(solution)/shard_map/all_to_all | solution.py:175
  228.3 68.4 %all-gather.8.cloned.1.call-start = ((), (), s32[]{:S(2)}) async-start(), calls=%async_computation.13 | async-start | bytes 2621440 | tf_op jit(solution)/shard_map/all_gather | solution.py:677
  257.6 67.4 %all-to-all-start.4 = ((bf16[4,128,2048]{2,1,0:T(8,128)(2,1)}), bf16[4,128,2048]{2,1,0:T(8,128)(2,1)S(1)}, u32[]{:S(2)}, u32[]{:S(2)}) async-start(bf16[4,128,2048]{2,1,0:T(8,128)(2,1)} %get-tuple-element.38), calls=%async_computation.4 | async-start | bytes 4194304 | tf_op jit(solution)/shard_map/all_to_all | solution.py:175
  296.6 28.4 %collective-permute-start.12 = (bf16[4,128,2048]{2,1,0:T(8,128)(2,1)}, bf16[4,128,2048]{2,1,0:T(8,128)(2,1)}, u32[]{:S(2)}, u32[]{:S(2)}) collective-permute-start(bf16[4,128,2048]{2,1,0:T(8,128)(2,1)} %all-gather.8.cloned.1.call-done), channel_id=1, source_target_pairs={{0,8},{8,0},{1,9},{9,1},{2,10},{10,2},{3,11},{11,3},{4,12},{12,4},... | collective-permute-start | bytes 6291464 | tf_op jit(solution)/shard_map/ppermute | solution.py:97
  373.4 53.3 %all-to-all-start.5 = ((bf16[4,128,2048]{2,1,0:T(8,128)(2,1)}), bf16[4,128,2048]{2,1,0:T(8,128)(2,1)S(1)}, u32[]{:S(2)}, u32[]{:S(2)}) async-start(bf16[4,128,2048]{2,1,0:T(8,128)(2,1)} %add_convert_fusion), calls=%async_computation.5 | async-start | bytes 4194304 | tf_op jit(solution)/shard_map/all_to_all | solution.py:175
  432.3 31.8 %all-to-all-start.6 = ((bf16[4,128,2048]{2,1,0:T(8,128)(2,1)}), bf16[4,128,2048]{2,1,0:T(8,128)(2,1)}, u32[]{:S(2)}, u32[]{:S(2)}) async-start(bf16[4,128,2048]{2,1,0:T(8,128)(2,1)} %get-tuple-element.49), calls=%async_computation.6 | async-start | bytes 4194304 | tf_op jit(solution)/shard_map/all_to_all | solution.py:175
  436.9 186.3 %reduce-scatter.4.cloned.1.call-start = ((), (), s32[]{:S(2)}) async-start(), calls=%async_computation.14 | async-start | bytes 15728640
  537.4 31.3 %collective-permute-start.17 = (bf16[4,4,64,768]{3,2,0,1:T(8,128)(2,1)}, bf16[4,4,64,768]{3,2,0,1:T(8,128)(2,1)}, u32[]{:S(2)}, u32[]{:S(2)}) collective-permute-start(bf16[4,4,64,768]{3,2,0,1:T(8,128)(2,1)} %fusion.4), channel_id=1, source_target_pairs={{0,8},{8,0},{1,9},{9,1},{2,10},{10,2},{3,11},{11,3},{4,12},{12,4},... | collective-permute-start | bytes 4718600 | tf_op jit(solution)/shard_map/ppermute | solution.py:97
  537.4 25.6 %collective-permute-start.18 = (bf16[128,2048]{1,0:T(8,128)(2,1)S(1)}, bf16[128,2048]{1,0:T(8,128)(2,1)S(1)}, u32[]{:S(2)}, u32[]{:S(2)}) collective-permute-start(bf16[128,2048]{1,0:T(8,128)(2,1)S(1)} %copy-done.32), channel_id=1, source_target_pairs={{0,6},{2,4},{4,2},{6,0},{1,7},{3,5},{5,3},{7,1},{8,14},{10,12},{12... | collective-permute-start | bytes 1572872 | tf_op jit(solution)/shard_map/ppermute | solution.py:97
  537.7 45.5 %all-to-all-start.9 = ((bf16[4,128,2048]{2,1,0:T(8,128)(2,1)}), bf16[4,128,2048]{2,1,0:T(8,128)(2,1)}, u32[]{:S(2)}, u32[]{:S(2)}) async-start(bf16[4,128,2048]{2,1,0:T(8,128)(2,1)} %get-tuple-element.53), calls=%async_computation.9 | async-start | bytes 4194304 | tf_op jit(solution)/shard_map/all_to_all | solution.py:175
  575.3 26.3 %collective-permute-start.20 = (bf16[4,64,768]{2,1,0:T(8,128)(2,1)}, bf16[4,64,768]{2,1,0:T(8,128)(2,1)}, u32[]{:S(2)}, u32[]{:S(2)}) collective-permute-start(bf16[4,64,768]{2,1,0:T(8,128)(2,1)} %get-tuple-element.72), channel_id=1, source_target_pairs={{0,4},{2,6},{4,0},{6,2},{1,5},{3,7},{5,1},{7,3},{8,12},{10,14},{12... | collective-permute-start | bytes 1179656 | tf_op jit(solution)/shard_map/ppermute | solution.py:97
  575.3 26.3 %collective-permute-start.19 = (bf16[4,64,768]{2,1,0:T(8,128)(2,1)S(1)}, bf16[4,64,768]{2,1,0:T(8,128)(2,1)}, u32[]{:S(2)}, u32[]{:S(2)}) collective-permute-start(bf16[4,64,768]{2,1,0:T(8,128)(2,1)S(1)} %get-tuple-element.70), channel_id=1, source_target_pairs={{0,2},{2,0},{4,6},{6,4},{1,3},{3,1},{5,7},{7,5},{8,10},{10,8},{12,... | collective-permute-start | bytes 1179656 | tf_op jit(solution)/shard_map/ppermute | solution.py:97
  583.2 37.6 %collective-permute-start.25 = (bf16[4,4,64,512]{3,2,1,0:T(8,128)(2,1)}, bf16[4,4,64,512]{3,2,1,0:T(8,128)(2,1)}, u32[]{:S(2)}, u32[]{:S(2)}) collective-permute-start(bf16[4,4,64,512]{3,2,1,0:T(8,128)(2,1)} %fusion.5), channel_id=1, source_target_pairs={{0,8},{8,0},{1,9},{9,1},{2,10},{10,2},{3,11},{11,3},{4,12},{12,4},... | collective-permute-start | bytes 3145736 | tf_op jit(solution)/shard_map/ppermute | solution.py:97
  624.7 27.1 %collective-permute-start.32 = (bf16[4,64,3072]{2,1,0:T(8,128)(2,1)S(1)}, bf16[4,64,3072]{2,1,0:T(8,128)(2,1)S(1)}, u32[]{:S(2)}, u32[]{:S(2)}) collective-permute-start(bf16[4,64,3072]{2,1,0:T(8,128)(2,1)S(1)} %dynamic-slice_bitcast_fusion), channel_id=1, source_target_pairs={{0,8},{8,0},{1,9},{9,1},{2,10},{10,2},{3,11},{11,3},{4,12},{12,4},... | collective-permute-start | bytes 4718600 | tf_op jit(solution)/shard_map/ppermute | solution.py:97
  652.8 34.4 %collective-permute-start.33 = (bf16[2,64,3072]{2,1,0:T(8,128)(2,1)}, bf16[2,64,3072]{2,1,0:T(8,128)(2,1)}, u32[]{:S(2)}, u32[]{:S(2)}) collective-permute-start(bf16[2,64,3072]{2,1,0:T(8,128)(2,1)} %pad_maximum_fusion.2), channel_id=1, source_target_pairs={{0,2},{2,0},{4,6},{6,4},{1,3},{3,1},{5,7},{7,5},{8,10},{10,8},{12,... | collective-permute-start | bytes 2359304 | tf_op jit(solution)/shard_map/ppermute | solution.py:97
  656.0 53.2 %collective-permute-start.34 = (bf16[2,64,3072]{2,1,0:T(8,128)(2,1)}, bf16[2,64,3072]{2,1,0:T(8,128)(2,1)}, u32[]{:S(2)}, u32[]{:S(2)}) collective-permute-start(bf16[2,64,3072]{2,1,0:T(8,128)(2,1)} %pad_maximum_fusion.3), channel_id=1, source_target_pairs={{0,4},{2,6},{4,0},{6,2},{1,5},{3,7},{5,1},{7,3},{8,12},{10,14},{12... | collective-permute-start | bytes 2359304 | tf_op jit(solution)/shard_map/ppermute | solution.py:97
  658.1 67.4 %collective-permute-start.35 = (bf16[2,64,3072]{2,1,0:T(8,128)(2,1)}, bf16[2,64,3072]{2,1,0:T(8,128)(2,1)}, u32[]{:S(2)}, u32[]{:S(2)}) collective-permute-start(bf16[2,64,3072]{2,1,0:T(8,128)(2,1)} %pad_maximum_fusion.4), channel_id=1, source_target_pairs={{0,6},{2,4},{4,2},{6,0},{1,7},{3,5},{5,3},{7,1},{8,14},{10,12},{12... | collective-permute-start | bytes 2359304 | tf_op jit(solution)/shard_map/ppermute | solution.py:97
  (66 other events, 657.2 us)
Sparse Core Ops, SparseCore 0:
  26.2 44.3 all-gather.3
  90.5 123.4 all-gather.5
  235.5 61.1 all-gather.7
  473.1 138.0 reduce-scatter.3
